TPU v7x, 32 devices: a whole 2x2x4 slice. The times are simulated.
32 devices in a mesh: pos: 16 (over z, x, core), off: 2 (over y).
Axes of the slice: x: 2, y: 2, z: 4, core: 2. Of those that a mesh axis runs over, the one named last changes fastest.
Arguments:
- bin_embed: bfloat16 [1024, 128], P('pos'), may hold values from -6 to 6
- block_slot: int32 [16], replicated, may hold values from 0 to 15, each once
- proj_weight: bfloat16 [128, 64], replicated, may hold values from -0.5 to 0.5
- proj_bias: float32 [64], replicated, may hold values from -3 to 3
- conv_weight: bfloat16 [4, 576, 64], replicated, may hold values from -0.25 to 0.25
- conv_bias: float32 [4, 64], replicated, may hold values from -2 to 2
Outputs:
- contact: bfloat16 [16, 2, 64, 4096], P('pos', 'off')
Inputs may be any that keep to these rules, and one draw needn't show every extreme that they name: block_slot names every number of 0 to 15 once; bin block b's embeddings are rows block_slot[b] * 64 to block_slot[b] * 64 + 63 of bin_embed.
All inputs are finite; a program needn't handle non-finite values.
Results may differ from a plain program's by a relative error of at most 0.015.
Values may be sent and summed in bfloat16 or wider, within the bound.
No kernel may reach another device: no remote copies, remote signals or barrier semaphores. Data moves between devices by JAX's collectives and lax.ppermute only.
A program may use at most 64 MiB of HBM per device.

v0:
```python
import jax
import jax.numpy as jnp
from jax import lax
from jax.sharding import PartitionSpec as P

TILE = 64
LAYERS = 4


def shifted(value, axis, steps):
    count = lax.axis_size(axis)
    pairs = [(source, (source + steps) % count) for source in range(count)]
    return lax.ppermute(value, axis, pairs)


def from_behind(array, axis, by):
    length = lax.axis_size(axis)
    pairs = [(i, i + by) for i in range(length) if 0 <= i + by < length]
    return lax.ppermute(array, axis, pairs)


def flip_tiles(tiles):
    return jnp.swapaxes(tiles, 1, 2)


def on_device(bin_embed, block_slot, proj_weight, proj_bias, conv_weight, conv_bias):
    channels = proj_weight.shape[1]
    tiles_dev = bin_embed.shape[0] // TILE
    blocks_all = block_slot.shape[0]
    position = lax.axis_index("pos")
    offset = lax.axis_index("off")
    row_blocks = position * tiles_dev + jnp.arange(tiles_dev, dtype=jnp.int32)
    col_blocks = (row_blocks + offset) % blocks_all
    wanted = block_slot[jnp.concatenate([row_blocks, col_blocks])]
    table = lax.all_gather(bin_embed, "pos", axis=0, tiled=True).reshape(
        blocks_all, TILE, bin_embed.shape[1]
    )
    picked = table[wanted].reshape(2 * tiles_dev * TILE, bin_embed.shape[1])
    projected = jnp.dot(picked, proj_weight, preferred_element_type=jnp.float32).astype(
        jnp.bfloat16
    )
    projected = projected.reshape(2, tiles_dev, TILE, channels)
    pair_sum = (
        projected[0][:, :, None, :].astype(jnp.float32)
        + projected[1][:, None, :, :].astype(jnp.float32)
        + proj_bias
    )
    current = pair_sum.astype(jnp.bfloat16)
    first_band = offset == 0
    second_band = offset == 1
    final_tile = tiles_dev - 1
    for layer_index in range(LAYERS):
        dilation = 2**layer_index
        edge = TILE - dilation
        hidden = jax.nn.gelu(current.astype(jnp.float32)).astype(jnp.bfloat16)
        top_rows = hidden[:, :dilation]
        bottom_rows = hidden[:, edge:]
        left_cols = hidden[:, :, :dilation]
        right_cols = hidden[:, :, edge:]
        from_prev = shifted(bottom_rows, "pos", 1)
        from_after = shifted(top_rows, "pos", -1)
        below_prev = jnp.concatenate([from_prev, bottom_rows[:final_tile]], axis=0)
        above_after = jnp.concatenate([top_rows[1:], from_after], axis=0)
        upper, right_strip = from_behind((below_prev, left_cols), "off", -1)
        lower, left_strip = from_behind((above_after, right_cols), "off", 1)
        upper_right = from_behind(below_prev[:, :, :dilation], "off", -2)
        lower_left = from_behind(above_after[:, :, edge:], "off", 2)
        upper_left = below_prev[:, :, edge:]
        lower_right = above_after[:, :, :dilation]
        left_strip = jnp.where(first_band, flip_tiles(upper), left_strip)
        lower = jnp.where(first_band, flip_tiles(right_strip), lower)
        lower_left = jnp.where(
            first_band,
            flip_tiles(upper_right),
            jnp.where(second_band, flip_tiles(bottom_rows[:, :, :dilation]), lower_left),
        )
        top_band = jnp.concatenate([upper_left, upper, upper_right], axis=2)
        middle = jnp.concatenate([left_strip, hidden, right_strip], axis=2)
        bottom_band = jnp.concatenate([lower_left, lower, lower_right], axis=2)
        padded = jnp.concatenate([top_band, middle, bottom_band], axis=1)
        summed = jnp.zeros((tiles_dev, TILE, TILE, channels), jnp.float32)
        for row_tap in range(3):
            for col_tap in range(3):
                tap_index = 3 * row_tap + col_tap
                window = padded[
                    :,
                    row_tap * dilation : row_tap * dilation + TILE,
                    col_tap * dilation : col_tap * dilation + TILE,
                ]
                kernel = conv_weight[layer_index, tap_index * channels : (tap_index + 1) * channels]
                summed = summed + jnp.einsum(
                    "prcd,de->prce", window, kernel, preferred_element_type=jnp.float32
                )
        current = (current.astype(jnp.float32) + summed + conv_bias[layer_index]).astype(
            jnp.bfloat16
        )
    return current.reshape(tiles_dev, 1, TILE, TILE * channels)


def solution(mesh):
    placed = (P("pos", None), P(), P(), P(), P(), P())
    return jax.shard_map(
        on_device,
        mesh=mesh,
        in_specs=placed,
        out_specs=P("pos", "off", None, None),
        check_vma=False,
    )
```

profile of v0, /device:TPU:0, one launch (start us, length us, event | category | flops | bytes accessed | tf_op | source)
XLA Modules:
  0.0 146.3 jit_solution(7575857380395265277)
XLA Ops:
  0.1 1.3 gather_fusion
  1.4 24.0 %all_gather.3 = bf16[1024,128]{1,0:T(8,128)(2,1)S(1)} all-gather(bf16[64,128]{1,0:T(8,128)(2,1)} %param.6), channel_id=1, replica_groups=mesh['pos'=16,'off'=2] {'pos'}, dimensions={0}, use_global_device_ids=true | all-gather | bytes 278528 | tf_op jit(solution)/shard_map/all_gather | solution.py:35
  26.4 1.5 %fusion.5 = bf16[1,64,64,64]{3,1,2,0:T(8,128)(2,1)S(1)} fusion(f32[64]{0:T(128)} %param.9, f32[64,64]{1,0:T(8,128)S(1)} %copy.212, f32[64,64]{1,0:T(8,128)S(1)} %copy.211), kind=kLoop, calls=%fused_computation.31 | loop fusion | flops 3407872 | bytes 557312 | tf_op jit(solution)/shard_map/convert_element_type | solution.py:55
  28.4 3.4 %collective-permute-start.3 = (bf16[1,64,1,64]{3,1,2,0:T(8,128)(2,1)S(1)}, bf16[1,64,1,64]{3,1,2,0:T(8,128)(2,1)S(1)}, u32[]{:S(2)}, u32[]{:S(2)}) collective-permute-start(bf16[1,64,1,64]{3,1,2,0:T(8,128)(2,1)S(1)} %get-tuple-element.27), channel_id=1, source_target_pairs={{0,1},{2,3},{4,5},{6,7},{8,9},{10,11},{12,13},{14,15},{16,17},{18,... | collective-permute-start | bytes 24584 | tf_op jit(solution)/shard_map/ppermute | solution.py:19
  31.8 1.3 collective-permute-start.4
  33.1 3.9 %collective-permute-start.5 = (bf16[1,1,64,64]{3,2,1,0:T(8,128)(2,1)S(1)}, bf16[1,1,64,64]{3,2,1,0:T(8,128)(2,1)S(1)}, u32[]{:S(2)}, u32[]{:S(2)}) collective-permute-start(bf16[1,1,64,64]{3,2,1,0:T(8,128)(2,1)S(1)} %copy.227), channel_id=1, source_target_pairs={{0,30},{2,0},{4,2},{6,4},{8,6},{10,8},{12,10},{14,12},{16,14},{18,... | collective-permute-start | bytes 24584 | tf_op jit(solution)/shard_map/ppermute | solution.py:13
  37.0 2.2 %fusion.38 = f32[64,64,64]{2,1,0:T(8,128)} fusion(f32[64]{0:T(128)S(1)} %copy-done.4, f32[64,64]{1,0:T(8,128)S(1)} %copy.212, f32[64,64]{1,0:T(8,128)S(1)} %copy.211, bf16[4,576,64]{1,2,0:T(8,128)(2,1)S(1)} %copy-done.3), kind=kOutput, calls=%fused_computation.75 | convolution fusion | flops 36962304 | bytes 1131008 | tf_op jit(solution)/shard_map/prcd,de->prce/dot_general | solution.py:91
  41.3 1.3 collective-permute-start.1
  42.6 4.5 %collective-permute-start.7 = (bf16[1,1,64,64]{3,2,1,0:T(8,128)(2,1)S(1)}, bf16[1,1,64,64]{3,2,1,0:T(8,128)(2,1)S(1)}, u32[]{:S(2)}, u32[]{:S(2)}) collective-permute-start(bf16[1,1,64,64]{3,2,1,0:T(8,128)(2,1)S(1)} %collective-permute-done.5), channel_id=1, source_target_pairs={{0,1},{2,3},{4,5},{6,7},{8,9},{10,11},{12,13},{14,15},{16,17},{18,... | collective-permute-start | bytes 24584 | tf_op jit(solution)/shard_map/ppermute | solution.py:19
  48.6 3.0 %maximum_maximum_fusion.6 = (bf16[1,65,66,64]{3,2,1,0:T(8,128)(2,1)S(1)}, bf16[1,65,66,64]{3,2,1,0:T(8,128)(2,1)S(1)}) fusion(bf16[1,64,1,64]{3,2,1,0:T(2,128)(2,1)S(1)} %copy.217, bf16[1,64,64,64]{3,2,1,0:T(8,128)(2,1)S(1)} %copy.216, bf16[1,64,1,64]{3,2,1,0:T(2,128)(2,1)S(1)} %copy.215, bf16[1,1,66,64]{3,2,1,0:T(8,128)(2,1)S(1)} %copy.218, ...), kind=kLoop, calls=%fused_computation.72 | loop fusion | flops 5491200 | bytes 1655808 | tf_op jit(solution)/shard_map/concatenate | solution.py:80
  56.1 1.9 %fusion.13 = bf16[64,64,64]{2,1,0:T(8,128)(2,1)S(1)} fusion(f32[64,64,64]{2,1,0:T(8,128)S(1)} %fusion.79, f32[64,64,64]{2,1,0:T(8,128)S(1)} %fusion.80, f32[64,64,64]{2,1,0:T(8,128)S(1)} %fusion.81, f32[64,64,64]{2,1,0:T(8,128)S(1)} %copy-done.2, f32[64,64,64]{2,1,0:T(8,128)S(1)} %fusion.88, f32[64,64,64]{2,1,0:T(8,128)S(1)} %fusion.84, ...), kind=kOutput, calls=%fused_computation.39 | convolution fusion | flops 37486592 | bytes 18433024 | tf_op jit(solution)/shard_map/prcd,de->prce/dot_general | solution.py:91
  59.0 4.5 %collective-permute-start.13 = (bf16[1,2,64,64]{3,2,1,0:T(8,128)(2,1)S(1)}, bf16[1,2,64,64]{3,2,1,0:T(8,128)(2,1)S(1)}, u32[]{:S(2)}, u32[]{:S(2)}) collective-permute-start(bf16[1,2,64,64]{3,2,1,0:T(8,128)(2,1)S(1)} %get-tuple-element.24), channel_id=1, source_target_pairs={{0,30},{2,0},{4,2},{6,4},{8,6},{10,8},{12,10},{14,12},{16,14},{18,... | collective-permute-start | bytes 49160 | tf_op jit(solution)/shard_map/ppermute | solution.py:13
  63.5 1.3 collective-permute-start.12
  67.3 4.4 %collective-permute-start.11 = (bf16[1,64,2,64]{3,2,1,0:T(2,128)(2,1)S(1)}, bf16[1,64,2,64]{3,2,1,0:T(2,128)(2,1)S(1)}, u32[]{:S(2)}, u32[]{:S(2)}) collective-permute-start(bf16[1,64,2,64]{3,2,1,0:T(2,128)(2,1)S(1)} %get-tuple-element.21), channel_id=1, source_target_pairs={{0,1},{2,3},{4,5},{6,7},{8,9},{10,11},{12,13},{14,15},{16,17},{18,... | collective-permute-start | bytes 49160 | tf_op jit(solution)/shard_map/ppermute | solution.py:19
  71.7 1.3 collective-permute-start.9
  73.0 4.5 %collective-permute-start.15 = (bf16[1,2,64,64]{3,2,1,0:T(8,128)(2,1)S(1)}, bf16[1,2,64,64]{3,2,1,0:T(8,128)(2,1)S(1)}, u32[]{:S(2)}, u32[]{:S(2)}) collective-permute-start(bf16[1,2,64,64]{3,2,1,0:T(8,128)(2,1)S(1)} %collective-permute-done.13), channel_id=1, source_target_pairs={{0,1},{2,3},{4,5},{6,7},{8,9},{10,11},{12,13},{14,15},{16,17},{18,... | collective-permute-start | bytes 49160 | tf_op jit(solution)/shard_map/ppermute | solution.py:19
  79.1 3.1 %maximum_maximum_fusion.4 = (bf16[1,66,68,64]{3,2,1,0:T(8,128)(2,1)S(1)}, bf16[1,66,68,64]{3,2,1,0:T(8,128)(2,1)S(1)}) fusion(bf16[1,64,2,64]{3,2,1,0:T(2,128)(2,1)S(1)} %copy.235, bf16[1,64,64,64]{3,2,1,0:T(8,128)(2,1)S(1)} %fusion.194, bf16[1,64,2,64]{3,2,1,0:T(2,128)(2,1)S(1)} %broadcast_select_fusion, bf16[1,2,68,64]{3,2,1,0:T(8,128)(2,1)S(1)} %copy.236, ...), kind=kLoop, calls=%fused_computation.70 | loop fusion | flops 5744640 | bytes 1740800 | tf_op jit(solution)/shard_map/concatenate | solution.py:80
  85.0 1.3 fusion.21
  87.3 4.5 %collective-permute-start.21 = (bf16[1,4,64,64]{3,2,1,0:T(8,128)(2,1)S(1)}, bf16[1,4,64,64]{3,2,1,0:T(8,128)(2,1)S(1)}, u32[]{:S(2)}, u32[]{:S(2)}) collective-permute-start(bf16[1,4,64,64]{3,2,1,0:T(8,128)(2,1)S(1)} %get-tuple-element.20), channel_id=1, source_target_pairs={{0,30},{2,0},{4,2},{6,4},{8,6},{10,8},{12,10},{14,12},{16,14},{18,... | collective-permute-start | bytes 98312 | tf_op jit(solution)/shard_map/ppermute | solution.py:13
  91.8 1.3 collective-permute-start.20
  95.8 4.2 %collective-permute-start.19 = (bf16[1,64,4,64]{3,2,1,0:T(4,128)(2,1)S(1)}, bf16[1,64,4,64]{3,2,1,0:T(4,128)(2,1)S(1)}, u32[]{:S(2)}, u32[]{:S(2)}) collective-permute-start(bf16[1,64,4,64]{3,2,1,0:T(4,128)(2,1)S(1)} %get-tuple-element.17), channel_id=1, source_target_pairs={{0,1},{2,3},{4,5},{6,7},{8,9},{10,11},{12,13},{14,15},{16,17},{18,... | collective-permute-start | bytes 98312 | tf_op jit(solution)/shard_map/ppermute | solution.py:19
  100.0 1.3 collective-permute-start.17
  101.3 4.8 %collective-permute-start.23 = (bf16[1,4,64,64]{3,2,1,0:T(8,128)(2,1)S(1)}, bf16[1,4,64,64]{3,2,1,0:T(8,128)(2,1)S(1)}, u32[]{:S(2)}, u32[]{:S(2)}) collective-permute-start(bf16[1,4,64,64]{3,2,1,0:T(8,128)(2,1)S(1)} %collective-permute-done.21), channel_id=1, source_target_pairs={{0,1},{2,3},{4,5},{6,7},{8,9},{10,11},{12,13},{14,15},{16,17},{18,... | collective-permute-start | bytes 98312 | tf_op jit(solution)/shard_map/ppermute | solution.py:19
  107.8 3.4 %maximum_maximum_fusion.2 = (bf16[1,68,72,64]{3,2,1,0:T(8,128)(2,1)S(1)}, bf16[1,68,72,64]{3,2,1,0:T(8,128)(2,1)S(1)}) fusion(bf16[1,64,4,64]{3,2,1,0:T(4,128)(2,1)S(1)} %copy.250, bf16[1,64,64,64]{3,2,1,0:T(8,128)(2,1)S(1)} %fusion.192, bf16[1,64,4,64]{3,2,1,0:T(4,128)(2,1)S(1)} %bitcast_select_fusion.3, bf16[1,4,72,64]{3,2,1,0:T(8,128)(2,1)S(1)} %copy.251, ...), kind=kLoop, calls=%fused_computation.68 | loop fusion | flops 6266880 | bytes 1916928 | tf_op jit(solution)/shard_map/concatenate | solution.py:80
  113.9 1.3 fusion.29
  116.2 4.5 %collective-permute-start.29 = (bf16[1,8,64,64]{3,2,1,0:T(8,128)(2,1)S(1)}, bf16[1,8,64,64]{3,2,1,0:T(8,128)(2,1)S(1)}, u32[]{:S(2)}, u32[]{:S(2)}) collective-permute-start(bf16[1,8,64,64]{3,2,1,0:T(8,128)(2,1)S(1)} %get-tuple-element.16), channel_id=1, source_target_pairs={{0,30},{2,0},{4,2},{6,4},{8,6},{10,8},{12,10},{14,12},{16,14},{18,... | collective-permute-start | bytes 196616 | tf_op jit(solution)/shard_map/ppermute | solution.py:13
  120.7 1.3 collective-permute-start.28
  125.4 4.3 %collective-permute-start.27 = (bf16[1,64,8,64]{3,2,1,0:T(8,128)(2,1)S(1)}, bf16[1,64,8,64]{3,2,1,0:T(8,128)(2,1)S(1)}, u32[]{:S(2)}, u32[]{:S(2)}) collective-permute-start(bf16[1,64,8,64]{3,2,1,0:T(8,128)(2,1)S(1)} %get-tuple-element.13), channel_id=1, source_target_pairs={{0,1},{2,3},{4,5},{6,7},{8,9},{10,11},{12,13},{14,15},{16,17},{18,... | collective-permute-start | bytes 196616 | tf_op jit(solution)/shard_map/ppermute | solution.py:19
  129.7 1.3 collective-permute-start.25
  131.0 4.8 %collective-permute-start.31 = (bf16[1,8,64,64]{3,2,1,0:T(8,128)(2,1)S(1)}, bf16[1,8,64,64]{3,2,1,0:T(8,128)(2,1)S(1)}, u32[]{:S(2)}, u32[]{:S(2)}) collective-permute-start(bf16[1,8,64,64]{3,2,1,0:T(8,128)(2,1)S(1)} %collective-permute-done.29), channel_id=1, source_target_pairs={{0,1},{2,3},{4,5},{6,7},{8,9},{10,11},{12,13},{14,15},{16,17},{18,... | collective-permute-start | bytes 196616 | tf_op jit(solution)/shard_map/ppermute | solution.py:19
  138.1 2.7 %maximum_maximum_fusion = (bf16[1,72,80,64]{3,2,1,0:T(8,128)(2,1)S(1)}, bf16[1,72,80,64]{3,2,1,0:T(8,128)(2,1)S(1)}) fusion(bf16[1,64,8,64]{3,2,1,0:T(8,128)(2,1)S(1)} %copy.265, bf16[1,64,64,64]{3,2,1,0:T(8,128)(2,1)S(1)} %fusion.190, bf16[1,64,8,64]{3,2,1,0:T(8,128)(2,1)S(1)} %bitcast_select_fusion.1, bf16[1,8,80,64]{3,2,1,0:T(8,128)(2,1)S(1)} %copy.266, ...), kind=kLoop, calls=%fused_computation.66 | loop fusion | flops 7372800 | bytes 2293760 | tf_op jit(solution)/shard_map/concatenate | solution.py:80
  144.7 1.6 %reshape.443 = bf16[1,1,64,4096]{3,2,1,0:T(8,128)(2,1)} reshape(bf16[64,64,64]{2,1,0:T(8,128)(2,1)S(1)} %fusion.37) | data formatting | bytes 1048576 | tf_op jit(solution)/shard_map/reshape | solution.py:97
  (154 shorter events, 35.3 us)
Async XLA Ops:
  28.0 11.9 %collective-permute-start = (bf16[1,1,64,64]{3,1,2,0:T(2,128)(2,1)S(1)}, bf16[1,1,64,64]{3,1,2,0:T(2,128)(2,1)S(1)}, u32[]{:S(2)}, u32[]{:S(2)}) collective-permute-start(bf16[1,1,64,64]{3,1,2,0:T(2,128)(2,1)S(1)} %get-tuple-element.29), channel_id=1, source_target_pairs={{0,2},{2,4},{4,6},{6,8},{8,10},{10,12},{12,14},{14,16},{16,18},{18... | collective-permute-start | bytes 24584 | tf_op jit(solution)/shard_map/ppermute | solution.py:13
  28.4 18.8 %collective-permute-start.3 = (bf16[1,64,1,64]{3,1,2,0:T(8,128)(2,1)S(1)}, bf16[1,64,1,64]{3,1,2,0:T(8,128)(2,1)S(1)}, u32[]{:S(2)}, u32[]{:S(2)}) collective-permute-start(bf16[1,64,1,64]{3,1,2,0:T(8,128)(2,1)S(1)} %get-tuple-element.27), channel_id=1, source_target_pairs={{0,1},{2,3},{4,5},{6,7},{8,9},{10,11},{12,13},{14,15},{16,17},{18,... | collective-permute-start | bytes 24584 | tf_op jit(solution)/shard_map/ppermute | solution.py:19
  31.8 10.8 %collective-permute-start.4 = (bf16[1,64,1,64]{3,1,2,0:T(8,128)(2,1)S(1)}, bf16[1,64,1,64]{3,1,2,0:T(8,128)(2,1)S(1)}, u32[]{:S(2)}, u32[]{:S(2)}) collective-permute-start(bf16[1,64,1,64]{3,1,2,0:T(8,128)(2,1)S(1)} %get-tuple-element.28), channel_id=1, source_target_pairs={{1,0},{3,2},{5,4},{7,6},{9,8},{11,10},{13,12},{15,14},{17,16},{19,... | collective-permute-start | bytes 24584 | tf_op jit(solution)/shard_map/ppermute | solution.py:19
  33.1 7.5 %collective-permute-start.5 = (bf16[1,1,64,64]{3,2,1,0:T(8,128)(2,1)S(1)}, bf16[1,1,64,64]{3,2,1,0:T(8,128)(2,1)S(1)}, u32[]{:S(2)}, u32[]{:S(2)}) collective-permute-start(bf16[1,1,64,64]{3,2,1,0:T(8,128)(2,1)S(1)} %copy.227), channel_id=1, source_target_pairs={{0,30},{2,0},{4,2},{6,4},{8,6},{10,8},{12,10},{14,12},{16,14},{18,... | collective-permute-start | bytes 24584 | tf_op jit(solution)/shard_map/ppermute | solution.py:13
  39.9 7.2 %collective-permute-start.2 = (bf16[1,1,1,64]{3,1,2,0:T(2,128)(2,1)S(1)}, bf16[1,1,1,64]{3,1,2,0:T(2,128)(2,1)S(1)}, u32[]{:S(2)}, u32[]{:S(2)}) collective-permute-start(bf16[1,1,1,64]{3,1,2,0:T(2,128)(2,1)S(1)} %get-tuple-element.44), channel_id=1, source_target_pairs={} | collective-permute-start | bytes 392 | tf_op jit(solution)/shard_map/ppermute | solution.py:19
  40.6 6.6 %collective-permute-start.6 = (bf16[1,1,1,64]{3,1,2,0:T(2,128)(2,1)S(1)}, bf16[1,1,1,64]{3,1,2,0:T(2,128)(2,1)S(1)}, u32[]{:S(2)}, u32[]{:S(2)}) collective-permute-start(bf16[1,1,1,64]{3,1,2,0:T(2,128)(2,1)S(1)} %get-tuple-element.45), channel_id=1, source_target_pairs={} | collective-permute-start | bytes 392 | tf_op jit(solution)/shard_map/ppermute | solution.py:19
  41.3 5.9 %collective-permute-start.1 = (bf16[1,1,64,64]{3,1,2,0:T(2,128)(2,1)S(1)}, bf16[1,1,64,64]{3,1,2,0:T(2,128)(2,1)S(1)}, u32[]{:S(2)}, u32[]{:S(2)}) collective-permute-start(bf16[1,1,64,64]{3,1,2,0:T(2,128)(2,1)S(1)} %collective-permute-done), channel_id=1, source_target_pairs={{1,0},{3,2},{5,4},{7,6},{9,8},{11,10},{13,12},{15,14},{17,16},{19,... | collective-permute-start | bytes 24584 | tf_op jit(solution)/shard_map/ppermute | solution.py:19
  42.6 6.0 %collective-permute-start.7 = (bf16[1,1,64,64]{3,2,1,0:T(8,128)(2,1)S(1)}, bf16[1,1,64,64]{3,2,1,0:T(8,128)(2,1)S(1)}, u32[]{:S(2)}, u32[]{:S(2)}) collective-permute-start(bf16[1,1,64,64]{3,2,1,0:T(8,128)(2,1)S(1)} %collective-permute-done.5), channel_id=1, source_target_pairs={{0,1},{2,3},{4,5},{6,7},{8,9},{10,11},{12,13},{14,15},{16,17},{18,... | collective-permute-start | bytes 24584 | tf_op jit(solution)/shard_map/ppermute | solution.py:19
  58.9 6.1 %collective-permute-start.8 = (bf16[1,2,64,64]{3,1,2,0:T(2,128)(2,1)S(1)}, bf16[1,2,64,64]{3,1,2,0:T(2,128)(2,1)S(1)}, u32[]{:S(2)}, u32[]{:S(2)}) collective-permute-start(bf16[1,2,64,64]{3,1,2,0:T(2,128)(2,1)S(1)} %copy.289), channel_id=1, source_target_pairs={{0,2},{2,4},{4,6},{6,8},{8,10},{10,12},{12,14},{14,16},{16,18},{18... | collective-permute-start | bytes 49160 | tf_op jit(solution)/shard_map/ppermute | solution.py:13
  59.0 6.6 %collective-permute-start.13 = (bf16[1,2,64,64]{3,2,1,0:T(8,128)(2,1)S(1)}, bf16[1,2,64,64]{3,2,1,0:T(8,128)(2,1)S(1)}, u32[]{:S(2)}, u32[]{:S(2)}) collective-permute-start(bf16[1,2,64,64]{3,2,1,0:T(8,128)(2,1)S(1)} %get-tuple-element.24), channel_id=1, source_target_pairs={{0,30},{2,0},{4,2},{6,4},{8,6},{10,8},{12,10},{14,12},{16,14},{18,... | collective-permute-start | bytes 49160 | tf_op jit(solution)/shard_map/ppermute | solution.py:13
  63.5 9.5 %collective-permute-start.12 = (bf16[1,64,2,64]{3,1,2,0:T(8,128)(2,1)S(1)}, bf16[1,64,2,64]{3,1,2,0:T(8,128)(2,1)S(1)}, u32[]{:S(2)}, u32[]{:S(2)}) collective-permute-start(bf16[1,64,2,64]{3,1,2,0:T(8,128)(2,1)S(1)} %copy.290), channel_id=1, source_target_pairs={{1,0},{3,2},{5,4},{7,6},{9,8},{11,10},{13,12},{15,14},{17,16},{19,... | collective-permute-start | bytes 49160 | tf_op jit(solution)/shard_map/ppermute | solution.py:19
  65.0 12.6 %collective-permute-start.10 = (bf16[1,2,2,64]{3,1,2,0:T(2,128)(2,1)S(1)}, bf16[1,2,2,64]{3,1,2,0:T(2,128)(2,1)S(1)}, u32[]{:S(2)}, u32[]{:S(2)}) collective-permute-start(bf16[1,2,2,64]{3,1,2,0:T(2,128)(2,1)S(1)} %get-tuple-element.40), channel_id=1, source_target_pairs={} | collective-permute-start | bytes 1544 | tf_op jit(solution)/shard_map/ppermute | solution.py:19
  65.6 12.0 %collective-permute-start.14 = (bf16[1,2,2,64]{3,2,1,0:T(2,128)(2,1)S(1)}, bf16[1,2,2,64]{3,2,1,0:T(2,128)(2,1)S(1)}, u32[]{:S(2)}, u32[]{:S(2)}) collective-permute-start(bf16[1,2,2,64]{3,2,1,0:T(2,128)(2,1)S(1)} %get-tuple-element.41), channel_id=1, source_target_pairs={} | collective-permute-start | bytes 1544 | tf_op jit(solution)/shard_map/ppermute | solution.py:19
  67.3 10.3 %collective-permute-start.11 = (bf16[1,64,2,64]{3,2,1,0:T(2,128)(2,1)S(1)}, bf16[1,64,2,64]{3,2,1,0:T(2,128)(2,1)S(1)}, u32[]{:S(2)}, u32[]{:S(2)}) collective-permute-start(bf16[1,64,2,64]{3,2,1,0:T(2,128)(2,1)S(1)} %get-tuple-element.21), channel_id=1, source_target_pairs={{0,1},{2,3},{4,5},{6,7},{8,9},{10,11},{12,13},{14,15},{16,17},{18,... | collective-permute-start | bytes 49160 | tf_op jit(solution)/shard_map/ppermute | solution.py:19
  71.7 6.0 %collective-permute-start.9 = (bf16[1,2,64,64]{3,1,2,0:T(2,128)(2,1)S(1)}, bf16[1,2,64,64]{3,1,2,0:T(2,128)(2,1)S(1)}, u32[]{:S(2)}, u32[]{:S(2)}) collective-permute-start(bf16[1,2,64,64]{3,1,2,0:T(2,128)(2,1)S(1)} %collective-permute-done.8), channel_id=1, source_target_pairs={{1,0},{3,2},{5,4},{7,6},{9,8},{11,10},{13,12},{15,14},{17,16},{19,... | collective-permute-start | bytes 49160 | tf_op jit(solution)/shard_map/ppermute | solution.py:19
  73.0 6.1 %collective-permute-start.15 = (bf16[1,2,64,64]{3,2,1,0:T(8,128)(2,1)S(1)}, bf16[1,2,64,64]{3,2,1,0:T(8,128)(2,1)S(1)}, u32[]{:S(2)}, u32[]{:S(2)}) collective-permute-start(bf16[1,2,64,64]{3,2,1,0:T(8,128)(2,1)S(1)} %collective-permute-done.13), channel_id=1, source_target_pairs={{0,1},{2,3},{4,5},{6,7},{8,9},{10,11},{12,13},{14,15},{16,17},{18,... | collective-permute-start | bytes 49160 | tf_op jit(solution)/shard_map/ppermute | solution.py:19
  87.2 6.4 %collective-permute-start.16 = (bf16[1,4,64,64]{3,1,2,0:T(4,128)(2,1)S(1)}, bf16[1,4,64,64]{3,1,2,0:T(4,128)(2,1)S(1)}, u32[]{:S(2)}, u32[]{:S(2)}) collective-permute-start(bf16[1,4,64,64]{3,1,2,0:T(4,128)(2,1)S(1)} %copy.301), channel_id=1, source_target_pairs={{0,2},{2,4},{4,6},{6,8},{8,10},{10,12},{12,14},{14,16},{16,18},{18... | collective-permute-start | bytes 98312 | tf_op jit(solution)/shard_map/ppermute | solution.py:13
  87.3 7.0 %collective-permute-start.21 = (bf16[1,4,64,64]{3,2,1,0:T(8,128)(2,1)S(1)}, bf16[1,4,64,64]{3,2,1,0:T(8,128)(2,1)S(1)}, u32[]{:S(2)}, u32[]{:S(2)}) collective-permute-start(bf16[1,4,64,64]{3,2,1,0:T(8,128)(2,1)S(1)} %get-tuple-element.20), channel_id=1, source_target_pairs={{0,30},{2,0},{4,2},{6,4},{8,6},{10,8},{12,10},{14,12},{16,14},{18,... | collective-permute-start | bytes 98312 | tf_op jit(solution)/shard_map/ppermute | solution.py:13
  91.8 9.5 %collective-permute-start.20 = (bf16[1,64,4,64]{3,1,2,0:T(8,128)(2,1)S(1)}, bf16[1,64,4,64]{3,1,2,0:T(8,128)(2,1)S(1)}, u32[]{:S(2)}, u32[]{:S(2)}) collective-permute-start(bf16[1,64,4,64]{3,1,2,0:T(8,128)(2,1)S(1)} %copy.302), channel_id=1, source_target_pairs={{1,0},{3,2},{5,4},{7,6},{9,8},{11,10},{13,12},{15,14},{17,16},{19,... | collective-permute-start | bytes 98312 | tf_op jit(solution)/shard_map/ppermute | solution.py:19
  93.6 12.6 %collective-permute-start.18 = (bf16[1,4,4,64]{3,1,2,0:T(4,128)(2,1)S(1)}, bf16[1,4,4,64]{3,1,2,0:T(4,128)(2,1)S(1)}, u32[]{:S(2)}, u32[]{:S(2)}) collective-permute-start(bf16[1,4,4,64]{3,1,2,0:T(4,128)(2,1)S(1)} %get-tuple-element.36), channel_id=1, source_target_pairs={} | collective-permute-start | bytes 6152 | tf_op jit(solution)/shard_map/ppermute | solution.py:19
  94.3 11.9 %collective-permute-start.22 = (bf16[1,4,4,64]{3,2,1,0:T(4,128)(2,1)S(1)}, bf16[1,4,4,64]{3,2,1,0:T(4,128)(2,1)S(1)}, u32[]{:S(2)}, u32[]{:S(2)}) collective-permute-start(bf16[1,4,4,64]{3,2,1,0:T(4,128)(2,1)S(1)} %get-tuple-element.37), channel_id=1, source_target_pairs={} | collective-permute-start | bytes 6152 | tf_op jit(solution)/shard_map/ppermute | solution.py:19
  95.8 10.4 %collective-permute-start.19 = (bf16[1,64,4,64]{3,2,1,0:T(4,128)(2,1)S(1)}, bf16[1,64,4,64]{3,2,1,0:T(4,128)(2,1)S(1)}, u32[]{:S(2)}, u32[]{:S(2)}) collective-permute-start(bf16[1,64,4,64]{3,2,1,0:T(4,128)(2,1)S(1)} %get-tuple-element.17), channel_id=1, source_target_pairs={{0,1},{2,3},{4,5},{6,7},{8,9},{10,11},{12,13},{14,15},{16,17},{18,... | collective-permute-start | bytes 98312 | tf_op jit(solution)/shard_map/ppermute | solution.py:19
  100.0 6.2 %collective-permute-start.17 = (bf16[1,4,64,64]{3,1,2,0:T(4,128)(2,1)S(1)}, bf16[1,4,64,64]{3,1,2,0:T(4,128)(2,1)S(1)}, u32[]{:S(2)}, u32[]{:S(2)}) collective-permute-start(bf16[1,4,64,64]{3,1,2,0:T(4,128)(2,1)S(1)} %collective-permute-done.16), channel_id=1, source_target_pairs={{1,0},{3,2},{5,4},{7,6},{9,8},{11,10},{13,12},{15,14},{17,16},{19,... | collective-permute-start | bytes 98312 | tf_op jit(solution)/shard_map/ppermute | solution.py:19
  101.3 6.4 %collective-permute-start.23 = (bf16[1,4,64,64]{3,2,1,0:T(8,128)(2,1)S(1)}, bf16[1,4,64,64]{3,2,1,0:T(8,128)(2,1)S(1)}, u32[]{:S(2)}, u32[]{:S(2)}) collective-permute-start(bf16[1,4,64,64]{3,2,1,0:T(8,128)(2,1)S(1)} %collective-permute-done.21), channel_id=1, source_target_pairs={{0,1},{2,3},{4,5},{6,7},{8,9},{10,11},{12,13},{14,15},{16,17},{18,... | collective-permute-start | bytes 98312 | tf_op jit(solution)/shard_map/ppermute | solution.py:19
  116.1 7.1 %collective-permute-start.24 = (bf16[1,8,64,64]{3,1,2,0:T(8,128)(2,1)S(1)}, bf16[1,8,64,64]{3,1,2,0:T(8,128)(2,1)S(1)}, u32[]{:S(2)}, u32[]{:S(2)}) collective-permute-start(bf16[1,8,64,64]{3,1,2,0:T(8,128)(2,1)S(1)} %copy.313), channel_id=1, source_target_pairs={{0,2},{2,4},{4,6},{6,8},{8,10},{10,12},{12,14},{14,16},{16,18},{18... | collective-permute-start | bytes 196616 | tf_op jit(solution)/shard_map/ppermute | solution.py:13
  116.2 7.7 %collective-permute-start.29 = (bf16[1,8,64,64]{3,2,1,0:T(8,128)(2,1)S(1)}, bf16[1,8,64,64]{3,2,1,0:T(8,128)(2,1)S(1)}, u32[]{:S(2)}, u32[]{:S(2)}) collective-permute-start(bf16[1,8,64,64]{3,2,1,0:T(8,128)(2,1)S(1)} %get-tuple-element.16), channel_id=1, source_target_pairs={{0,30},{2,0},{4,2},{6,4},{8,6},{10,8},{12,10},{14,12},{16,14},{18,... | collective-permute-start | bytes 196616 | tf_op jit(solution)/shard_map/ppermute | solution.py:13
  120.7 10.3 %collective-permute-start.28 = (bf16[1,64,8,64]{3,1,2,0:T(8,128)(2,1)S(1)}, bf16[1,64,8,64]{3,1,2,0:T(8,128)(2,1)S(1)}, u32[]{:S(2)}, u32[]{:S(2)}) collective-permute-start(bf16[1,64,8,64]{3,1,2,0:T(8,128)(2,1)S(1)} %copy.314), channel_id=1, source_target_pairs={{1,0},{3,2},{5,4},{7,6},{9,8},{11,10},{13,12},{15,14},{17,16},{19,... | collective-permute-start | bytes 196616 | tf_op jit(solution)/shard_map/ppermute | solution.py:19
  123.2 12.7 %collective-permute-start.26 = (bf16[1,8,8,64]{3,1,2,0:T(8,128)(2,1)S(1)}, bf16[1,8,8,64]{3,1,2,0:T(8,128)(2,1)S(1)}, u32[]{:S(2)}, u32[]{:S(2)}) collective-permute-start(bf16[1,8,8,64]{3,1,2,0:T(8,128)(2,1)S(1)} %get-tuple-element.32), channel_id=1, source_target_pairs={} | collective-permute-start | bytes 24584 | tf_op jit(solution)/shard_map/ppermute | solution.py:19
  123.9 12.0 %collective-permute-start.30 = (bf16[1,8,8,64]{3,2,1,0:T(8,128)(2,1)S(1)}, bf16[1,8,8,64]{3,2,1,0:T(8,128)(2,1)S(1)}, u32[]{:S(2)}, u32[]{:S(2)}) collective-permute-start(bf16[1,8,8,64]{3,2,1,0:T(8,128)(2,1)S(1)} %get-tuple-element.33), channel_id=1, source_target_pairs={} | collective-permute-start | bytes 24584 | tf_op jit(solution)/shard_map/ppermute | solution.py:19
  125.4 10.6 %collective-permute-start.27 = (bf16[1,64,8,64]{3,2,1,0:T(8,128)(2,1)S(1)}, bf16[1,64,8,64]{3,2,1,0:T(8,128)(2,1)S(1)}, u32[]{:S(2)}, u32[]{:S(2)}) collective-permute-start(bf16[1,64,8,64]{3,2,1,0:T(8,128)(2,1)S(1)} %get-tuple-element.13), channel_id=1, source_target_pairs={{0,1},{2,3},{4,5},{6,7},{8,9},{10,11},{12,13},{14,15},{16,17},{18,... | collective-permute-start | bytes 196616 | tf_op jit(solution)/shard_map/ppermute | solution.py:19
  129.7 6.9 %collective-permute-start.25 = (bf16[1,8,64,64]{3,1,2,0:T(8,128)(2,1)S(1)}, bf16[1,8,64,64]{3,1,2,0:T(8,128)(2,1)S(1)}, u32[]{:S(2)}, u32[]{:S(2)}) collective-permute-start(bf16[1,8,64,64]{3,1,2,0:T(8,128)(2,1)S(1)} %collective-permute-done.24), channel_id=1, source_target_pairs={{1,0},{3,2},{5,4},{7,6},{9,8},{11,10},{13,12},{15,14},{17,16},{19,... | collective-permute-start | bytes 196616 | tf_op jit(solution)/shard_map/ppermute | solution.py:19
  131.0 7.1 %collective-permute-start.31 = (bf16[1,8,64,64]{3,2,1,0:T(8,128)(2,1)S(1)}, bf16[1,8,64,64]{3,2,1,0:T(8,128)(2,1)S(1)}, u32[]{:S(2)}, u32[]{:S(2)}) collective-permute-start(bf16[1,8,64,64]{3,2,1,0:T(8,128)(2,1)S(1)} %collective-permute-done.29), channel_id=1, source_target_pairs={{0,1},{2,3},{4,5},{6,7},{8,9},{10,11},{12,13},{14,15},{16,17},{18,... | collective-permute-start | bytes 196616 | tf_op jit(solution)/shard_map/ppermute | solution.py:19
  (6 other events, 110.6 us)
where the time goes:
time: 147 us; the launch traced here: 146 us
  starting transfers between devices  68.6 us (47%)
  blocking collectives  24 us (16%)
  matrix products  23.6 us (16%)
  other arithmetic  16.7 us (11%)
  waiting for transfers between devices  6.41 us (4%)
  local copies, waits for them, and re-layouts  5.93 us (4%)
    ppermute x24, starting transfers between devices, from_behind(): return lax.ppermute(array, axis, pairs)  50.7 us
    all_gather x1, blocking collectives, on_device(): lax.all_gather(bin_embed, 'pos', axis=0, tiled=True)  24 us
    dot_general x36, matrix products, on_device(): jnp.einsum('prcd,de->prce', window, kernel, preferred_element_type=jnp.fl...  23.5 us
    ppermute x8, starting transfers between devices, shifted(): return lax.ppermute(value, axis, pairs)  17.9 us
    concatenate x4, other arithmetic, on_device(): padded = jnp.concatenate([top_band, middle, bottom_band], axis=1)  12.2 us
    ppermute x24, waiting for transfers between devices, from_behind(): return lax.ppermute(array, axis, pairs)  4.46 us
    convert_element_type x4, other arithmetic, on_device(): hidden = jax.nn.gelu(current.astype(jnp.float32)).astype(jnp.bfloat16)  3.75 us
  transfers between devices with their start and end apart: 32, of which 8 were waited for; matrix products, arithmetic and copies ran while one was open for 5% of the time, Pallas kernels for 0%

commit v1 on v0

v1 whole, which is shorter than its diff:
```python
import functools

import jax
import jax.numpy as jnp
from jax import lax
from jax.experimental import pallas as pl
from jax.experimental.pallas import tpu as pltpu
from jax.sharding import PartitionSpec as P

GROUP = 4
BASE = 8


def gelu(x):
    u = x * (0.7978845608028654 + 0.035677408136300125 * (x * x))
    half = 0.5 * x
    return half + half * jnp.tanh(u)


def place(col, halo, dil):
    u = col + halo
    within = u % (2 * dil)
    return (u // (2 * dil)) * dil + within % dil, within // dil


def columns(group, halo, dil):
    first = (group // dil) * 2 * dil + group % dil - halo
    return first, first + dil


def weights_kernel(layers, ch, cw_ref, t_ref):
    zero = jnp.zeros((ch, ch), t_ref.dtype)
    for l in range(layers):
        for i in range(3):
            taps = [cw_ref[l, (3 * i + j) * ch : (3 * i + j + 1) * ch, :] for j in range(3)]
            for a in range(6):
                row = [taps[a - b] if 0 <= a - b <= 2 else zero for b in (0, 2, 1, 3)]
                t_ref[l, (6 * i + a) * ch : (6 * i + a + 1) * ch, :] = jnp.concatenate(row, axis=1)


def tile_kernel(
    dims, slot_ref, emb_ref, pw_ref, pb_ref, t_ref, cb_ref, out_ref, x_ref, g_ref, h_ref, z_ref, bins_ref
):
    layers, tile, ch, npos, noff, order = dims
    wide = 2 * ch
    edge = 16
    rows = tile + 2 * edge
    halos = [2**layers - 2**l for l in range(layers + 1)]
    me, off = lax.axis_index("pos"), lax.axis_index("off")
    low = lax.broadcasted_iota(jnp.int32, (1, wide), 1) < ch

    def pick(lo, hi):
        return jnp.where(low, lo, hi)

    def both(value, half):
        turned = pltpu.roll(value, ch, 1)
        return pick(turned, value) if half else pick(value, turned)

    def block(b):
        away = jnp.bitwise_xor(slot_ref[lax.rem(b + npos, npos)], me)
        index = 0
        for place_in, bit in enumerate(order):
            index += jnp.bitwise_and(lax.shift_right_logical(away, bit), 1) << place_in
        return index

    pw = pw_ref[...]
    pw = jnp.concatenate([pw, pw], axis=1)

    def bins(b):
        first, here, last = (emb_ref[block(b + k)] for k in (-1, 0, 1))
        picked = jnp.concatenate([first[tile - edge :], here, last[:edge]], axis=0)
        return jnp.dot(picked, pw, preferred_element_type=jnp.float32).astype(jnp.bfloat16).astype(jnp.float32)

    row_bins = bins(me) + pb_ref[...]
    bins_ref[...] = bins(me + off)
    pairs = (tile + 2 * halos[0]) // 2
    first = edge - halos[0]
    col_bins = pick(
        bins_ref[pl.ds(first, pairs, stride=2), :], bins_ref[pl.ds(first + 1, pairs, stride=2), :]
    )

    def keep(a, b):
        return (jnp.abs(off + b - a) < noff).astype(jnp.float32)

    keeps = {(a, b): keep(a, b) for a in (-1, 0, 1) for b in (-1, 0, 1)}

    def band(col):
        return -1 if col < 0 else 1 if col >= tile else 0

    def activate(l, group, x, start):
        lo, hi = (band(c) for c in columns(group, halos[l], 2**l))
        size = x.shape[0]
        for a, begin, end in ((-1, 0, edge), (0, edge, edge + tile), (1, edge + tile, rows)):
            begin, end = max(begin, start), min(end, start + size)
            if begin >= end:
                continue
            g = gelu(x[begin - start : end - start])
            if (a, lo, hi) != (0, 0, 0):
                g = g * pick(keeps[a, lo], keeps[a, hi])
            g_ref[group, BASE + begin : BASE + end, :] = g

    def mirror(l):
        halo, dil = halos[l], 2**l
        groups = (tile + 2 * halo) // 2
        deep = -(-halo // 8) * 8
        top, mid, bot = BASE, BASE + edge, BASE + edge + tile

        def write_bottom(group, c1, c2, limit):
            if c1 >= limit:
                return
            lo = z_ref[(c1 + edge) * edge : (c1 + edge) * edge + deep, :]
            if c2 < limit:
                hi = z_ref[(c2 + edge) * edge : (c2 + edge) * edge + deep, :]
            else:
                hi = g_ref[group, bot : bot + deep, :]
            g_ref[group, bot : bot + deep, :] = pick(lo, hi)

        @pl.when(off == 0)
        def _():
            for k in range(halo):
                group, half = place(tile + k, halo, dil)
                z_ref[pl.ds(k, edge + tile, stride=edge), :] = both(g_ref[group, top:bot, :], half)
            for group in range(groups):
                write_bottom(group, *columns(group, halo, dil), tile)
            for r in range(tile):
                group, half = place(r, halo, dil)
                z_ref[pl.ds(r, edge, stride=tile), :] = both(g_ref[group, top:mid, :], half)
            for group in range(groups):
                c1, c2 = columns(group, halo, dil)
                if c1 < 0:
                    lo = z_ref[(c1 + edge) * tile : (c1 + edge + 1) * tile, :]
                    if c2 < 0:
                        hi = z_ref[(c2 + edge) * tile : (c2 + edge + 1) * tile, :]
                    else:
                        hi = g_ref[group, mid:bot, :]
                    g_ref[group, mid:bot, :] = pick(lo, hi)

        @pl.when(off == 1)
        def _():
            for k in range(halo):
                group, half = place(k, halo, dil)
                z_ref[pl.ds(k, edge, stride=edge), :] = both(g_ref[group, bot - edge : bot, :], half)
            for group in range(groups):
                write_bottom(group, *columns(group, halo, dil), 0)

    for group in range(pairs):
        x = row_bins + col_bins[group : group + 1]
        x_ref[0, group, :, :] = x
        activate(0, group, x, 0)

    for l in range(layers):
        dil = 2**l
        start = (edge - halos[l + 1]) // 8 * 8
        size = rows - 2 * start
        groups = (tile + 2 * halos[l]) // 2
        if l:
            mirror(l)
        for group in range(groups):
            for i in range(3):
                begin = BASE + start + (i - 1) * dil
                h_ref[i, group, 0:size, :] = g_ref[group, begin : begin + size, :].astype(jnp.bfloat16)
        blocks = [(j, e) for j in range((tile + 2 * halos[l + 1]) // (4 * dil)) for e in range(dil)]
        bias = cb_ref[l : l + 1, :]
        now, later = l % 2, (l + 1) % 2
        done = {}
        for at in range(0, len(blocks), GROUP):
            some = blocks[at : at + GROUP]
            lhs = jnp.concatenate(
                [
                    jnp.concatenate(
                        [h_ref[i, (2 * j + s) * dil + e, 0:size, :] for i in range(3) for s in range(3)], axis=1
                    )
                    for j, e in some
                ],
                axis=0,
            )
            acc = jnp.dot(lhs, t_ref[l], preferred_element_type=jnp.float32)
            for n, (j, e) in enumerate(some):
                old = [x_ref[now, (2 * j + s) * dil + e, start : start + size, :] for s in range(3)]
                carried = (
                    pick(pltpu.roll(old[0], ch, 1), old[1]),
                    pick(old[1], pltpu.roll(old[2], ch, 1)),
                )
                for s in range(2):
                    x = acc[n * size : (n + 1) * size, s * wide : (s + 1) * wide] + carried[s] + bias
                    group = j * 2 * dil + e + s * dil
                    if l + 1 < layers:
                        x_ref[later, group, start : start + size, :] = x
                        activate(l + 1, group, x, start)
                    else:
                        x_ref[later, group, start : start + size, :] = x
    final = layers % 2
    stretch = 2**layers
    for j in range(tile // (2 * stretch)):
        for e in range(0, stretch, 2):
            even, odd = (
                x_ref[final, j * stretch + e + s, edge : edge + tile, :] for s in range(2)
            )
            col = 2 * stretch * j + e
            out_ref[:, col * ch : (col + 2) * ch] = pick(even, pltpu.roll(odd, ch, 1)).astype(out_ref.dtype)
            col += stretch
            out_ref[:, col * ch : (col + 2) * ch] = pick(pltpu.roll(even, ch, 1), odd).astype(out_ref.dtype)


def on_device(bin_embed, block_slot, proj_weight, proj_bias, conv_weight, conv_bias):
    npos, noff = lax.axis_size("pos"), lax.axis_size("off")
    tile, emb = bin_embed.shape
    layers, taps, ch = conv_weight.shape
    bits = npos.bit_length() - 1
    order = tuple(reversed(range(bits)))
    table = bin_embed[None]
    for bit in order:
        there = lax.ppermute(table, "pos", [(i, i ^ (1 << bit)) for i in range(npos)])
        table = jnp.concatenate([table, there], axis=0)
    vmem = pl.BlockSpec(memory_space=pltpu.VMEM)
    toeplitz = pl.pallas_call(
        functools.partial(weights_kernel, layers, ch),
        out_shape=jax.ShapeDtypeStruct((layers, 2 * taps, 4 * ch), conv_weight.dtype),
        in_specs=[vmem],
        out_specs=vmem,
        cost_estimate=pl.CostEstimate(flops=2000000, bytes_accessed=4000000, transcendentals=0),
    )(conv_weight)
    wide = 2 * ch
    groups = tile // 2 + 2**layers - 1
    high = tile + 32
    out = pl.pallas_call(
        functools.partial(tile_kernel, (layers, tile, ch, npos, noff, order)),
        out_shape=jax.ShapeDtypeStruct((tile, tile * ch), jnp.bfloat16),
        in_specs=[pl.BlockSpec(memory_space=pltpu.SMEM)] + [vmem] * 5,
        out_specs=vmem,
        scratch_shapes=[
            pltpu.VMEM((2, groups, high, wide), jnp.float32),
            pltpu.VMEM((groups, high + 2 * BASE, wide), jnp.float32),
            pltpu.VMEM((3, groups, high, wide), jnp.bfloat16),
            pltpu.VMEM((16 * (tile + 16), wide), jnp.float32),
            pltpu.VMEM((high, wide), jnp.float32),
        ],
        compiler_params=pltpu.CompilerParams(vmem_limit_bytes=48 * 1024 * 1024),
        cost_estimate=pl.CostEstimate(flops=8000000000, bytes_accessed=4000000, transcendentals=2000000),
    )(
        block_slot,
        table,
        proj_weight,
        jnp.concatenate([proj_bias, proj_bias])[None],
        toeplitz,
        jnp.concatenate([conv_bias, conv_bias], axis=1),
    )
    return out.reshape(1, 1, tile, tile * ch)


def solution(mesh):
    placed = (P("pos", None), P(), P(), P(), P(), P())
    return jax.shard_map(
        on_device,
        mesh=mesh,
        in_specs=placed,
        out_specs=P("pos", "off", None, None),
        check_vma=False,
    )
```

time: 147 us -> 34.3 us (0.23)
  starting transfers between devices: 68.6 us -> 7.49 us
  blocking collectives: 24 us -> 0 us
  matrix products: 23.6 us -> 0 us
  other arithmetic: 16.7 us -> 2.38 us
  Pallas kernels: 0 us -> 14.1 us
  waiting for transfers between devices: 6.41 us -> 4.49 us
    ppermute x32 -> x4, starting transfers between devices: 68.6 us -> 7.49 us  [on_device(): there = lax.ppermute(table, 'pos', [(i, i ^ 1 << bit) for i in range(npos)])]
    all_gather x1 -> x0, blocking collectives: 24 us -> none  [on_device(): lax.all_gather(bin_embed, 'pos', axis=0, tiled=True)]
    dot_general x37 -> x0, matrix products: 23.6 us -> none  [the longest x36 23.5 us: on_device(): jnp.einsum('prcd,de->prce', window, kernel, preferred_element_type=jnp.fl...]
    pallas_call x0 -> x2, Pallas kernels: none -> 14.1 us  [the longest x1 11.4 us: on_device(): pl.pallas_call(functools.partial(tile_kernel, (layers, tile, ch, npos, no...]
    concatenate x8 -> x4, other arithmetic: 12.4 us -> 1.58 us  [the longest x1 0.83 us: on_device(): jnp.concatenate([conv_bias, conv_bias], axis=1)]
    unnamed x19 -> x12, local copies, waits for them, and re-layouts: 0.99 us -> 5.31 us
    convert_element_type x5 -> x0, other arithmetic: 3.85 us -> none  [the longest x4 3.75 us: on_device(): hidden = jax.nn.gelu(current.astype(jnp.float32)).astype(jnp.bfloat16)]
    ppermute x32 -> x4, waiting for transfers between devices: 6.41 us -> 4.49 us  [on_device(): there = lax.ppermute(table, 'pos', [(i, i ^ 1 << bit) for i in range(npos)])]
  transfers between devices with their start and end apart: 32 -> 4, of which waited for: 8 -> 3; matrix products, arithmetic and copies ran while one was open for 5% -> 16% of each run, Pallas kernels for 0% -> 8%
where the time goes in v1:
time: 34.3 us; the launch traced here: 33.8 us
  Pallas kernels  14.1 us (41%)
  starting transfers between devices  7.49 us (22%)
  local copies, waits for them, and re-layouts  5.33 us (16%)
  waiting for transfers between devices  4.49 us (13%)
  other arithmetic  2.38 us (7%)
    pallas_call x1, Pallas kernels, on_device(): pl.pallas_call(functools.partial(tile_kernel, (layers, tile, ch, npos, no...  11.4 us
    ppermute x4, starting transfers between devices, on_device(): there = lax.ppermute(table, 'pos', [(i, i ^ 1 << bit) for i in range(npos)])  7.49 us
    unnamed x12, local copies, waits for them, and re-layouts  5.31 us
    ppermute x4, waiting for transfers between devices, on_device(): there = lax.ppermute(table, 'pos', [(i, i ^ 1 << bit) for i in range(npos)])  4.49 us
    pallas_call x1, Pallas kernels, on_device(): pl.pallas_call(functools.partial(weights_kernel, layers, ch), out_shape=j...  2.7 us
    concatenate x1, other arithmetic, on_device(): jnp.concatenate([conv_bias, conv_bias], axis=1)  0.83 us
    broadcast_in_dim x1, other arithmetic, on_device(): jnp.concatenate([proj_bias, proj_bias])[None]  0.8 us
    concatenate x3, other arithmetic, on_device(): table = jnp.concatenate([table, there], axis=0)  0.75 us
  transfers between devices with their start and end apart: 4, of which 3 were waited for; matrix products, arithmetic and copies ran while one was open for 16% of the time, Pallas kernels for 8%

profile of v1, /device:TPU:0, one launch (start us, length us, event | category | flops | bytes accessed | tf_op | source)
XLA Modules:
  0.0 33.8 jit_solution(3745048306506156198)
XLA Ops:
  0.0 0.0 copy-start.2
  0.0 4.0 %collective-permute-start = (bf16[1,64,128]{2,1,0:T(8,128)(2,1)}, bf16[1,64,128]{2,1,0:T(8,128)(2,1)S(1)}, u32[]{:S(2)}, u32[]{:S(2)}) collective-permute-start(bf16[1,64,128]{2,1,0:T(8,128)(2,1)} %bitcast.5), channel_id=1, source_target_pairs={{0,16},{2,18},{4,20},{6,22},{8,24},{10,26},{12,28},{14,30},{16,0},... | collective-permute-start | bytes 49160 | tf_op jit(solution)/shard_map/ppermute | solution.py:213
  4.0 0.8 %constant_dynamic-update-slice_fusion.4 = bf16[16,64,128]{2,1,0:T(8,128)(2,1)S(1)} fusion(bf16[64,128]{1,0:T(8,128)(2,1)} %param.6), kind=kLoop, calls=%fused_computation.7 | loop fusion | bytes 32768
  4.8 0.8 %pad_maximum_fusion.3.cb_ref = f32[4,128]{1,0:T(4,128)S(1)} fusion(f32[4,64]{1,0:T(4,128)} %param.11), kind=kLoop, calls=%fused_computation.8 | loop fusion | flops 512 | bytes 3072 | tf_op jit(solution)/shard_map/concatenate | solution.py:246
  5.6 0.4 %collective-permute-done = bf16[1,64,128]{2,1,0:T(8,128)(2,1)S(1)} collective-permute-done((bf16[1,64,128]{2,1,0:T(8,128)(2,1)}, bf16[1,64,128]{2,1,0:T(8,128)(2,1)S(1)}, u32[]{:S(2)}, u32[]{:S(2)}) %collective-permute-start) | collective-permute-done | bytes 16416 | tf_op jit(solution)/shard_map/ppermute | solution.py:213
  6.0 0.7 %pad_maximum_fusion.2 = bf16[2,64,128]{2,1,0:T(8,128)(2,1)S(1)} fusion(bf16[1,64,128]{2,1,0:T(8,128)(2,1)S(1)} %collective-permute-done, bf16[1,64,128]{2,1,0:T(8,128)(2,1)} %bitcast.6), kind=kLoop, calls=%fused_computation.2 | loop fusion | flops 16384 | bytes 65536 | tf_op jit(solution)/shard_map/concatenate | solution.py:214
  6.8 1.8 %collective-permute-start.1 = (bf16[2,64,128]{2,1,0:T(8,128)(2,1)S(1)}, bf16[2,64,128]{2,1,0:T(8,128)(2,1)S(1)}, u32[]{:S(2)}, u32[]{:S(2)}) collective-permute-start(bf16[2,64,128]{2,1,0:T(8,128)(2,1)S(1)} %pad_maximum_fusion.2), channel_id=1, source_target_pairs={{0,8},{2,10},{4,12},{6,14},{8,0},{10,2},{12,4},{14,6},{16,24},{18,... | collective-permute-start | bytes 98312 | tf_op jit(solution)/shard_map/ppermute | solution.py:213
  8.6 0.8 %maximum_bitcast_fusion.pb_ref = f32[1,128]{1,0:T(1,128)S(1)} fusion(f32[64]{0:T(128)} %param.9), kind=kLoop, calls=%fused_computation.9 | loop fusion | flops 128 | bytes 768 | tf_op jit(solution)/shard_map/broadcast_in_dim | solution.py:244
  9.4 0.0 copy-start.1
  9.4 2.0 %copy.7.cw_ref = bf16[4,576,64]{2,1,0:T(8,128)(2,1)} copy(bf16[4,576,64]{1,2,0:T(8,128)(2,1)} %param.10) | data formatting | bytes 589824 | tf_op args[4]
  11.4 0.8 %copy.8.pw_ref = bf16[128,64]{1,0:T(8,128)(2,1)S(1)} copy(bf16[128,64]{0,1:T(8,128)(2,1)} %param.8) | data formatting | bytes 32768 | tf_op args[2]
  12.3 2.7 %shard_map.64.t_ref = bf16[4,1152,256]{2,1,0:T(8,128)(2,1)} custom-call(bf16[4,576,64]{2,1,0:T(8,128)(2,1)} %copy.7.cw_ref), custom_call_target="tpu_custom_call" | custom-call | flops 2000000 | bytes 4000000 | tf_op jit(solution)/shard_map/pallas_call | solution.py:216
  15.0 0.0 collective-permute-done.1
  15.0 0.0 copy-done.2
  15.0 1.6 %collective-permute-start.2 = (bf16[4,64,128]{2,1,0:T(8,128)(2,1)S(1)}, bf16[4,64,128]{2,1,0:T(8,128)(2,1)S(1)}, u32[]{:S(2)}, u32[]{:S(2)}) collective-permute-start(bf16[4,64,128]{2,1,0:T(8,128)(2,1)S(1)} %pad_maximum_fusion.1), channel_id=1, source_target_pairs={{0,4},{2,6},{4,0},{6,2},{8,12},{10,14},{12,8},{14,10},{16,20},{18,... | collective-permute-start | bytes 196616 | tf_op jit(solution)/shard_map/ppermute | solution.py:213
  16.6 2.8 %collective-permute-done.2 = bf16[4,64,128]{2,1,0:T(8,128)(2,1)S(1)} collective-permute-done((bf16[4,64,128]{2,1,0:T(8,128)(2,1)S(1)}, bf16[4,64,128]{2,1,0:T(8,128)(2,1)S(1)}, u32[]{:S(2)}, u32[]{:S(2)}) %collective-permute-start.2) | collective-permute-done | bytes 65568 | tf_op jit(solution)/shard_map/ppermute | solution.py:213
  19.3 0.1 collective-permute-start.3
  19.5 1.3 %collective-permute-done.3 = bf16[8,64,128]{2,1,0:T(8,128)(2,1)S(1)} collective-permute-done((bf16[8,64,128]{2,1,0:T(8,128)(2,1)S(1)}, bf16[8,64,128]{2,1,0:T(8,128)(2,1)S(1)}, u32[]{:S(2)}, u32[]{:S(2)}) %collective-permute-start.3) | collective-permute-done | bytes 131104 | tf_op jit(solution)/shard_map/ppermute | solution.py:213
  20.8 0.0 copy-done.1
  20.8 0.0 copy-start
  20.8 1.7 %copy-done = bf16[4,1152,256]{2,1,0:T(8,128)(2,1)S(1)} copy-done((bf16[4,1152,256]{2,1,0:T(8,128)(2,1)S(1)}, bf16[4,1152,256]{2,1,0:T(8,128)(2,1)}, u32[]{:S(2)}) %copy-start) | copy-done | bytes 2359320
  22.5 11.4 %shard_map.65 = bf16[64,4096]{1,0:T(8,128)(2,1)} custom-call(s32[16]{0:T(128)S(1)} %copy-done.1, bf16[16,64,128]{2,1,0:T(8,128)(2,1)S(1)} %constant_dynamic-update-slice_fusion.emb_ref, bf16[128,64]{1,0:T(8,128)(2,1)S(1)} %copy.8.pw_ref, f32[1,128]{1,0:T(1,128)S(1)} %maximum_bitcast_fusion.pb_ref, bf16[4,1152,256]{2,1,0:T(8,128)(2,1)S(1)} %copy-done, ...), custom_call_target="tpu_custom_call" | custom-call | flops 8000000000 | bytes 4000000 | tf_op jit(solution)/shard_map/pallas_call | solution.py:226
  (6 shorter events, 0.1 us)
Async XLA Ops:
  0.0 15.0 %copy-start.2 = (bf16[64,128]{1,0:T(8,128)(2,1)S(1)}, bf16[64,128]{1,0:T(8,128)(2,1)}, u32[]{:S(2)}) copy-start(bf16[64,128]{1,0:T(8,128)(2,1)} %param.6) | copy-start | bytes 49156
  0.0 6.0 %collective-permute-start = (bf16[1,64,128]{2,1,0:T(8,128)(2,1)}, bf16[1,64,128]{2,1,0:T(8,128)(2,1)S(1)}, u32[]{:S(2)}, u32[]{:S(2)}) collective-permute-start(bf16[1,64,128]{2,1,0:T(8,128)(2,1)} %bitcast.5), channel_id=1, source_target_pairs={{0,16},{2,18},{4,20},{6,22},{8,24},{10,26},{12,28},{14,30},{16,0},... | collective-permute-start | bytes 49160 | tf_op jit(solution)/shard_map/ppermute | solution.py:213
  6.8 8.2 %collective-permute-start.1 = (bf16[2,64,128]{2,1,0:T(8,128)(2,1)S(1)}, bf16[2,64,128]{2,1,0:T(8,128)(2,1)S(1)}, u32[]{:S(2)}, u32[]{:S(2)}) collective-permute-start(bf16[2,64,128]{2,1,0:T(8,128)(2,1)S(1)} %pad_maximum_fusion.2), channel_id=1, source_target_pairs={{0,8},{2,10},{4,12},{6,14},{8,0},{10,2},{12,4},{14,6},{16,24},{18,... | collective-permute-start | bytes 98312 | tf_op jit(solution)/shard_map/ppermute | solution.py:213
  9.4 11.4 %copy-start.1 = (s32[16]{0:T(128)S(1)}, s32[16]{0:T(128)}, u32[]{:S(2)}) copy-start(s32[16]{0:T(128)} %slot_ref.1) | copy-start | bytes 196
  15.0 4.3 %collective-permute-start.2 = (bf16[4,64,128]{2,1,0:T(8,128)(2,1)S(1)}, bf16[4,64,128]{2,1,0:T(8,128)(2,1)S(1)}, u32[]{:S(2)}, u32[]{:S(2)}) collective-permute-start(bf16[4,64,128]{2,1,0:T(8,128)(2,1)S(1)} %pad_maximum_fusion.1), channel_id=1, source_target_pairs={{0,4},{2,6},{4,0},{6,2},{8,12},{10,14},{12,8},{14,10},{16,20},{18,... | collective-permute-start | bytes 196616 | tf_op jit(solution)/shard_map/ppermute | solution.py:213
  19.3 1.4 %collective-permute-start.3 = (bf16[8,64,128]{2,1,0:T(8,128)(2,1)S(1)}, bf16[8,64,128]{2,1,0:T(8,128)(2,1)S(1)}, u32[]{:S(2)}, u32[]{:S(2)}) collective-permute-start(bf16[8,64,128]{2,1,0:T(8,128)(2,1)S(1)} %pad_maximum_fusion), channel_id=1, source_target_pairs={{0,2},{2,0},{4,6},{6,4},{8,10},{10,8},{12,14},{14,12},{16,18},{18,... | collective-permute-start | bytes 393224 | tf_op jit(solution)/shard_map/ppermute | solution.py:213
  20.8 1.7 %copy-start = (bf16[4,1152,256]{2,1,0:T(8,128)(2,1)S(1)}, bf16[4,1152,256]{2,1,0:T(8,128)(2,1)}, u32[]{:S(2)}) copy-start(bf16[4,1152,256]{2,1,0:T(8,128)(2,1)} %shard_map.64.t_ref) | copy-start | bytes 7077892

commit v2 on v1

--- a/solution.py
+++ b/solution.py
@@ -28,19 +28,22 @@
     return first, first + dil
 
 
-def weights_kernel(layers, ch, cw_ref, t_ref):
+def weights_kernel(ch, cw_ref, t_ref):
+    taps = jnp.transpose(cw_ref[...].astype(jnp.float32)).astype(t_ref.dtype)
     zero = jnp.zeros((ch, ch), t_ref.dtype)
-    for l in range(layers):
-        for i in range(3):
-            taps = [cw_ref[l, (3 * i + j) * ch : (3 * i + j + 1) * ch, :] for j in range(3)]
-            for a in range(6):
-                row = [taps[a - b] if 0 <= a - b <= 2 else zero for b in (0, 2, 1, 3)]
-                t_ref[l, (6 * i + a) * ch : (6 * i + a + 1) * ch, :] = jnp.concatenate(row, axis=1)
+    for i in range(3):
+        for a in range(6):
+            row = [
+                taps[(3 * i + a - b) * ch : (3 * i + a - b + 1) * ch] if 0 <= a - b <= 2 else zero
+                for b in (0, 2, 1, 3)
+            ]
+            t_ref[(6 * i + a) * ch : (6 * i + a + 1) * ch, :] = jnp.concatenate(row, axis=1)
 
 
 def tile_kernel(
-    dims, slot_ref, emb_ref, pw_ref, pb_ref, t_ref, cb_ref, out_ref, x_ref, g_ref, h_ref, z_ref, bins_ref
+    dims, slot_ref, emb_ref, pw_ref, pb_ref, cb_ref, *refs
 ):
+    t_refs, (out_ref, x_ref, g_ref, h_ref, z_ref, bins_ref) = refs[: dims[0]], refs[dims[0] :]
     layers, tile, ch, npos, noff, order = dims
     wide = 2 * ch
     edge = 16
@@ -64,12 +67,12 @@
         return index
 
     pw = pw_ref[...]
-    pw = jnp.concatenate([pw, pw], axis=1)
 
     def bins(b):
         first, here, last = (emb_ref[block(b + k)] for k in (-1, 0, 1))
         picked = jnp.concatenate([first[tile - edge :], here, last[:edge]], axis=0)
-        return jnp.dot(picked, pw, preferred_element_type=jnp.float32).astype(jnp.bfloat16).astype(jnp.float32)
+        made = lax.dot_general(picked, pw, (((1,), (1,)), ((), ())), preferred_element_type=jnp.float32)
+        return made.astype(jnp.bfloat16).astype(jnp.float32)
 
     row_bins = bins(me) + pb_ref[...]
     bins_ref[...] = bins(me + off)
@@ -174,7 +177,7 @@
                 ],
                 axis=0,
             )
-            acc = jnp.dot(lhs, t_ref[l], preferred_element_type=jnp.float32)
+            acc = jnp.dot(lhs, t_refs[l][...], preferred_element_type=jnp.float32)
             for n, (j, e) in enumerate(some):
                 old = [x_ref[now, (2 * j + s) * dil + e, start : start + size, :] for s in range(3)]
                 carried = (
@@ -202,31 +205,18 @@
             out_ref[:, col * ch : (col + 2) * ch] = pick(pltpu.roll(even, ch, 1), odd).astype(out_ref.dtype)
 
 
-def on_device(bin_embed, block_slot, proj_weight, proj_bias, conv_weight, conv_bias):
-    npos, noff = lax.axis_size("pos"), lax.axis_size("off")
-    tile, emb = bin_embed.shape
-    layers, taps, ch = conv_weight.shape
-    bits = npos.bit_length() - 1
-    order = tuple(reversed(range(bits)))
-    table = bin_embed[None]
-    for bit in order:
-        there = lax.ppermute(table, "pos", [(i, i ^ (1 << bit)) for i in range(npos)])
-        table = jnp.concatenate([table, there], axis=0)
+def tile_call(npos, noff, order, layers, block_slot, table, proj_weight, proj_bias, conv_bias, banded):
+    tile = table.shape[1]
+    ch = proj_weight.shape[0] // 2
     vmem = pl.BlockSpec(memory_space=pltpu.VMEM)
-    toeplitz = pl.pallas_call(
-        functools.partial(weights_kernel, layers, ch),
-        out_shape=jax.ShapeDtypeStruct((layers, 2 * taps, 4 * ch), conv_weight.dtype),
-        in_specs=[vmem],
-        out_specs=vmem,
-        cost_estimate=pl.CostEstimate(flops=2000000, bytes_accessed=4000000, transcendentals=0),
-    )(conv_weight)
     wide = 2 * ch
     groups = tile // 2 + 2**layers - 1
     high = tile + 32
-    out = pl.pallas_call(
+    return pl.pallas_call(
         functools.partial(tile_kernel, (layers, tile, ch, npos, noff, order)),
         out_shape=jax.ShapeDtypeStruct((tile, tile * ch), jnp.bfloat16),
-        in_specs=[pl.BlockSpec(memory_space=pltpu.SMEM)] + [vmem] * 5,
+        in_specs=[pl.BlockSpec(memory_space=pltpu.SMEM)]
+        + [vmem] * (4 + layers),
         out_specs=vmem,
         scratch_shapes=[
             pltpu.VMEM((2, groups, high, wide), jnp.float32),
@@ -237,14 +227,68 @@
         ],
         compiler_params=pltpu.CompilerParams(vmem_limit_bytes=48 * 1024 * 1024),
         cost_estimate=pl.CostEstimate(flops=8000000000, bytes_accessed=4000000, transcendentals=2000000),
-    )(
-        block_slot,
-        table,
-        proj_weight,
-        jnp.concatenate([proj_bias, proj_bias])[None],
-        toeplitz,
-        jnp.concatenate([conv_bias, conv_bias], axis=1),
-    )
+    )(block_slot, table, proj_weight, proj_bias, conv_bias, *banded)
+
+
+def parameters_kernel(emb_ref, pw_ref, pb_ref, cb_ref, own_ref, pw2_ref, pb2_ref, cb2_ref):
+    own_ref[0] = emb_ref[...]
+    for ref, to, axis in ((pw_ref, pw2_ref, 0), (pb_ref, pb2_ref, 1), (cb_ref, cb2_ref, 1)):
+        to[...] = jnp.concatenate([ref[...]] * 2, axis=axis)
+
+
+def parameters_call(bin_embed, proj_weight, proj_bias, conv_bias):
+    vmem = pl.BlockSpec(memory_space=pltpu.VMEM)
+    ch, emb = proj_weight.shape
+    return pl.pallas_call(
+        parameters_kernel,
+        out_shape=(
+            jax.ShapeDtypeStruct((1,) + bin_embed.shape, bin_embed.dtype),
+            jax.ShapeDtypeStruct((2 * ch, emb), proj_weight.dtype),
+            jax.ShapeDtypeStruct((1, 2 * ch), proj_bias.dtype),
+            jax.ShapeDtypeStruct((conv_bias.shape[0], 2 * ch), conv_bias.dtype),
+        ),
+        in_specs=[vmem] * 4,
+        out_specs=(vmem,) * 4,
+        cost_estimate=pl.CostEstimate(flops=1000000, bytes_accessed=1000000, transcendentals=0),
+    )(bin_embed, proj_weight, proj_bias, conv_bias)
+
+
+def band_call(weight):
+    ch, taps = weight.shape
+    vmem = pl.BlockSpec(memory_space=pltpu.VMEM)
+    return pl.pallas_call(
+        functools.partial(weights_kernel, ch),
+        out_shape=jax.ShapeDtypeStruct((2 * taps, 4 * ch), weight.dtype),
+        in_specs=[vmem],
+        out_specs=vmem,
+        cost_estimate=pl.CostEstimate(flops=1000000, bytes_accessed=1000000, transcendentals=0),
+    )(weight)
+
+
+def on_device(bin_embed, block_slot, proj_weight, proj_bias, conv_weight, conv_bias):
+    npos, noff = lax.axis_size("pos"), lax.axis_size("off")
+    tile, emb = bin_embed.shape
+    layers, taps, ch = conv_weight.shape
+    bits = npos.bit_length() - 1
+    order = tuple(reversed(range(bits)))
+    turned = jnp.swapaxes(conv_weight, 1, 2)
+    zero = lax.optimization_barrier(jnp.zeros((1,), block_slot.dtype))
+    table = bin_embed[None]
+    weights, banded, bands = [turned[l] for l in range(layers)], [], [0, 2, 2]
+    for stage, bit in enumerate(order):
+        there = lax.ppermute(table, "pos", [(i, i ^ (1 << bit)) for i in range(npos)])
+        if stage == 0:
+            table, *small = parameters_call(bin_embed, proj_weight.T, proj_bias[None], conv_bias)
+            slots = jnp.maximum(block_slot, zero)
+            there, table, small, slots, weights = lax.optimization_barrier((there, table, small, slots, weights))
+        else:
+            count = bands[stage] if stage < len(bands) else 0
+            made = [band_call(weight) for weight in weights[:count]]
+            there, made, weights = lax.optimization_barrier((there, made, weights[count:]))
+            banded += made
+        table = jnp.concatenate([table, there], axis=0)
+    banded += [band_call(weight) for weight in weights]
+    out = tile_call(npos, noff, order, layers, slots, table, *small, banded)
     return out.reshape(1, 1, tile, tile * ch)
 
 

time: 34.3 us -> 35.1 us (1.023)
  Pallas kernels: 14.1 us -> 20.6 us
  waiting for transfers between devices: 4.49 us -> 1.28 us
  other arithmetic: 2.38 us -> 0.82 us
  local copies, waits for them, and re-layouts: 5.33 us -> 4.57 us
    pallas_call x2 -> x6, Pallas kernels: 14.1 us -> 20.6 us  [the longest x1 11.5 us: tile_call(): pl.pallas_call(functools.partial(tile_kernel, (layers, tile, ch, npos, no...]
    ppermute x4, waiting for transfers between devices: 4.49 us -> 1.28 us  [on_device(): there = lax.ppermute(table, 'pos', [(i, i ^ 1 << bit) for i in range(npos)])]
    unnamed x12 -> x22, local copies, waits for them, and re-layouts: 5.31 us -> 2.84 us
    squeeze x0 -> x1, local copies, waits for them, and re-layouts: none -> 1.71 us  [on_device(): weights, banded, bands = ([turned[l] for l in range(layers)], [], [0, 2, 2])]
    concatenate x1 -> x0, other arithmetic: 0.83 us -> none  [on_device(): jnp.concatenate([conv_bias, conv_bias], axis=1)]
    broadcast_in_dim x1 -> x0, other arithmetic: 0.8 us -> none  [on_device(): jnp.concatenate([proj_bias, proj_bias])[None]]
  transfers between devices with their start and end apart: 4 -> 4, of which waited for: 3 -> 1; matrix products, arithmetic and copies ran while one was open for 16% -> 5% of each run, Pallas kernels for 8% -> 26%
where the time goes in v2:
time: 35.1 us; the launch traced here: 34.6 us
  Pallas kernels  20.6 us (59%)
  starting transfers between devices  7.24 us (21%)
  local copies, waits for them, and re-layouts  4.57 us (13%)
  waiting for transfers between devices  1.28 us (4%)
  other arithmetic  0.82 us (2%)
    pallas_call x1, Pallas kernels, tile_call(): pl.pallas_call(functools.partial(tile_kernel, (layers, tile, ch, npos, no...  11.5 us
    pallas_call x4, Pallas kernels, band_call(): pl.pallas_call(functools.partial(weights_kernel, ch), out_shape=jax.Shape...  7.7 us
    ppermute x4, starting transfers between devices, on_device(): there = lax.ppermute(table, 'pos', [(i, i ^ 1 << bit) for i in range(npos)])  7.24 us
    unnamed x22, local copies, waits for them, and re-layouts  2.84 us
    squeeze x1, local copies, waits for them, and re-layouts, on_device(): weights, banded, bands = ([turned[l] for l in range(layers)], [], [0, 2, 2])  1.71 us
    pallas_call x1, Pallas kernels, parameters_call(): pl.pallas_call(parameters_kernel, out_shape=(jax.ShapeDtypeStruct((1,) +...  1.39 us
    ppermute x4, waiting for transfers between devices, on_device(): there = lax.ppermute(table, 'pos', [(i, i ^ 1 << bit) for i in range(npos)])  1.28 us
    concatenate x3, other arithmetic, on_device(): table = jnp.concatenate([table, there], axis=0)  0.82 us
  transfers between devices with their start and end apart: 4, of which 1 were waited for; matrix products, arithmetic and copies ran while one was open for 5% of the time, Pallas kernels for 26%

profile of v2, /device:TPU:0, one launch (start us, length us, event | category | flops | bytes accessed | tf_op | source)
XLA Modules:
  0.0 34.6 jit_solution(1316954591769007880)
XLA Ops:
  0.0 4.0 %collective-permute-start = (bf16[1,64,128]{2,1,0:T(8,128)(2,1)}, bf16[1,64,128]{2,1,0:T(8,128)(2,1)S(1)}, u32[]{:S(2)}, u32[]{:S(2)}) collective-permute-start(bf16[1,64,128]{2,1,0:T(8,128)(2,1)} %bitcast.16), channel_id=1, source_target_pairs={{0,16},{2,18},{4,20},{6,22},{8,24},{10,26},{12,28},{14,30},{16,0},... | collective-permute-start | bytes 49160 | tf_op jit(solution)/shard_map/ppermute | solution.py:279
  4.0 1.7 %slice_bitcast_fusion = (bf16[64,576]{1,0:T(8,128)(2,1)}, bf16[64,576]{1,0:T(8,128)(2,1)}, bf16[64,576]{1,0:T(8,128)(2,1)}, bf16[64,576]{1,0:T(8,128)(2,1)}) fusion(bf16[4,64,576]{2,1,0:T(8,128)(2,1)} %bitcast.14), kind=kLoop, calls=%fused_computation.1 | loop fusion | bytes 589824 | tf_op jit(solution)/shard_map/squeeze | solution.py:277
  5.8 0.0 copy-start.8
  5.8 0.7 %copy-done.8 = s32[16]{0:T(128)S(1)} copy-done((s32[16]{0:T(128)S(1)}, s32[16]{0:T(128)}, u32[]{:S(2)}) %copy-start.8) | copy-done | bytes 88
  6.4 1.4 %shard_map.64 = (bf16[1,64,128]{2,1,0:T(8,128)(2,1)}, bf16[128,128]{1,0:T(8,128)(2,1)}, f32[1,128]{1,0:T(1,128)}, f32[4,128]{1,0:T(4,128)}) custom-call(bf16[64,128]{1,0:T(8,128)(2,1)} %emb_ref.1, bf16[64,128]{1,0:T(8,128)(2,1)} %bitcast.15, f32[1,64]{1,0:T(1,128)} %bitcast.17, f32[4,64]{1,0:T(4,128)} %cb_ref.1), custom_call_target="tpu_custom_call" | custom-call | flops 1000000 | bytes 1000000 | tf_op jit(solution)/shard_map/pallas_call | solution.py:242
  7.8 0.0 collective-permute-done
  7.8 0.0 copy-start.7
  7.8 0.8 %pad_maximum_fusion.2 = bf16[2,64,128]{2,1,0:T(8,128)(2,1)S(1)} fusion(bf16[1,64,128]{2,1,0:T(8,128)(2,1)S(1)} %collective-permute-done, bf16[1,64,128]{2,1,0:T(8,128)(2,1)} %get-tuple-element.32), kind=kLoop, calls=%fused_computation.6 | loop fusion | flops 16384 | bytes 65536 | tf_op jit(solution)/shard_map/concatenate | solution.py:289
  8.6 1.6 %collective-permute-start.1 = (bf16[2,64,128]{2,1,0:T(8,128)(2,1)S(1)}, bf16[2,64,128]{2,1,0:T(8,128)(2,1)S(1)}, u32[]{:S(2)}, u32[]{:S(2)}) collective-permute-start(bf16[2,64,128]{2,1,0:T(8,128)(2,1)S(1)} %pad_maximum_fusion.2), channel_id=1, source_target_pairs={{0,8},{2,10},{4,12},{6,14},{8,0},{10,2},{12,4},{14,6},{16,24},{18,... | collective-permute-start | bytes 98312 | tf_op jit(solution)/shard_map/ppermute | solution.py:279
  10.2 0.0 copy-done.7
  10.2 1.9 %shard_map.65.refs_0_ = bf16[1152,256]{1,0:T(8,128)(2,1)} custom-call(bf16[64,576]{1,0:T(8,128)(2,1)} %get-tuple-element.34.cw_ref), custom_call_target="tpu_custom_call" | custom-call | flops 1000000 | bytes 1000000 | tf_op jit(solution)/shard_map/pallas_call | solution.py:259
  12.1 1.9 %shard_map.66.refs_1_ = bf16[1152,256]{1,0:T(8,128)(2,1)} custom-call(bf16[64,576]{1,0:T(8,128)(2,1)} %get-tuple-element.35.cw_ref), custom_call_target="tpu_custom_call" | custom-call | flops 1000000 | bytes 1000000 | tf_op jit(solution)/shard_map/pallas_call | solution.py:259
  14.0 0.0 collective-permute-done.1
  14.0 1.6 %collective-permute-start.2 = (bf16[4,64,128]{2,1,0:T(8,128)(2,1)S(1)}, bf16[4,64,128]{2,1,0:T(8,128)(2,1)S(1)}, u32[]{:S(2)}, u32[]{:S(2)}) collective-permute-start(bf16[4,64,128]{2,1,0:T(8,128)(2,1)S(1)} %pad_maximum_fusion.1), channel_id=1, source_target_pairs={{0,4},{2,6},{4,0},{6,2},{8,12},{10,14},{12,8},{14,10},{16,20},{18,... | collective-permute-start | bytes 196616 | tf_op jit(solution)/shard_map/ppermute | solution.py:279
  15.6 1.9 %shard_map.67.refs_2_ = bf16[1152,256]{1,0:T(8,128)(2,1)} custom-call(bf16[64,576]{1,0:T(8,128)(2,1)} %get-tuple-element.39.cw_ref), custom_call_target="tpu_custom_call" | custom-call | flops 1000000 | bytes 1000000 | tf_op jit(solution)/shard_map/pallas_call | solution.py:259
  17.5 0.0 copy-start
  17.5 2.0 %shard_map.68.refs_3_ = bf16[1152,256]{1,0:T(8,128)(2,1)} custom-call(bf16[64,576]{1,0:T(8,128)(2,1)} %get-tuple-element.40.cw_ref), custom_call_target="tpu_custom_call" | custom-call | flops 1000000 | bytes 1000000 | tf_op jit(solution)/shard_map/pallas_call | solution.py:259
  19.5 0.0 collective-permute-done.2
  19.5 0.1 collective-permute-start.3
  19.6 0.0 copy-start.4
  19.6 0.0 copy-start.5
  19.6 0.0 copy-start.6
  19.6 1.3 %collective-permute-done.3 = bf16[8,64,128]{2,1,0:T(8,128)(2,1)S(1)} collective-permute-done((bf16[8,64,128]{2,1,0:T(8,128)(2,1)S(1)}, bf16[8,64,128]{2,1,0:T(8,128)(2,1)S(1)}, u32[]{:S(2)}, u32[]{:S(2)}) %collective-permute-start.3) | collective-permute-done | bytes 131104 | tf_op jit(solution)/shard_map/ppermute | solution.py:279
  20.9 0.0 copy-done
  20.9 0.0 copy-done.1
  21.0 0.0 copy-done.4
  21.0 0.0 copy-done.5
  21.0 0.0 copy-done.6
  21.0 0.0 copy-start.2
  21.0 1.1 %copy-done.2 = bf16[1152,256]{1,0:T(8,128)(2,1)S(1)} copy-done((bf16[1152,256]{1,0:T(8,128)(2,1)S(1)}, bf16[1152,256]{1,0:T(8,128)(2,1)}, u32[]{:S(2)}) %copy-start.2) | copy-done | bytes 589848
  22.0 1.1 %copy-done.3 = bf16[1152,256]{1,0:T(8,128)(2,1)S(1)} copy-done((bf16[1152,256]{1,0:T(8,128)(2,1)S(1)}, bf16[1152,256]{1,0:T(8,128)(2,1)}, u32[]{:S(2)}) %copy-start.3) | copy-done | bytes 589848
  23.1 11.5 %shard_map.69 = bf16[64,4096]{1,0:T(8,128)(2,1)} custom-call(s32[16]{0:T(128)S(1)} %broadcast_maximum_fusion.slot_ref, bf16[16,64,128]{2,1,0:T(8,128)(2,1)S(1)} %constant_dynamic-update-slice_fusion.emb_ref, bf16[128,128]{1,0:T(8,128)(2,1)S(1)} %copy-done.4, f32[1,128]{1,0:T(1,128)S(1)} %copy-done.6, f32[4,128]{1,0:T(4,128)S(1)} %copy-done.5, ...), custom_call_target="tpu_custom_call" | custom-call | flops 8000000000 | bytes 4000000 | tf_op jit(solution)/shard_map/pallas_call | solution.py:215
  (10 shorter events, 0.1 us)
Async XLA Ops:
  0.0 7.8 %collective-permute-start = (bf16[1,64,128]{2,1,0:T(8,128)(2,1)}, bf16[1,64,128]{2,1,0:T(8,128)(2,1)S(1)}, u32[]{:S(2)}, u32[]{:S(2)}) collective-permute-start(bf16[1,64,128]{2,1,0:T(8,128)(2,1)} %bitcast.16), channel_id=1, source_target_pairs={{0,16},{2,18},{4,20},{6,22},{8,24},{10,26},{12,28},{14,30},{16,0},... | collective-permute-start | bytes 49160 | tf_op jit(solution)/shard_map/ppermute | solution.py:279
  5.8 0.7 %copy-start.8 = (s32[16]{0:T(128)S(1)}, s32[16]{0:T(128)}, u32[]{:S(2)}) copy-start(s32[16]{0:T(128)} %param.7) | copy-start | bytes 196
  7.8 2.4 %copy-start.7 = (bf16[1,64,128]{2,1,0:T(8,128)(2,1)S(1)}, bf16[1,64,128]{2,1,0:T(8,128)(2,1)}, u32[]{:S(2)}) copy-start(bf16[1,64,128]{2,1,0:T(8,128)(2,1)} %get-tuple-element.32) | copy-start | bytes 49156
  8.6 5.4 %collective-permute-start.1 = (bf16[2,64,128]{2,1,0:T(8,128)(2,1)S(1)}, bf16[2,64,128]{2,1,0:T(8,128)(2,1)S(1)}, u32[]{:S(2)}, u32[]{:S(2)}) collective-permute-start(bf16[2,64,128]{2,1,0:T(8,128)(2,1)S(1)} %pad_maximum_fusion.2), channel_id=1, source_target_pairs={{0,8},{2,10},{4,12},{6,14},{8,0},{10,2},{12,4},{14,6},{16,24},{18,... | collective-permute-start | bytes 98312 | tf_op jit(solution)/shard_map/ppermute | solution.py:279
  14.0 5.5 %collective-permute-start.2 = (bf16[4,64,128]{2,1,0:T(8,128)(2,1)S(1)}, bf16[4,64,128]{2,1,0:T(8,128)(2,1)S(1)}, u32[]{:S(2)}, u32[]{:S(2)}) collective-permute-start(bf16[4,64,128]{2,1,0:T(8,128)(2,1)S(1)} %pad_maximum_fusion.1), channel_id=1, source_target_pairs={{0,4},{2,6},{4,0},{6,2},{8,12},{10,14},{12,8},{14,10},{16,20},{18,... | collective-permute-start | bytes 196616 | tf_op jit(solution)/shard_map/ppermute | solution.py:279
  17.5 3.5 %copy-start = (bf16[1152,256]{1,0:T(8,128)(2,1)S(1)}, bf16[1152,256]{1,0:T(8,128)(2,1)}, u32[]{:S(2)}) copy-start(bf16[1152,256]{1,0:T(8,128)(2,1)} %shard_map.65.refs_0_) | copy-start | bytes 1769476
  17.5 3.5 %copy-start.1 = (bf16[1152,256]{1,0:T(8,128)(2,1)S(1)}, bf16[1152,256]{1,0:T(8,128)(2,1)}, u32[]{:S(2)}) copy-start(bf16[1152,256]{1,0:T(8,128)(2,1)} %shard_map.66.refs_1_) | copy-start | bytes 1769476
  19.5 1.4 %collective-permute-start.3 = (bf16[8,64,128]{2,1,0:T(8,128)(2,1)S(1)}, bf16[8,64,128]{2,1,0:T(8,128)(2,1)S(1)}, u32[]{:S(2)}, u32[]{:S(2)}) collective-permute-start(bf16[8,64,128]{2,1,0:T(8,128)(2,1)S(1)} %pad_maximum_fusion), channel_id=1, source_target_pairs={{0,2},{2,0},{4,6},{6,4},{8,10},{10,8},{12,14},{14,12},{16,18},{18,... | collective-permute-start | bytes 393224 | tf_op jit(solution)/shard_map/ppermute | solution.py:279
  19.6 1.3 %copy-start.4 = (bf16[128,128]{1,0:T(8,128)(2,1)S(1)}, bf16[128,128]{1,0:T(8,128)(2,1)}, u32[]{:S(2)}) copy-start(bf16[128,128]{1,0:T(8,128)(2,1)} %get-tuple-element.42.pw_ref) | copy-start | bytes 98308
  19.6 1.3 %copy-start.5 = (f32[4,128]{1,0:T(4,128)S(1)}, f32[4,128]{1,0:T(4,128)}, u32[]{:S(2)}) copy-start(f32[4,128]{1,0:T(4,128)} %get-tuple-element.44.cb_ref) | copy-start | bytes 6148
  19.6 1.3 %copy-start.6 = (f32[1,128]{1,0:T(1,128)S(1)}, f32[1,128]{1,0:T(1,128)}, u32[]{:S(2)}) copy-start(f32[1,128]{1,0:T(1,128)} %get-tuple-element.43.pb_ref) | copy-start | bytes 1540
  21.0 1.1 %copy-start.2 = (bf16[1152,256]{1,0:T(8,128)(2,1)S(1)}, bf16[1152,256]{1,0:T(8,128)(2,1)}, u32[]{:S(2)}) copy-start(bf16[1152,256]{1,0:T(8,128)(2,1)} %shard_map.67.refs_2_) | copy-start | bytes 1769476
  22.0 1.1 %copy-start.3 = (bf16[1152,256]{1,0:T(8,128)(2,1)S(1)}, bf16[1152,256]{1,0:T(8,128)(2,1)}, u32[]{:S(2)}) copy-start(bf16[1152,256]{1,0:T(8,128)(2,1)} %shard_map.68.refs_3_) | copy-start | bytes 1769476

commit v3 on v2

--- a/solution.py
+++ b/solution.py
@@ -28,16 +28,17 @@
     return first, first + dil
 
 
-def weights_kernel(ch, cw_ref, t_ref):
-    taps = jnp.transpose(cw_ref[...].astype(jnp.float32)).astype(t_ref.dtype)
-    zero = jnp.zeros((ch, ch), t_ref.dtype)
-    for i in range(3):
-        for a in range(6):
-            row = [
-                taps[(3 * i + a - b) * ch : (3 * i + a - b + 1) * ch] if 0 <= a - b <= 2 else zero
-                for b in (0, 2, 1, 3)
-            ]
-            t_ref[(6 * i + a) * ch : (6 * i + a + 1) * ch, :] = jnp.concatenate(row, axis=1)
+def weights_kernel(ch, which, cw_ref, *t_refs):
+    zero = jnp.zeros((ch, ch), cw_ref.dtype)
+    for l, t_ref in zip(which, t_refs):
+        taps = jnp.transpose(cw_ref[l].astype(jnp.float32)).astype(t_ref.dtype)
+        for i in range(3):
+            for a in range(6):
+                row = [
+                    taps[(3 * i + a - b) * ch : (3 * i + a - b + 1) * ch] if 0 <= a - b <= 2 else zero
+                    for b in (0, 2, 1, 3)
+                ]
+                t_ref[(6 * i + a) * ch : (6 * i + a + 1) * ch, :] = jnp.concatenate(row, axis=1)
 
 
 def tile_kernel(
@@ -230,39 +231,41 @@
     )(block_slot, table, proj_weight, proj_bias, conv_bias, *banded)
 
 
-def parameters_kernel(emb_ref, pw_ref, pb_ref, cb_ref, own_ref, pw2_ref, pb2_ref, cb2_ref):
+def parameters_kernel(emb_ref, pw_ref, pb_ref, cb_ref, cw_ref, own_ref, pw2_ref, pb2_ref, cb2_ref, cw2_ref):
     own_ref[0] = emb_ref[...]
+    cw2_ref[...] = cw_ref[...]
     for ref, to, axis in ((pw_ref, pw2_ref, 0), (pb_ref, pb2_ref, 1), (cb_ref, cb2_ref, 1)):
         to[...] = jnp.concatenate([ref[...]] * 2, axis=axis)
 
 
-def parameters_call(bin_embed, proj_weight, proj_bias, conv_bias):
+def parameters_call(bin_embed, proj_weight, proj_bias, conv_bias, weights):
     vmem = pl.BlockSpec(memory_space=pltpu.VMEM)
     ch, emb = proj_weight.shape
     return pl.pallas_call(
         parameters_kernel,
         out_shape=(
-            jax.ShapeDtypeStruct((1,) + bin_embed.shape, bin_embed.dtype),
-            jax.ShapeDtypeStruct((2 * ch, emb), proj_weight.dtype),
-            jax.ShapeDtypeStruct((1, 2 * ch), proj_bias.dtype),
-            jax.ShapeDtypeStruct((conv_bias.shape[0], 2 * ch), conv_bias.dtype),
+            pltpu.VMEM((1,) + bin_embed.shape, bin_embed.dtype),
+            pltpu.VMEM((2 * ch, emb), proj_weight.dtype),
+            pltpu.VMEM((1, 2 * ch), proj_bias.dtype),
+            pltpu.VMEM((conv_bias.shape[0], 2 * ch), conv_bias.dtype),
+            pltpu.VMEM(weights.shape, weights.dtype),
         ),
-        in_specs=[vmem] * 4,
-        out_specs=(vmem,) * 4,
+        in_specs=[vmem] * 5,
+        out_specs=(vmem,) * 5,
         cost_estimate=pl.CostEstimate(flops=1000000, bytes_accessed=1000000, transcendentals=0),
-    )(bin_embed, proj_weight, proj_bias, conv_bias)
-
-
-def band_call(weight):
-    ch, taps = weight.shape
+    )(bin_embed, proj_weight, proj_bias, conv_bias, weights)
+
+
+def band_call(weights, which):
+    layers, ch, taps = weights.shape
     vmem = pl.BlockSpec(memory_space=pltpu.VMEM)
     return pl.pallas_call(
-        functools.partial(weights_kernel, ch),
-        out_shape=jax.ShapeDtypeStruct((2 * taps, 4 * ch), weight.dtype),
+        functools.partial(weights_kernel, ch, which),
+        out_shape=(pltpu.VMEM((2 * taps, 4 * ch), weights.dtype),) * len(which),
         in_specs=[vmem],
-        out_specs=vmem,
+        out_specs=(vmem,) * len(which),
         cost_estimate=pl.CostEstimate(flops=1000000, bytes_accessed=1000000, transcendentals=0),
-    )(weight)
+    )(weights)
 
 
 def on_device(bin_embed, block_slot, proj_weight, proj_bias, conv_weight, conv_bias):
@@ -274,20 +277,20 @@
     turned = jnp.swapaxes(conv_weight, 1, 2)
     zero = lax.optimization_barrier(jnp.zeros((1,), block_slot.dtype))
     table = bin_embed[None]
-    weights, banded, bands = [turned[l] for l in range(layers)], [], [0, 2, 2]
+    banded, todo = [], tuple(range(layers))
     for stage, bit in enumerate(order):
         there = lax.ppermute(table, "pos", [(i, i ^ (1 << bit)) for i in range(npos)])
         if stage == 0:
-            table, *small = parameters_call(bin_embed, proj_weight.T, proj_bias[None], conv_bias)
+            table, *small, turned = parameters_call(bin_embed, proj_weight.T, proj_bias[None], conv_bias, turned)
             slots = jnp.maximum(block_slot, zero)
-            there, table, small, slots, weights = lax.optimization_barrier((there, table, small, slots, weights))
-        else:
-            count = bands[stage] if stage < len(bands) else 0
-            made = [band_call(weight) for weight in weights[:count]]
-            there, made, weights = lax.optimization_barrier((there, made, weights[count:]))
-            banded += made
+            there, table, small, slots, turned = lax.optimization_barrier((there, table, small, slots, turned))
+        elif todo:
+            made = band_call(turned, todo[:2])
+            there, made, turned = lax.optimization_barrier((there, made, turned))
+            banded, todo = banded + list(made), todo[2:]
         table = jnp.concatenate([table, there], axis=0)
-    banded += [band_call(weight) for weight in weights]
+    if todo:
+        banded += band_call(turned, todo)
     out = tile_call(npos, noff, order, layers, slots, table, *small, banded)
     return out.reshape(1, 1, tile, tile * ch)
 

time: 35.1 us -> 27.2 us (0.77)
  Pallas kernels: 20.6 us -> 14.9 us
  local copies, waits for them, and re-layouts: 4.57 us -> 0.78 us
  waiting for transfers between devices: 1.28 us -> 3.31 us
  other arithmetic: 0.82 us -> 0.03 us
  starting transfers between devices: 7.24 us -> 7.94 us
    pallas_call x5 -> x3, Pallas kernels: 9.09 us -> 3.59 us  [the longest x2 2.45 us: band_call(): pl.pallas_call(functools.partial(weights_kernel, ch, which), out_shape=(p...]
    unnamed x22 -> x8, local copies, waits for them, and re-layouts: 2.84 us -> 0.76 us
    ppermute x4, waiting for transfers between devices: 1.28 us -> 3.31 us  [on_device(): there = lax.ppermute(table, 'pos', [(i, i ^ 1 << bit) for i in range(npos)])]
    squeeze x1 -> x0, local copies, waits for them, and re-layouts: 1.71 us -> none  [on_device(): weights, banded, bands = ([turned[l] for l in range(layers)], [], [0, 2, 2])]
    concatenate x3, other arithmetic: 0.82 us -> 0.03 us  [on_device(): table = jnp.concatenate([table, there], axis=0)]
    ppermute x4, starting transfers between devices: 7.24 us -> 7.94 us  [on_device(): there = lax.ppermute(table, 'pos', [(i, i ^ 1 << bit) for i in range(npos)])]
  transfers between devices with their start and end apart: 4 -> 4, of which waited for: 1 -> 4; matrix products, arithmetic and copies ran while one was open for 5% -> 0% of each run, Pallas kernels for 26% -> 13%
where the time goes in v3:
time: 27.2 us; the launch traced here: 27 us
  Pallas kernels  14.9 us (55%)
  starting transfers between devices  7.94 us (29%)
  waiting for transfers between devices  3.31 us (12%)
  local copies, waits for them, and re-layouts  0.78 us (3%)
    pallas_call x1, Pallas kernels, tile_call(): pl.pallas_call(functools.partial(tile_kernel, (layers, tile, ch, npos, no...  11.3 us
    ppermute x4, starting transfers between devices, on_device(): there = lax.ppermute(table, 'pos', [(i, i ^ 1 << bit) for i in range(npos)])  7.94 us
    ppermute x4, waiting for transfers between devices, on_device(): there = lax.ppermute(table, 'pos', [(i, i ^ 1 << bit) for i in range(npos)])  3.31 us
    pallas_call x2, Pallas kernels, band_call(): pl.pallas_call(functools.partial(weights_kernel, ch, which), out_shape=(p...  2.45 us
    pallas_call x1, Pallas kernels, parameters_call(): pl.pallas_call(parameters_kernel, out_shape=(pltpu.VMEM((1,) + bin_embed....  1.14 us
    unnamed x8, local copies, waits for them, and re-layouts  0.76 us
  transfers between devices with their start and end apart: 4, of which 4 were waited for; matrix products, arithmetic and copies ran while one was open for 0% of the time, Pallas kernels for 13%

profile of v3, /device:TPU:0, one launch (start us, length us, event | category | flops | bytes accessed | tf_op | source)
XLA Modules:
  0.0 27.0 jit_solution(1605121326981040952)
XLA Ops:
  0.0 0.0 copy-start.1
  0.0 4.0 %collective-permute-start = (bf16[1,64,128]{2,1,0:T(8,128)(2,1)}, bf16[1,64,128]{2,1,0:T(8,128)(2,1)S(1)}, u32[]{:S(2)}, u32[]{:S(2)}) collective-permute-start(bf16[1,64,128]{2,1,0:T(8,128)(2,1)} %bitcast.8), channel_id=1, source_target_pairs={{0,16},{2,18},{4,20},{6,22},{8,24},{10,26},{12,28},{14,30},{16,0},... | collective-permute-start | bytes 49160 | tf_op jit(solution)/shard_map/ppermute | solution.py:282
  4.0 0.0 copy-done.1
  4.0 1.1 %shard_map.64 = (bf16[1,64,128]{2,1,0:T(8,128)(2,1)S(1)}, bf16[128,128]{1,0:T(8,128)(2,1)S(1)}, f32[1,128]{1,0:T(1,128)S(1)}, f32[4,128]{1,0:T(4,128)S(1)}, bf16[4,64,576]{2,1,0:T(8,128)(2,1)S(1)}) custom-call(bf16[64,128]{1,0:T(8,128)(2,1)} %emb_ref.1, bf16[64,128]{1,0:T(8,128)(2,1)} %bitcast.7, f32[1,64]{1,0:T(1,128)} %bitcast.9, f32[4,64]{1,0:T(4,128)} %cb_ref.1, ...), custom_call_target="tpu_custom_call" | custom-call | flops 1000000 | bytes 1000000 | tf_op jit(solution)/shard_map/pallas_call | solution.py:244
  5.2 0.0 copy-start
  5.2 0.7 %copy-done = bf16[4,64,576]{2,1,0:T(8,128)(2,1)} copy-done((bf16[4,64,576]{2,1,0:T(8,128)(2,1)}, bf16[4,64,576]{2,1,0:T(8,128)(2,1)S(1)}, u32[]{:S(2)}) %copy-start) | copy-done | bytes 294936
  5.9 0.1 collective-permute-done
  6.0 1.9 %collective-permute-start.1 = (bf16[2,64,128]{2,1,0:T(8,128)(2,1)S(1)}, bf16[2,64,128]{2,1,0:T(8,128)(2,1)S(1)}, u32[]{:S(2)}, u32[]{:S(2)}) collective-permute-start(bf16[2,64,128]{2,1,0:T(8,128)(2,1)S(1)} %pad_maximum_fusion.2), channel_id=1, source_target_pairs={{0,8},{2,10},{4,12},{6,14},{8,0},{10,2},{12,4},{14,6},{16,24},{18,... | collective-permute-start | bytes 98312 | tf_op jit(solution)/shard_map/ppermute | solution.py:282
  7.9 1.2 %shard_map.65 = (bf16[1152,256]{1,0:T(8,128)(2,1)S(1)}, bf16[1152,256]{1,0:T(8,128)(2,1)S(1)}) custom-call(bf16[4,64,576]{2,1,0:T(8,128)(2,1)} %copy-done), custom_call_target="tpu_custom_call" | custom-call | flops 1000000 | bytes 1000000 | tf_op jit(solution)/shard_map/pallas_call | solution.py:262
  9.1 0.8 %collective-permute-done.1 = bf16[2,64,128]{2,1,0:T(8,128)(2,1)S(1)} collective-permute-done((bf16[2,64,128]{2,1,0:T(8,128)(2,1)S(1)}, bf16[2,64,128]{2,1,0:T(8,128)(2,1)S(1)}, u32[]{:S(2)}, u32[]{:S(2)}) %collective-permute-start.1) | collective-permute-done | bytes 32800 | tf_op jit(solution)/shard_map/ppermute | solution.py:282
  9.9 1.9 %collective-permute-start.2 = (bf16[4,64,128]{2,1,0:T(8,128)(2,1)S(1)}, bf16[4,64,128]{2,1,0:T(8,128)(2,1)S(1)}, u32[]{:S(2)}, u32[]{:S(2)}) collective-permute-start(bf16[4,64,128]{2,1,0:T(8,128)(2,1)S(1)} %pad_maximum_fusion.1), channel_id=1, source_target_pairs={{0,4},{2,6},{4,0},{6,2},{8,12},{10,14},{12,8},{14,10},{16,20},{18,... | collective-permute-start | bytes 196616 | tf_op jit(solution)/shard_map/ppermute | solution.py:282
  11.9 1.2 %shard_map.66 = (bf16[1152,256]{1,0:T(8,128)(2,1)S(1)}, bf16[1152,256]{1,0:T(8,128)(2,1)S(1)}) custom-call(bf16[4,64,576]{2,1,0:T(8,128)(2,1)} %copy-done), custom_call_target="tpu_custom_call" | custom-call | flops 1000000 | bytes 1000000 | tf_op jit(solution)/shard_map/pallas_call | solution.py:262
  13.1 1.2 %collective-permute-done.2 = bf16[4,64,128]{2,1,0:T(8,128)(2,1)S(1)} collective-permute-done((bf16[4,64,128]{2,1,0:T(8,128)(2,1)S(1)}, bf16[4,64,128]{2,1,0:T(8,128)(2,1)S(1)}, u32[]{:S(2)}, u32[]{:S(2)}) %collective-permute-start.2) | collective-permute-done | bytes 65568 | tf_op jit(solution)/shard_map/ppermute | solution.py:282
  14.3 0.1 collective-permute-start.3
  14.4 1.3 %collective-permute-done.3 = bf16[8,64,128]{2,1,0:T(8,128)(2,1)S(1)} collective-permute-done((bf16[8,64,128]{2,1,0:T(8,128)(2,1)S(1)}, bf16[8,64,128]{2,1,0:T(8,128)(2,1)S(1)}, u32[]{:S(2)}, u32[]{:S(2)}) %collective-permute-start.3) | collective-permute-done | bytes 131104 | tf_op jit(solution)/shard_map/ppermute | solution.py:282
  15.7 11.3 %shard_map.67 = bf16[64,4096]{1,0:T(8,128)(2,1)} custom-call(s32[16]{0:T(128)S(1)} %broadcast_maximum_fusion.slot_ref, bf16[16,64,128]{2,1,0:T(8,128)(2,1)S(1)} %constant_dynamic-update-slice_fusion.emb_ref, bf16[128,128]{1,0:T(8,128)(2,1)S(1)} %get-tuple-element.44.pw_ref, f32[1,128]{1,0:T(1,128)S(1)} %get-tuple-element.45.pb_ref, ...), custom_call_target="tpu_custom_call" | custom-call | flops 8000000000 | bytes 4000000 | tf_op jit(solution)/shard_map/pallas_call | solution.py:216
  (9 shorter events, 0.1 us)
Async XLA Ops:
  0.0 4.0 %copy-start.1 = (s32[16]{0:T(128)S(1)}, s32[16]{0:T(128)}, u32[]{:S(2)}) copy-start(s32[16]{0:T(128)} %param.7) | copy-start | bytes 196
  0.0 6.0 %collective-permute-start = (bf16[1,64,128]{2,1,0:T(8,128)(2,1)}, bf16[1,64,128]{2,1,0:T(8,128)(2,1)S(1)}, u32[]{:S(2)}, u32[]{:S(2)}) collective-permute-start(bf16[1,64,128]{2,1,0:T(8,128)(2,1)} %bitcast.8), channel_id=1, source_target_pairs={{0,16},{2,18},{4,20},{6,22},{8,24},{10,26},{12,28},{14,30},{16,0},... | collective-permute-start | bytes 49160 | tf_op jit(solution)/shard_map/ppermute | solution.py:282
  5.2 0.7 %copy-start = (bf16[4,64,576]{2,1,0:T(8,128)(2,1)}, bf16[4,64,576]{2,1,0:T(8,128)(2,1)S(1)}, u32[]{:S(2)}) copy-start(bf16[4,64,576]{2,1,0:T(8,128)(2,1)S(1)} %get-tuple-element.40.cw_ref) | copy-start | bytes 884740
  6.0 3.9 %collective-permute-start.1 = (bf16[2,64,128]{2,1,0:T(8,128)(2,1)S(1)}, bf16[2,64,128]{2,1,0:T(8,128)(2,1)S(1)}, u32[]{:S(2)}, u32[]{:S(2)}) collective-permute-start(bf16[2,64,128]{2,1,0:T(8,128)(2,1)S(1)} %pad_maximum_fusion.2), channel_id=1, source_target_pairs={{0,8},{2,10},{4,12},{6,14},{8,0},{10,2},{12,4},{14,6},{16,24},{18,... | collective-permute-start | bytes 98312 | tf_op jit(solution)/shard_map/ppermute | solution.py:282
  9.9 4.3 %collective-permute-start.2 = (bf16[4,64,128]{2,1,0:T(8,128)(2,1)S(1)}, bf16[4,64,128]{2,1,0:T(8,128)(2,1)S(1)}, u32[]{:S(2)}, u32[]{:S(2)}) collective-permute-start(bf16[4,64,128]{2,1,0:T(8,128)(2,1)S(1)} %pad_maximum_fusion.1), channel_id=1, source_target_pairs={{0,4},{2,6},{4,0},{6,2},{8,12},{10,14},{12,8},{14,10},{16,20},{18,... | collective-permute-start | bytes 196616 | tf_op jit(solution)/shard_map/ppermute | solution.py:282
  14.3 1.4 %collective-permute-start.3 = (bf16[8,64,128]{2,1,0:T(8,128)(2,1)S(1)}, bf16[8,64,128]{2,1,0:T(8,128)(2,1)S(1)}, u32[]{:S(2)}, u32[]{:S(2)}) collective-permute-start(bf16[8,64,128]{2,1,0:T(8,128)(2,1)S(1)} %pad_maximum_fusion), channel_id=1, source_target_pairs={{0,2},{2,0},{4,6},{6,4},{8,10},{10,8},{12,14},{14,12},{16,18},{18,... | collective-permute-start | bytes 393224 | tf_op jit(solution)/shard_map/ppermute | solution.py:282

commit v4 on v3

v4 whole, which is shorter than its diff:
```python
import functools

import jax
import jax.numpy as jnp
from jax import lax
from jax.experimental import pallas as pl
from jax.experimental.pallas import tpu as pltpu
from jax.sharding import PartitionSpec as P

GROUP = 4
BASE = 8
EDGE = 16


def gelu(x):
    u = x * (0.7978845608028654 + 0.035677408136300125 * (x * x))
    half = 0.5 * x
    return half + half * jnp.tanh(u)


def place(col, halo, dil):
    u = col + halo
    within = u % (2 * dil)
    return (u // (2 * dil)) * dil + within % dil, within // dil


def columns(group, halo, dil):
    first = (group // dil) * 2 * dil + group % dil - halo
    return first, first + dil


def weights_kernel(ch, which, cw_ref, *t_refs):
    zero = jnp.zeros((ch, ch), cw_ref.dtype)
    for l, t_ref in zip(which, t_refs):
        taps = jnp.transpose(cw_ref[l].astype(jnp.float32)).astype(t_ref.dtype)
        for i in range(3):
            for a in range(6):
                row = [
                    taps[(3 * i + a - b) * ch : (3 * i + a - b + 1) * ch] if 0 <= a - b <= 2 else zero
                    for b in (0, 2, 1, 3)
                ]
                t_ref[(6 * i + a) * ch : (6 * i + a + 1) * ch, :] = jnp.concatenate(row, axis=1)


def tile_kernel(dims, slot_ref, emb_ref, pw_ref, pb_ref, cb_ref, *refs):
    layers, tile, ch, npos, noff, order = dims
    t_refs = refs[:layers]
    out_ref, x_ref, g_ref, side_ref, left_ref, corner_ref, bins_ref, made_ref, sems = refs[layers:]
    wide = 2 * ch
    edge = EDGE
    rows = tile + 2 * edge
    halos = [2**layers - 2**l for l in range(layers + 1)]
    top, mid, bot = BASE, BASE + edge, BASE + edge + tile
    side_step, left_step = edge + 1, tile + 1
    me, off = lax.axis_index("pos"), lax.axis_index("off")
    low = lax.broadcasted_iota(jnp.int32, (1, wide), 1) < ch
    diagonal, beside = off == 0, off == 1

    def pick(lo, hi):
        return jnp.where(low, lo, hi)

    def both(value):
        turned = pltpu.roll(value, ch, 1)
        return pick(value, turned), pick(turned, value)

    def block(b):
        slot = slot_ref[lax.rem(b + npos, npos)]
        if not order:
            return slot
        away = jnp.bitwise_xor(slot, me)
        bits = [jnp.bitwise_and(lax.shift_right_logical(away, bit), 1) for bit in order]
        for bit in bits[:-1]:
            bits[-1] = jnp.bitwise_xor(bits[-1], bit)
        return sum(bit << n for n, bit in enumerate(bits))

    pw = pw_ref[...]

    def bins(b):
        first, here, last = (emb_ref[block(b + k)] for k in (-1, 0, 1))
        picked = jnp.concatenate([first[tile - edge :], here, last[:edge]], axis=0)
        made = lax.dot_general(picked, pw, (((1,), (1,)), ((), ())), preferred_element_type=jnp.float32)
        return made.astype(jnp.bfloat16).astype(jnp.float32)

    row_bins = bins(me) + pb_ref[...]
    bins_ref[...] = bins(me + off)
    pairs = (tile + 2 * halos[0]) // 2
    first = edge - halos[0]
    col_bins = pick(
        bins_ref[pl.ds(first, pairs, stride=2), :], bins_ref[pl.ds(first + 1, pairs, stride=2), :]
    )

    keeps = {
        (a, b): (jnp.abs(off + b - a) < noff).astype(jnp.float32) for a in (-1, 0, 1) for b in (-1, 0, 1)
    }

    def band(col):
        return -1 if col < 0 else 1 if col >= tile else 0

    ready = [set() for _ in range(layers)]
    seen = [set() for _ in range(layers)]
    waiting = [[] for _ in range(layers)]

    def activate(l, group, x, start):
        lo, hi = (band(c) for c in columns(group, halos[l], 2**l))
        size = x.shape[0]
        for a, begin, end in ((-1, 0, edge), (0, edge, edge + tile), (1, edge + tile, rows)):
            begin, end = max(begin, start), min(end, start + size)
            if begin < end:
                g = gelu(x[begin - start : end - start])
                if (a, lo, hi) != (0, 0, 0):
                    g = g * pick(keeps[a, lo], keeps[a, hi])
                g_ref[group, BASE + begin : BASE + end, :] = g

    def mirror(l, group):
        halo, dil = halos[l], 2**l
        deep = -(-halo // 8) * 8
        cols = columns(group, halo, dil)
        seen[l].update(cols)
        if any(tile <= c < tile + halo for c in cols):
            for c, value in zip(cols, both(g_ref[group, top:bot, :])):
                if c >= tile:
                    side_ref[pl.ds(c - tile, edge + tile, stride=side_step), :] = value
        if any(0 <= c < tile for c in cols):
            for c, value in zip(cols, both(g_ref[group, top:mid, :])):
                if 0 <= c < tile:
                    left_ref[pl.ds(c, edge, stride=left_step), :] = value
        if any(0 <= c < halo for c in cols):
            for c, value in zip(cols, both(g_ref[group, bot - edge : bot, :])):
                if 0 <= c < halo:
                    corner_ref[pl.ds(c, edge, stride=side_step), :] = value
        waiting[l].append(group)
        for group in list(waiting[l]):
            c1, c2 = columns(group, halo, dil)
            if c1 < tile and not seen[l].issuperset(range(tile, tile + halo)):
                continue
            if c1 < 0 and not seen[l].issuperset(range(tile)):
                continue
            waiting[l].remove(group)
            ready[l].add(group)
            if c1 < tile:
                now = g_ref[group, bot : bot + deep, :]
                at = [(c + edge) * side_step for c in (c1, c2)]
                made = [side_ref[k : k + deep, :] if c < tile else now for c, k in zip((c1, c2), at)]
                new = jnp.where(diagonal, pick(*made), now)
                if c1 < 0:
                    made = [corner_ref[k : k + deep, :] if c < 0 else now for c, k in zip((c1, c2), at)]
                    new = jnp.where(beside, pick(*made), new)
                g_ref[group, bot : bot + deep, :] = new
            if c1 < 0:
                now = g_ref[group, mid:bot, :]
                at = [(c + edge) * left_step for c in (c1, c2)]
                made = [left_ref[k : k + tile, :] if c < 0 else now for c, k in zip((c1, c2), at)]
                g_ref[group, mid:bot, :] = jnp.where(diagonal, pick(*made), now)

    def begin(group):
        x = row_bins + col_bins[group : group + 1]
        x_ref[0, group, :, :] = x
        activate(0, group, x, 0)
        ready[0].add(group)

    stretch = 2**layers
    span = 2 * stretch * ch

    def send(j):
        here = (slice(None), pl.ds(j * span, span))
        return pltpu.make_async_copy(made_ref.at[here], out_ref.at[here], sems.at[j])

    def finish(l, some, acc):
        dil = 2**l
        start = (edge - halos[l + 1]) // 8 * 8
        size = rows - 2 * start
        for n, (j, e) in enumerate(some):
            old = [x_ref[l % 2, (2 * j + s) * dil + e, start : start + size, :] for s in range(3)]
            carried = (pick(pltpu.roll(old[0], ch, 1), old[1]), pick(old[1], pltpu.roll(old[2], ch, 1)))
            new = [
                acc[n * size : (n + 1) * size, s * wide : (s + 1) * wide] + carried[s] + cb_ref[l : l + 1, :]
                for s in range(2)
            ]
            if l + 1 < layers:
                for s, x in enumerate(new):
                    group = j * 2 * dil + e + s * dil
                    x_ref[(l + 1) % 2, group, start : start + size, :] = x
                    activate(l + 1, group, x, start)
                    mirror(l + 1, group)
            elif e % 2 == 0:
                even = new
            else:
                for s in range(2):
                    col = (stretch * 2 * j + e - 1 + s * dil) * ch
                    value = pick(even[s], pltpu.roll(new[s], ch, 1))
                    made_ref[:, col : col + wide] = value.astype(made_ref.dtype)
                    col += stretch * ch
                    value = pick(pltpu.roll(even[s], ch, 1), new[s])
                    made_ref[:, col : col + wide] = value.astype(made_ref.dtype)
                if e == dil - 1:
                    send(j).start()

    unfinished = None
    for l in range(layers):
        dil = 2**l
        start = (edge - halos[l + 1]) // 8 * 8
        size = rows - 2 * start
        count = (tile + 2 * halos[l + 1]) // (4 * dil)
        blocks = [(j, e) for j in reversed(range(count)) for e in range(dil)]
        for at in range(0, len(blocks), GROUP):
            some = blocks[at : at + GROUP]
            need = [(2 * j + s) * dil + e for j, e in some for s in range(3)]
            if l == 0:
                for group in need:
                    if group not in ready[0]:
                        begin(group)
            if not ready[l].issuperset(need):
                finish(*unfinished)
                unfinished = None
            assert ready[l].issuperset(need)

            def taps(j, e):
                return [
                    g_ref[(2 * j + s) * dil + e, BASE + start + i * dil : BASE + start + i * dil + size, :].astype(
                        jnp.bfloat16
                    )
                    for i in (-1, 0, 1)
                    for s in range(3)
                ]

            lhs = jnp.concatenate([jnp.concatenate(taps(j, e), axis=1) for j, e in some], axis=0)
            acc = jnp.dot(lhs, t_refs[l][...], preferred_element_type=jnp.float32)
            if unfinished:
                finish(*unfinished)
            unfinished = (l, some, acc)
    finish(*unfinished)
    for j in range(tile // (2 * stretch)):
        send(j).wait()


def tile_call(npos, noff, order, layers, block_slot, table, proj_weight, proj_bias, conv_bias, banded):
    tile = table.shape[1]
    ch = proj_weight.shape[0] // 2
    vmem = pl.BlockSpec(memory_space=pltpu.VMEM)
    wide = 2 * ch
    groups = tile // 2 + 2**layers - 1
    high = tile + 2 * EDGE
    return pl.pallas_call(
        functools.partial(tile_kernel, (layers, tile, ch, npos, noff, order)),
        out_shape=jax.ShapeDtypeStruct((tile, tile * ch), jnp.bfloat16),
        in_specs=[pl.BlockSpec(memory_space=pltpu.SMEM)]
        + [vmem] * (4 + layers),
        out_specs=pl.BlockSpec(memory_space=pl.ANY),
        scratch_shapes=[
            pltpu.VMEM((2, groups, high, wide), jnp.float32),
            pltpu.VMEM((groups, high + 2 * BASE, wide), jnp.float32),
            pltpu.VMEM(((EDGE + 1) * (EDGE + tile), wide), jnp.float32),
            pltpu.VMEM(((tile + 1) * EDGE, wide), jnp.float32),
            pltpu.VMEM(((EDGE + 1) * EDGE, wide), jnp.float32),
            pltpu.VMEM((high, wide), jnp.float32),
            pltpu.VMEM((tile, tile * ch), jnp.bfloat16),
            pltpu.SemaphoreType.DMA((tile // 2 ** (layers + 1),)),
        ],
        compiler_params=pltpu.CompilerParams(vmem_limit_bytes=48 * 1024 * 1024),
        cost_estimate=pl.CostEstimate(flops=8000000000, bytes_accessed=4000000, transcendentals=2000000),
    )(block_slot, table, proj_weight, proj_bias, conv_bias, *banded)


def parameters_kernel(emb_ref, pw_ref, pb_ref, cb_ref, cw_ref, own_ref, pw2_ref, pb2_ref, cb2_ref, cw2_ref):
    own_ref[0] = emb_ref[...]
    cw2_ref[...] = cw_ref[...]
    for ref, to, axis in ((pw_ref, pw2_ref, 0), (pb_ref, pb2_ref, 1), (cb_ref, cb2_ref, 1)):
        to[...] = jnp.concatenate([ref[...]] * 2, axis=axis)


def parameters_call(bin_embed, proj_weight, proj_bias, conv_bias, weights):
    vmem = pl.BlockSpec(memory_space=pltpu.VMEM)
    ch, emb = proj_weight.shape
    return pl.pallas_call(
        parameters_kernel,
        out_shape=(
            pltpu.VMEM((1,) + bin_embed.shape, bin_embed.dtype),
            pltpu.VMEM((2 * ch, emb), proj_weight.dtype),
            pltpu.VMEM((1, 2 * ch), proj_bias.dtype),
            pltpu.VMEM((conv_bias.shape[0], 2 * ch), conv_bias.dtype),
            pltpu.VMEM(weights.shape, weights.dtype),
        ),
        in_specs=[vmem] * 5,
        out_specs=(vmem,) * 5,
        cost_estimate=pl.CostEstimate(flops=1000000, bytes_accessed=1000000, transcendentals=0),
    )(bin_embed, proj_weight, proj_bias, conv_bias, weights)


def band_call(weights, which):
    layers, ch, taps = weights.shape
    vmem = pl.BlockSpec(memory_space=pltpu.VMEM)
    return pl.pallas_call(
        functools.partial(weights_kernel, ch, which),
        out_shape=(pltpu.VMEM((2 * taps, 4 * ch), weights.dtype),) * len(which),
        in_specs=[vmem],
        out_specs=(vmem,) * len(which),
        cost_estimate=pl.CostEstimate(flops=1000000, bytes_accessed=1000000, transcendentals=0),
    )(weights)


def on_device(bin_embed, block_slot, proj_weight, proj_bias, conv_weight, conv_bias):
    npos, noff = lax.axis_size("pos"), lax.axis_size("off")
    tile, emb = bin_embed.shape
    layers, taps, ch = conv_weight.shape
    order = tuple(reversed(range(npos.bit_length() - 1))) if npos & (npos - 1) == 0 else ()
    turned = jnp.swapaxes(conv_weight, 1, 2)
    zero = lax.optimization_barrier(jnp.zeros((1,), block_slot.dtype))
    table = bin_embed[None]
    banded, todo = [], tuple(range(layers))
    for stage, bit in enumerate(order):
        there = lax.ppermute(table, "pos", [(i, i ^ (1 << bit | 1)) for i in range(npos)])
        if stage == 0:
            table, *small, turned = parameters_call(bin_embed, proj_weight.T, proj_bias[None], conv_bias, turned)
            slots = jnp.maximum(block_slot, zero)
            there, table, small, slots, turned = lax.optimization_barrier((there, table, small, slots, turned))
        elif todo:
            made = band_call(turned, todo[:2])
            there, made, turned = lax.optimization_barrier((there, made, turned))
            banded, todo = banded + list(made), todo[2:]
        table = jnp.concatenate([table, there], axis=0)
    if not order:
        _, *small, turned = parameters_call(bin_embed, proj_weight.T, proj_bias[None], conv_bias, turned)
        table, slots = lax.all_gather(bin_embed, "pos"), block_slot
    if todo:
        banded += band_call(turned, todo)
    out = tile_call(npos, noff, order, layers, slots, table, *small, banded)
    return out.reshape(1, 1, tile, tile * ch)


def solution(mesh):
    placed = (P("pos", None), P(), P(), P(), P(), P())
    return jax.shard_map(
        on_device,
        mesh=mesh,
        in_specs=placed,
        out_specs=P("pos", "off", None, None),
        check_vma=False,
    )
```

time: 27.2 us -> 22.1 us (0.81)
  Pallas kernels: 14.9 us -> 11.2 us
  waiting for transfers between devices: 3.31 us -> 2.13 us
    pallas_call x1, Pallas kernels: 11.3 us -> 7.61 us  [tile_call(): pl.pallas_call(functools.partial(tile_kernel, (layers, tile, ch, npos, no...]
    ppermute x4, waiting for transfers between devices: 3.31 us -> 2.13 us  [on_device(): lax.ppermute(table, 'pos', [(i, i ^ (1 << bit | 1)) for i in range(npos)])]
  transfers between devices with their start and end apart: 4 -> 4, of which waited for: 4 -> 3; matrix products, arithmetic and copies ran while one was open for 0% -> 0% of each run, Pallas kernels for 13% -> 16%
where the time goes in v4:
time: 22.1 us; the launch traced here: 21.9 us
  Pallas kernels  11.2 us (51%)
  starting transfers between devices  7.74 us (35%)
  waiting for transfers between devices  2.13 us (10%)
  local copies, waits for them, and re-layouts  0.78 us (4%)
    ppermute x4, starting transfers between devices, on_device(): lax.ppermute(table, 'pos', [(i, i ^ (1 << bit | 1)) for i in range(npos)])  7.74 us
    pallas_call x1, Pallas kernels, tile_call(): pl.pallas_call(functools.partial(tile_kernel, (layers, tile, ch, npos, no...  7.61 us
    pallas_call x2, Pallas kernels, band_call(): pl.pallas_call(functools.partial(weights_kernel, ch, which), out_shape=(p...  2.45 us
    ppermute x4, waiting for transfers between devices, on_device(): lax.ppermute(table, 'pos', [(i, i ^ (1 << bit | 1)) for i in range(npos)])  2.13 us
    pallas_call x1, Pallas kernels, parameters_call(): pl.pallas_call(parameters_kernel, out_shape=(pltpu.VMEM((1,) + bin_embed....  1.14 us
    unnamed x8, local copies, waits for them, and re-layouts  0.76 us
  transfers between devices with their start and end apart: 4, of which 3 were waited for; matrix products, arithmetic and copies ran while one was open for 0% of the time, Pallas kernels for 16%

profile of v4, /device:TPU:0, one launch (start us, length us, event | category | flops | bytes accessed | tf_op | source)
XLA Modules:
  0.0 21.9 jit_solution(1768243159177061190)
XLA Ops:
  0.0 0.0 copy-start.1
  0.0 3.5 %collective-permute-start = (bf16[1,64,128]{2,1,0:T(8,128)(2,1)}, bf16[1,64,128]{2,1,0:T(8,128)(2,1)S(1)}, u32[]{:S(2)}, u32[]{:S(2)}) collective-permute-start(bf16[1,64,128]{2,1,0:T(8,128)(2,1)} %bitcast.8), channel_id=1, source_target_pairs={{0,18},{2,16},{4,22},{6,20},{8,26},{10,24},{12,30},{14,28},{16,2},... | collective-permute-start | bytes 49160 | tf_op jit(solution)/shard_map/ppermute | solution.py:311
  3.5 0.0 copy-done.1
  3.5 1.1 %shard_map.64 = (bf16[1,64,128]{2,1,0:T(8,128)(2,1)S(1)}, bf16[128,128]{1,0:T(8,128)(2,1)S(1)}, f32[1,128]{1,0:T(1,128)S(1)}, f32[4,128]{1,0:T(4,128)S(1)}, bf16[4,64,576]{2,1,0:T(8,128)(2,1)S(1)}) custom-call(bf16[64,128]{1,0:T(8,128)(2,1)} %emb_ref.1, bf16[64,128]{1,0:T(8,128)(2,1)} %bitcast.7, f32[1,64]{1,0:T(1,128)} %bitcast.9, f32[4,64]{1,0:T(4,128)} %cb_ref.1, ...), custom_call_target="tpu_custom_call" | custom-call | flops 1000000 | bytes 1000000 | tf_op jit(solution)/shard_map/pallas_call | solution.py:274
  4.6 0.0 copy-start
  4.6 0.7 %copy-done = bf16[4,64,576]{2,1,0:T(8,128)(2,1)} copy-done((bf16[4,64,576]{2,1,0:T(8,128)(2,1)}, bf16[4,64,576]{2,1,0:T(8,128)(2,1)S(1)}, u32[]{:S(2)}) %copy-start) | copy-done | bytes 294936
  5.3 0.0 collective-permute-done
  5.4 1.9 %collective-permute-start.1 = (bf16[2,64,128]{2,1,0:T(8,128)(2,1)S(1)}, bf16[2,64,128]{2,1,0:T(8,128)(2,1)S(1)}, u32[]{:S(2)}, u32[]{:S(2)}) collective-permute-start(bf16[2,64,128]{2,1,0:T(8,128)(2,1)S(1)} %pad_maximum_fusion.2), channel_id=1, source_target_pairs={{0,10},{2,8},{4,14},{6,12},{8,2},{10,0},{12,6},{14,4},{16,26},{18,... | collective-permute-start | bytes 98312 | tf_op jit(solution)/shard_map/ppermute | solution.py:311
  7.3 1.2 %shard_map.65 = (bf16[1152,256]{1,0:T(8,128)(2,1)S(1)}, bf16[1152,256]{1,0:T(8,128)(2,1)S(1)}) custom-call(bf16[4,64,576]{2,1,0:T(8,128)(2,1)} %copy-done), custom_call_target="tpu_custom_call" | custom-call | flops 1000000 | bytes 1000000 | tf_op jit(solution)/shard_map/pallas_call | solution.py:292
  8.5 0.4 %collective-permute-done.1 = bf16[2,64,128]{2,1,0:T(8,128)(2,1)S(1)} collective-permute-done((bf16[2,64,128]{2,1,0:T(8,128)(2,1)S(1)}, bf16[2,64,128]{2,1,0:T(8,128)(2,1)S(1)}, u32[]{:S(2)}, u32[]{:S(2)}) %collective-permute-start.1) | collective-permute-done | bytes 32800 | tf_op jit(solution)/shard_map/ppermute | solution.py:311
  8.9 1.7 %collective-permute-start.2 = (bf16[4,64,128]{2,1,0:T(8,128)(2,1)S(1)}, bf16[4,64,128]{2,1,0:T(8,128)(2,1)S(1)}, u32[]{:S(2)}, u32[]{:S(2)}) collective-permute-start(bf16[4,64,128]{2,1,0:T(8,128)(2,1)S(1)} %pad_maximum_fusion.1), channel_id=1, source_target_pairs={{0,6},{2,4},{4,2},{6,0},{8,14},{10,12},{12,10},{14,8},{16,22},{18,... | collective-permute-start | bytes 196616 | tf_op jit(solution)/shard_map/ppermute | solution.py:311
  10.6 1.2 %shard_map.66 = (bf16[1152,256]{1,0:T(8,128)(2,1)S(1)}, bf16[1152,256]{1,0:T(8,128)(2,1)S(1)}) custom-call(bf16[4,64,576]{2,1,0:T(8,128)(2,1)} %copy-done), custom_call_target="tpu_custom_call" | custom-call | flops 1000000 | bytes 1000000 | tf_op jit(solution)/shard_map/pallas_call | solution.py:292
  11.9 0.8 %collective-permute-done.2 = bf16[4,64,128]{2,1,0:T(8,128)(2,1)S(1)} collective-permute-done((bf16[4,64,128]{2,1,0:T(8,128)(2,1)S(1)}, bf16[4,64,128]{2,1,0:T(8,128)(2,1)S(1)}, u32[]{:S(2)}, u32[]{:S(2)}) %collective-permute-start.2) | collective-permute-done | bytes 65568 | tf_op jit(solution)/shard_map/ppermute | solution.py:311
  12.7 0.6 %collective-permute-start.3 = (bf16[8,64,128]{2,1,0:T(8,128)(2,1)S(1)}, bf16[8,64,128]{2,1,0:T(8,128)(2,1)S(1)}, u32[]{:S(2)}, u32[]{:S(2)}) collective-permute-start(bf16[8,64,128]{2,1,0:T(8,128)(2,1)S(1)} %pad_maximum_fusion), channel_id=1, source_target_pairs={{0,2},{2,0},{4,6},{6,4},{8,10},{10,8},{12,14},{14,12},{16,18},{18,... | collective-permute-start | bytes 393224 | tf_op jit(solution)/shard_map/ppermute | solution.py:311
  13.3 1.0 %collective-permute-done.3 = bf16[8,64,128]{2,1,0:T(8,128)(2,1)S(1)} collective-permute-done((bf16[8,64,128]{2,1,0:T(8,128)(2,1)S(1)}, bf16[8,64,128]{2,1,0:T(8,128)(2,1)S(1)}, u32[]{:S(2)}, u32[]{:S(2)}) %collective-permute-start.3) | collective-permute-done | bytes 131104 | tf_op jit(solution)/shard_map/ppermute | solution.py:311
  14.3 7.6 %shard_map.67 = bf16[64,4096]{1,0:T(8,128)(2,1)} custom-call(s32[16]{0:T(128)S(1)} %broadcast_maximum_fusion.slot_ref, bf16[16,64,128]{2,1,0:T(8,128)(2,1)S(1)} %constant_dynamic-update-slice_fusion.emb_ref, bf16[128,128]{1,0:T(8,128)(2,1)S(1)} %get-tuple-element.44.pw_ref, f32[1,128]{1,0:T(1,128)S(1)} %get-tuple-element.45.pb_ref, ...), custom_call_target="tpu_custom_call" | custom-call | flops 8000000000 | bytes 4000000 | tf_op jit(solution)/shard_map/pallas_call | solution.py:243
  (9 shorter events, 0.1 us)
Async XLA Ops:
  0.0 3.5 %copy-start.1 = (s32[16]{0:T(128)S(1)}, s32[16]{0:T(128)}, u32[]{:S(2)}) copy-start(s32[16]{0:T(128)} %param.7) | copy-start | bytes 196
  0.0 5.3 %collective-permute-start = (bf16[1,64,128]{2,1,0:T(8,128)(2,1)}, bf16[1,64,128]{2,1,0:T(8,128)(2,1)S(1)}, u32[]{:S(2)}, u32[]{:S(2)}) collective-permute-start(bf16[1,64,128]{2,1,0:T(8,128)(2,1)} %bitcast.8), channel_id=1, source_target_pairs={{0,18},{2,16},{4,22},{6,20},{8,26},{10,24},{12,30},{14,28},{16,2},... | collective-permute-start | bytes 49160 | tf_op jit(solution)/shard_map/ppermute | solution.py:311
  4.6 0.7 %copy-start = (bf16[4,64,576]{2,1,0:T(8,128)(2,1)}, bf16[4,64,576]{2,1,0:T(8,128)(2,1)S(1)}, u32[]{:S(2)}) copy-start(bf16[4,64,576]{2,1,0:T(8,128)(2,1)S(1)} %get-tuple-element.40.cw_ref) | copy-start | bytes 884740
  5.4 3.5 %collective-permute-start.1 = (bf16[2,64,128]{2,1,0:T(8,128)(2,1)S(1)}, bf16[2,64,128]{2,1,0:T(8,128)(2,1)S(1)}, u32[]{:S(2)}, u32[]{:S(2)}) collective-permute-start(bf16[2,64,128]{2,1,0:T(8,128)(2,1)S(1)} %pad_maximum_fusion.2), channel_id=1, source_target_pairs={{0,10},{2,8},{4,14},{6,12},{8,2},{10,0},{12,6},{14,4},{16,26},{18,... | collective-permute-start | bytes 98312 | tf_op jit(solution)/shard_map/ppermute | solution.py:311
  8.9 3.8 %collective-permute-start.2 = (bf16[4,64,128]{2,1,0:T(8,128)(2,1)S(1)}, bf16[4,64,128]{2,1,0:T(8,128)(2,1)S(1)}, u32[]{:S(2)}, u32[]{:S(2)}) collective-permute-start(bf16[4,64,128]{2,1,0:T(8,128)(2,1)S(1)} %pad_maximum_fusion.1), channel_id=1, source_target_pairs={{0,6},{2,4},{4,2},{6,0},{8,14},{10,12},{12,10},{14,8},{16,22},{18,... | collective-permute-start | bytes 196616 | tf_op jit(solution)/shard_map/ppermute | solution.py:311
  12.7 1.6 %collective-permute-start.3 = (bf16[8,64,128]{2,1,0:T(8,128)(2,1)S(1)}, bf16[8,64,128]{2,1,0:T(8,128)(2,1)S(1)}, u32[]{:S(2)}, u32[]{:S(2)}) collective-permute-start(bf16[8,64,128]{2,1,0:T(8,128)(2,1)S(1)} %pad_maximum_fusion), channel_id=1, source_target_pairs={{0,2},{2,0},{4,6},{6,4},{8,10},{10,8},{12,14},{14,12},{16,18},{18,... | collective-permute-start | bytes 393224 | tf_op jit(solution)/shard_map/ppermute | solution.py:311

commit v5 on v4

--- a/solution.py
+++ b/solution.py
@@ -106,7 +106,7 @@
         for a, begin, end in ((-1, 0, edge), (0, edge, edge + tile), (1, edge + tile, rows)):
             begin, end = max(begin, start), min(end, start + size)
             if begin < end:
-                g = gelu(x[begin - start : end - start])
+                g = gelu(x[begin - start : end - start].astype(jnp.bfloat16)).astype(jnp.float32)
                 if (a, lo, hi) != (0, 0, 0):
                     g = g * pick(keeps[a, lo], keeps[a, hi])
                 g_ref[group, BASE + begin : BASE + end, :] = g
@@ -261,33 +261,39 @@
     )(block_slot, table, proj_weight, proj_bias, conv_bias, *banded)
 
 
-def parameters_kernel(emb_ref, pw_ref, pb_ref, cb_ref, cw_ref, own_ref, pw2_ref, pb2_ref, cb2_ref, cw2_ref):
+def parameters_kernel(
+    slot_ref, emb_ref, pw_ref, pb_ref, cb_ref, cw_ref, slot2_ref, own_ref, pw2_ref, pb2_ref, cb2_ref, cw2_ref
+):
+    for b in range(slot_ref.shape[0]):
+        slot2_ref[b] = slot_ref[b]
     own_ref[0] = emb_ref[...]
     cw2_ref[...] = cw_ref[...]
     for ref, to, axis in ((pw_ref, pw2_ref, 0), (pb_ref, pb2_ref, 1), (cb_ref, cb2_ref, 1)):
         to[...] = jnp.concatenate([ref[...]] * 2, axis=axis)
 
 
-def parameters_call(bin_embed, proj_weight, proj_bias, conv_bias, weights):
-    vmem = pl.BlockSpec(memory_space=pltpu.VMEM)
+def parameters_call(block_slot, bin_embed, proj_weight, proj_bias, conv_bias, weights):
+    vmem, smem = pl.BlockSpec(memory_space=pltpu.VMEM), pl.BlockSpec(memory_space=pltpu.SMEM)
     ch, emb = proj_weight.shape
     return pl.pallas_call(
         parameters_kernel,
         out_shape=(
+            pltpu.SMEM(block_slot.shape, block_slot.dtype),
             pltpu.VMEM((1,) + bin_embed.shape, bin_embed.dtype),
             pltpu.VMEM((2 * ch, emb), proj_weight.dtype),
             pltpu.VMEM((1, 2 * ch), proj_bias.dtype),
             pltpu.VMEM((conv_bias.shape[0], 2 * ch), conv_bias.dtype),
             pltpu.VMEM(weights.shape, weights.dtype),
         ),
-        in_specs=[vmem] * 5,
-        out_specs=(vmem,) * 5,
+        in_specs=[smem] + [vmem] * 5,
+        out_specs=(smem,) + (vmem,) * 5,
         cost_estimate=pl.CostEstimate(flops=1000000, bytes_accessed=1000000, transcendentals=0),
-    )(bin_embed, proj_weight, proj_bias, conv_bias, weights)
+    )(block_slot, bin_embed, proj_weight, proj_bias, conv_bias, weights)
 
 
 def band_call(weights, which):
     layers, ch, taps = weights.shape
+    weights = pltpu.with_memory_space_constraint(weights, pltpu.VMEM)
     vmem = pl.BlockSpec(memory_space=pltpu.VMEM)
     return pl.pallas_call(
         functools.partial(weights_kernel, ch, which),
@@ -304,14 +310,13 @@
     layers, taps, ch = conv_weight.shape
     order = tuple(reversed(range(npos.bit_length() - 1))) if npos & (npos - 1) == 0 else ()
     turned = jnp.swapaxes(conv_weight, 1, 2)
-    zero = lax.optimization_barrier(jnp.zeros((1,), block_slot.dtype))
     table = bin_embed[None]
     banded, todo = [], tuple(range(layers))
+    small = (block_slot, bin_embed, proj_weight.T, proj_bias[None], conv_bias, turned)
     for stage, bit in enumerate(order):
         there = lax.ppermute(table, "pos", [(i, i ^ (1 << bit | 1)) for i in range(npos)])
         if stage == 0:
-            table, *small, turned = parameters_call(bin_embed, proj_weight.T, proj_bias[None], conv_bias, turned)
-            slots = jnp.maximum(block_slot, zero)
+            slots, table, *small, turned = parameters_call(*small)
             there, table, small, slots, turned = lax.optimization_barrier((there, table, small, slots, turned))
         elif todo:
             made = band_call(turned, todo[:2])
@@ -319,8 +324,8 @@
             banded, todo = banded + list(made), todo[2:]
         table = jnp.concatenate([table, there], axis=0)
     if not order:
-        _, *small, turned = parameters_call(bin_embed, proj_weight.T, proj_bias[None], conv_bias, turned)
-        table, slots = lax.all_gather(bin_embed, "pos"), block_slot
+        slots, _, *small, turned = parameters_call(*small)
+        table = lax.all_gather(bin_embed, "pos")
     if todo:
         banded += band_call(turned, todo)
     out = tile_call(npos, noff, order, layers, slots, table, *small, banded)

time: 22.1 us -> 20.8 us (0.941)
  Pallas kernels: 11.2 us -> 8.21 us
  waiting for transfers between devices: 2.13 us -> 4.81 us
  local copies, waits for them, and re-layouts: 0.78 us -> 0.05 us
    ppermute x4, waiting for transfers between devices: 2.13 us -> 4.81 us  [on_device(): lax.ppermute(table, 'pos', [(i, i ^ (1 << bit | 1)) for i in range(npos)])]
    pallas_call x2, Pallas kernels: 2.45 us -> 0.5 us  [band_call(): pl.pallas_call(functools.partial(weights_kernel, ch, which), out_shape=(p...]
    pallas_call x1, Pallas kernels: 7.61 us -> 6.59 us  [tile_call(): pl.pallas_call(functools.partial(tile_kernel, (layers, tile, ch, npos, no...]
    unnamed x8 -> x4, local copies, waits for them, and re-layouts: 0.76 us -> 0.03 us
    ppermute x4, starting transfers between devices: 7.74 us -> 7.52 us  [on_device(): lax.ppermute(table, 'pos', [(i, i ^ (1 << bit | 1)) for i in range(npos)])]
  transfers between devices with their start and end apart: 4 -> 4, of which waited for: 3 -> 4; matrix products, arithmetic and copies ran while one was open for 0% -> 0% of each run, Pallas kernels for 16% -> 8%
where the time goes in v5:
time: 20.8 us; the launch traced here: 20.6 us
  Pallas kernels  8.21 us (39%)
  starting transfers between devices  7.52 us (36%)
  waiting for transfers between devices  4.81 us (23%)
    ppermute x4, starting transfers between devices, on_device(): lax.ppermute(table, 'pos', [(i, i ^ (1 << bit | 1)) for i in range(npos)])  7.52 us
    pallas_call x1, Pallas kernels, tile_call(): pl.pallas_call(functools.partial(tile_kernel, (layers, tile, ch, npos, no...  6.59 us
    ppermute x4, waiting for transfers between devices, on_device(): lax.ppermute(table, 'pos', [(i, i ^ (1 << bit | 1)) for i in range(npos)])  4.81 us
    pallas_call x1, Pallas kernels, parameters_call(): pl.pallas_call(parameters_kernel, out_shape=(pltpu.SMEM(block_slot.shape,...  1.12 us
    pallas_call x2, Pallas kernels, band_call(): pl.pallas_call(functools.partial(weights_kernel, ch, which), out_shape=(p...  0.5 us
  transfers between devices with their start and end apart: 4, of which 4 were waited for; matrix products, arithmetic and copies ran while one was open for 0% of the time, Pallas kernels for 8%

profile of v5, /device:TPU:0, one launch (start us, length us, event | category | flops | bytes accessed | tf_op | source)
XLA Modules:
  0.0 20.6 jit_solution(6158540567596525463)
XLA Ops:
  0.0 3.5 %collective-permute-start = (bf16[1,64,128]{2,1,0:T(8,128)(2,1)}, bf16[1,64,128]{2,1,0:T(8,128)(2,1)S(1)}, u32[]{:S(2)}, u32[]{:S(2)}) collective-permute-start(bf16[1,64,128]{2,1,0:T(8,128)(2,1)} %bitcast.7), channel_id=1, source_target_pairs={{0,18},{2,16},{4,22},{6,20},{8,26},{10,24},{12,30},{14,28},{16,2},... | collective-permute-start | bytes 49160 | tf_op jit(solution)/shard_map/ppermute | solution.py:317
  3.5 1.1 %shard_map.64 = (s32[16]{0:T(128)S(4)}, bf16[1,64,128]{2,1,0:T(8,128)(2,1)S(1)}, bf16[128,128]{1,0:T(8,128)(2,1)S(1)}, f32[1,128]{1,0:T(1,128)S(1)}, f32[4,128]{...) custom-call(s32[16]{0:T(128)} %slot_ref.1, bf16[64,128]{1,0:T(8,128)(2,1)} %emb_ref.1, bf16[64,128]{1,0:T(8,128)(2,1)} %bitcast.6, ...), custom_call_target="tpu_custom_call" | custom-call | flops 1000000 | bytes 1000000 | tf_op jit(solution)/shard_map/pallas_call | solution.py:278
  4.6 0.5 %collective-permute-done = bf16[1,64,128]{2,1,0:T(8,128)(2,1)S(1)} collective-permute-done((bf16[1,64,128]{2,1,0:T(8,128)(2,1)}, bf16[1,64,128]{2,1,0:T(8,128)(2,1)S(1)}, u32[]{:S(2)}, u32[]{:S(2)}) %collective-permute-start) | collective-permute-done | bytes 16416 | tf_op jit(solution)/shard_map/ppermute | solution.py:317
  5.1 1.9 %collective-permute-start.1 = (bf16[2,64,128]{2,1,0:T(8,128)(2,1)S(1)}, bf16[2,64,128]{2,1,0:T(8,128)(2,1)S(1)}, u32[]{:S(2)}, u32[]{:S(2)}) collective-permute-start(bf16[2,64,128]{2,1,0:T(8,128)(2,1)S(1)} %pad_maximum_fusion.2), channel_id=1, source_target_pairs={{0,10},{2,8},{4,14},{6,12},{8,2},{10,0},{12,6},{14,4},{16,26},{18,... | collective-permute-start | bytes 98312 | tf_op jit(solution)/shard_map/ppermute | solution.py:317
  7.0 0.3 %shard_map.65 = (bf16[1152,256]{1,0:T(8,128)(2,1)S(1)}, bf16[1152,256]{1,0:T(8,128)(2,1)S(1)}) custom-call(bf16[4,64,576]{2,1,0:T(8,128)(2,1)S(1)} %get-tuple-element.42.cw_ref), custom_call_target="tpu_custom_call" | custom-call | flops 1000000 | bytes 1000000 | tf_op jit(solution)/shard_map/pallas_call | solution.py:298
  7.3 1.3 %collective-permute-done.1 = bf16[2,64,128]{2,1,0:T(8,128)(2,1)S(1)} collective-permute-done((bf16[2,64,128]{2,1,0:T(8,128)(2,1)S(1)}, bf16[2,64,128]{2,1,0:T(8,128)(2,1)S(1)}, u32[]{:S(2)}, u32[]{:S(2)}) %collective-permute-start.1) | collective-permute-done | bytes 32800 | tf_op jit(solution)/shard_map/ppermute | solution.py:317
  8.6 1.8 %collective-permute-start.2 = (bf16[4,64,128]{2,1,0:T(8,128)(2,1)S(1)}, bf16[4,64,128]{2,1,0:T(8,128)(2,1)S(1)}, u32[]{:S(2)}, u32[]{:S(2)}) collective-permute-start(bf16[4,64,128]{2,1,0:T(8,128)(2,1)S(1)} %pad_maximum_fusion.1), channel_id=1, source_target_pairs={{0,6},{2,4},{4,2},{6,0},{8,14},{10,12},{12,10},{14,8},{16,22},{18,... | collective-permute-start | bytes 196616 | tf_op jit(solution)/shard_map/ppermute | solution.py:317
  10.4 0.3 %shard_map.66 = (bf16[1152,256]{1,0:T(8,128)(2,1)S(1)}, bf16[1152,256]{1,0:T(8,128)(2,1)S(1)}) custom-call(bf16[4,64,576]{2,1,0:T(8,128)(2,1)S(1)} %get-tuple-element.42.cw_ref), custom_call_target="tpu_custom_call" | custom-call | flops 1000000 | bytes 1000000 | tf_op jit(solution)/shard_map/pallas_call | solution.py:298
  10.7 1.9 %collective-permute-done.2 = bf16[4,64,128]{2,1,0:T(8,128)(2,1)S(1)} collective-permute-done((bf16[4,64,128]{2,1,0:T(8,128)(2,1)S(1)}, bf16[4,64,128]{2,1,0:T(8,128)(2,1)S(1)}, u32[]{:S(2)}, u32[]{:S(2)}) %collective-permute-start.2) | collective-permute-done | bytes 65568 | tf_op jit(solution)/shard_map/ppermute | solution.py:317
  12.6 0.4 %collective-permute-start.3 = (bf16[8,64,128]{2,1,0:T(8,128)(2,1)S(1)}, bf16[8,64,128]{2,1,0:T(8,128)(2,1)S(1)}, u32[]{:S(2)}, u32[]{:S(2)}) collective-permute-start(bf16[8,64,128]{2,1,0:T(8,128)(2,1)S(1)} %pad_maximum_fusion), channel_id=1, source_target_pairs={{0,2},{2,0},{4,6},{6,4},{8,10},{10,8},{12,14},{14,12},{16,18},{18,... | collective-permute-start | bytes 393224 | tf_op jit(solution)/shard_map/ppermute | solution.py:317
  13.0 1.0 %collective-permute-done.3 = bf16[8,64,128]{2,1,0:T(8,128)(2,1)S(1)} collective-permute-done((bf16[8,64,128]{2,1,0:T(8,128)(2,1)S(1)}, bf16[8,64,128]{2,1,0:T(8,128)(2,1)S(1)}, u32[]{:S(2)}, u32[]{:S(2)}) %collective-permute-start.3) | collective-permute-done | bytes 131104 | tf_op jit(solution)/shard_map/ppermute | solution.py:317
  14.1 6.6 %shard_map.67 = bf16[64,4096]{1,0:T(8,128)(2,1)} custom-call(s32[16]{0:T(128)S(4)} %get-tuple-element.35.slot_ref, bf16[16,64,128]{2,1,0:T(8,128)(2,1)S(1)} %constant_dynamic-update-slice_fusion.emb_ref, bf16[128,128]{1,0:T(8,128)(2,1)S(1)} %get-tuple-element.46.pw_ref, f32[1,128]{1,0:T(1,128)S(1)} %get-tuple-element.47.pb_ref, ...), custom_call_target="tpu_custom_call" | custom-call | flops 8000000000 | bytes 4000000 | tf_op jit(solution)/shard_map/pallas_call | solution.py:243
  (8 shorter events, 0.1 us)
Async XLA Ops:
  0.0 5.1 %collective-permute-start = (bf16[1,64,128]{2,1,0:T(8,128)(2,1)}, bf16[1,64,128]{2,1,0:T(8,128)(2,1)S(1)}, u32[]{:S(2)}, u32[]{:S(2)}) collective-permute-start(bf16[1,64,128]{2,1,0:T(8,128)(2,1)} %bitcast.7), channel_id=1, source_target_pairs={{0,18},{2,16},{4,22},{6,20},{8,26},{10,24},{12,30},{14,28},{16,2},... | collective-permute-start | bytes 49160 | tf_op jit(solution)/shard_map/ppermute | solution.py:317
  5.1 3.5 %collective-permute-start.1 = (bf16[2,64,128]{2,1,0:T(8,128)(2,1)S(1)}, bf16[2,64,128]{2,1,0:T(8,128)(2,1)S(1)}, u32[]{:S(2)}, u32[]{:S(2)}) collective-permute-start(bf16[2,64,128]{2,1,0:T(8,128)(2,1)S(1)} %pad_maximum_fusion.2), channel_id=1, source_target_pairs={{0,10},{2,8},{4,14},{6,12},{8,2},{10,0},{12,6},{14,4},{16,26},{18,... | collective-permute-start | bytes 98312 | tf_op jit(solution)/shard_map/ppermute | solution.py:317
  8.6 4.0 %collective-permute-start.2 = (bf16[4,64,128]{2,1,0:T(8,128)(2,1)S(1)}, bf16[4,64,128]{2,1,0:T(8,128)(2,1)S(1)}, u32[]{:S(2)}, u32[]{:S(2)}) collective-permute-start(bf16[4,64,128]{2,1,0:T(8,128)(2,1)S(1)} %pad_maximum_fusion.1), channel_id=1, source_target_pairs={{0,6},{2,4},{4,2},{6,0},{8,14},{10,12},{12,10},{14,8},{16,22},{18,... | collective-permute-start | bytes 196616 | tf_op jit(solution)/shard_map/ppermute | solution.py:317
  12.6 1.4 %collective-permute-start.3 = (bf16[8,64,128]{2,1,0:T(8,128)(2,1)S(1)}, bf16[8,64,128]{2,1,0:T(8,128)(2,1)S(1)}, u32[]{:S(2)}, u32[]{:S(2)}) collective-permute-start(bf16[8,64,128]{2,1,0:T(8,128)(2,1)S(1)} %pad_maximum_fusion), channel_id=1, source_target_pairs={{0,2},{2,0},{4,6},{6,4},{8,10},{10,8},{12,14},{14,12},{16,18},{18,... | collective-permute-start | bytes 393224 | tf_op jit(solution)/shard_map/ppermute | solution.py:317

commit v6 on v5

--- a/solution.py
+++ b/solution.py
@@ -42,7 +42,7 @@
                 t_ref[(6 * i + a) * ch : (6 * i + a + 1) * ch, :] = jnp.concatenate(row, axis=1)
 
 
-def tile_kernel(dims, slot_ref, emb_ref, pw_ref, pb_ref, cb_ref, *refs):
+def tile_kernel(dims, slot_ref, bin_ref, pb_ref, cb_ref, *refs):
     layers, tile, ch, npos, noff, order = dims
     t_refs = refs[:layers]
     out_ref, x_ref, g_ref, side_ref, left_ref, corner_ref, bins_ref, made_ref, sems = refs[layers:]
@@ -73,13 +73,9 @@
             bits[-1] = jnp.bitwise_xor(bits[-1], bit)
         return sum(bit << n for n, bit in enumerate(bits))
 
-    pw = pw_ref[...]
-
     def bins(b):
-        first, here, last = (emb_ref[block(b + k)] for k in (-1, 0, 1))
-        picked = jnp.concatenate([first[tile - edge :], here, last[:edge]], axis=0)
-        made = lax.dot_general(picked, pw, (((1,), (1,)), ((), ())), preferred_element_type=jnp.float32)
-        return made.astype(jnp.bfloat16).astype(jnp.float32)
+        first, here, last = (both(bin_ref[block(b + k)].astype(jnp.float32)) for k in (-1, 0, 1))
+        return jnp.concatenate([first[1][tile // 2 - edge :], here[0], here[1], last[0][:edge]], axis=0)
 
     row_bins = bins(me) + pb_ref[...]
     bins_ref[...] = bins(me + off)
@@ -233,9 +229,9 @@
         send(j).wait()
 
 
-def tile_call(npos, noff, order, layers, block_slot, table, proj_weight, proj_bias, conv_bias, banded):
-    tile = table.shape[1]
-    ch = proj_weight.shape[0] // 2
+def tile_call(npos, noff, order, layers, block_slot, table, proj_bias, conv_bias, banded):
+    tile = 2 * table.shape[1]
+    ch = proj_bias.shape[1] // 2
     vmem = pl.BlockSpec(memory_space=pltpu.VMEM)
     wide = 2 * ch
     groups = tile // 2 + 2**layers - 1
@@ -244,7 +240,7 @@
         functools.partial(tile_kernel, (layers, tile, ch, npos, noff, order)),
         out_shape=jax.ShapeDtypeStruct((tile, tile * ch), jnp.bfloat16),
         in_specs=[pl.BlockSpec(memory_space=pltpu.SMEM)]
-        + [vmem] * (4 + layers),
+        + [vmem] * (3 + layers),
         out_specs=pl.BlockSpec(memory_space=pl.ANY),
         scratch_shapes=[
             pltpu.VMEM((2, groups, high, wide), jnp.float32),
@@ -258,7 +254,13 @@
         ],
         compiler_params=pltpu.CompilerParams(vmem_limit_bytes=48 * 1024 * 1024),
         cost_estimate=pl.CostEstimate(flops=8000000000, bytes_accessed=4000000, transcendentals=2000000),
-    )(block_slot, table, proj_weight, proj_bias, conv_bias, *banded)
+    )(block_slot, table, proj_bias, conv_bias, *banded)
+
+
+def project(emb, weight):
+    made = lax.dot_general(emb, weight, (((1,), (1,)), ((), ())), preferred_element_type=jnp.float32)
+    half = made.shape[0] // 2
+    return jnp.concatenate([made[:half], made[half:]], axis=1).astype(jnp.bfloat16)
 
 
 def parameters_kernel(
@@ -266,21 +268,22 @@
 ):
     for b in range(slot_ref.shape[0]):
         slot2_ref[b] = slot_ref[b]
-    own_ref[0] = emb_ref[...]
+    own_ref[0] = project(emb_ref[...], pw_ref[...])
+    pw2_ref[...] = pw_ref[...]
     cw2_ref[...] = cw_ref[...]
-    for ref, to, axis in ((pw_ref, pw2_ref, 0), (pb_ref, pb2_ref, 1), (cb_ref, cb2_ref, 1)):
-        to[...] = jnp.concatenate([ref[...]] * 2, axis=axis)
+    for ref, to in ((pb_ref, pb2_ref), (cb_ref, cb2_ref)):
+        to[...] = jnp.concatenate([ref[...]] * 2, axis=1)
 
 
 def parameters_call(block_slot, bin_embed, proj_weight, proj_bias, conv_bias, weights):
     vmem, smem = pl.BlockSpec(memory_space=pltpu.VMEM), pl.BlockSpec(memory_space=pltpu.SMEM)
-    ch, emb = proj_weight.shape
+    tile, ch = bin_embed.shape[0], proj_weight.shape[0]
     return pl.pallas_call(
         parameters_kernel,
         out_shape=(
             pltpu.SMEM(block_slot.shape, block_slot.dtype),
-            pltpu.VMEM((1,) + bin_embed.shape, bin_embed.dtype),
-            pltpu.VMEM((2 * ch, emb), proj_weight.dtype),
+            pltpu.VMEM((1, tile // 2, 2 * ch), jnp.bfloat16),
+            pltpu.VMEM(proj_weight.shape, proj_weight.dtype),
             pltpu.VMEM((1, 2 * ch), proj_bias.dtype),
             pltpu.VMEM((conv_bias.shape[0], 2 * ch), conv_bias.dtype),
             pltpu.VMEM(weights.shape, weights.dtype),
@@ -289,6 +292,31 @@
         out_specs=(smem,) + (vmem,) * 5,
         cost_estimate=pl.CostEstimate(flops=1000000, bytes_accessed=1000000, transcendentals=0),
     )(block_slot, bin_embed, proj_weight, proj_bias, conv_bias, weights)
+
+
+def project_kernel(own_ref, emb_ref, pw_ref, out_ref):
+    count = emb_ref.shape[0]
+    if own_ref is not None:
+        out_ref[0] = own_ref[0]
+    for b in range(count):
+        out_ref[out_ref.shape[0] - count + b] = project(emb_ref[b], pw_ref[...])
+
+
+def project_call(own, embeds, proj_weight):
+    vmem = pl.BlockSpec(memory_space=pltpu.VMEM)
+    blocks, tile, _ = embeds.shape
+    ch = proj_weight.shape[0]
+    kernel, args = project_kernel, (own, embeds, proj_weight)
+    if own is None:
+        kernel, args = functools.partial(project_kernel, None), args[1:]
+    args = [pltpu.with_memory_space_constraint(arg, pltpu.VMEM) for arg in args]
+    return pl.pallas_call(
+        kernel,
+        out_shape=pltpu.VMEM((blocks + len(args) - 2, tile // 2, 2 * ch), jnp.bfloat16),
+        in_specs=[vmem] * len(args),
+        out_specs=vmem,
+        cost_estimate=pl.CostEstimate(flops=1000000, bytes_accessed=100000, transcendentals=0),
+    )(*args)
 
 
 def band_call(weights, which):
@@ -316,16 +344,18 @@
     for stage, bit in enumerate(order):
         there = lax.ppermute(table, "pos", [(i, i ^ (1 << bit | 1)) for i in range(npos)])
         if stage == 0:
-            slots, table, *small, turned = parameters_call(*small)
+            slots, table, projection, *small, turned = parameters_call(*small)
             there, table, small, slots, turned = lax.optimization_barrier((there, table, small, slots, turned))
-        elif todo:
+            table = project_call(table, there, projection)
+            continue
+        if todo:
             made = band_call(turned, todo[:2])
             there, made, turned = lax.optimization_barrier((there, made, turned))
             banded, todo = banded + list(made), todo[2:]
         table = jnp.concatenate([table, there], axis=0)
     if not order:
-        slots, _, *small, turned = parameters_call(*small)
-        table = lax.all_gather(bin_embed, "pos")
+        slots, _, projection, *small, turned = parameters_call(*small)
+        table = project_call(None, lax.all_gather(bin_embed, "pos"), projection)
     if todo:
         banded += band_call(turned, todo)
     out = tile_call(npos, noff, order, layers, slots, table, *small, banded)

time: 20.8 us -> 20.4 us (0.981)
  waiting for transfers between devices: 4.81 us -> 3.94 us
  Pallas kernels: 8.21 us -> 8.69 us
    ppermute x4, waiting for transfers between devices: 4.81 us -> 3.94 us  [on_device(): lax.ppermute(table, 'pos', [(i, i ^ (1 << bit | 1)) for i in range(npos)])]
  transfers between devices with their start and end apart: 4 -> 4, of which waited for: 4 -> 4; matrix products, arithmetic and copies ran while one was open for 0% -> 0% of each run, Pallas kernels for 8% -> 9%
where the time goes in v6:
time: 20.4 us; the launch traced here: 20.3 us
  Pallas kernels  8.69 us (43%)
  starting transfers between devices  7.56 us (37%)
  waiting for transfers between devices  3.94 us (19%)
    ppermute x4, starting transfers between devices, on_device(): lax.ppermute(table, 'pos', [(i, i ^ (1 << bit | 1)) for i in range(npos)])  7.56 us
    pallas_call x1, Pallas kernels, tile_call(): pl.pallas_call(functools.partial(tile_kernel, (layers, tile, ch, npos, no...  6.75 us
    ppermute x4, waiting for transfers between devices, on_device(): lax.ppermute(table, 'pos', [(i, i ^ (1 << bit | 1)) for i in range(npos)])  3.94 us
    pallas_call x1, Pallas kernels, parameters_call(): pl.pallas_call(parameters_kernel, out_shape=(pltpu.SMEM(block_slot.shape,...  1.25 us
    pallas_call x2, Pallas kernels, band_call(): pl.pallas_call(functools.partial(weights_kernel, ch, which), out_shape=(p...  0.5 us
  transfers between devices with their start and end apart: 4, of which 4 were waited for; matrix products, arithmetic and copies ran while one was open for 0% of the time, Pallas kernels for 9%

profile of v6, /device:TPU:0, one launch (start us, length us, event | category | flops | bytes accessed | tf_op | source)
XLA Modules:
  0.0 20.3 jit_solution(1988176850955326038)
XLA Ops:
  0.0 3.5 %collective-permute-start = (bf16[1,64,128]{2,1,0:T(8,128)(2,1)}, bf16[1,64,128]{2,1,0:T(8,128)(2,1)S(1)}, u32[]{:S(2)}, u32[]{:S(2)}) collective-permute-start(bf16[1,64,128]{2,1,0:T(8,128)(2,1)} %bitcast.7), channel_id=1, source_target_pairs={{0,18},{2,16},{4,22},{6,20},{8,26},{10,24},{12,30},{14,28},{16,2},... | collective-permute-start | bytes 49160 | tf_op jit(solution)/shard_map/ppermute | solution.py:345
  3.5 1.3 %shard_map.64 = (s32[16]{0:T(128)S(4)}, bf16[1,32,128]{2,1,0:T(8,128)(2,1)S(1)}, bf16[64,128]{1,0:T(8,128)(2,1)S(1)}, f32[1,128]{1,0:T(1,128)S(1)}, f32[4,128]{1...) custom-call(s32[16]{0:T(128)} %slot_ref.1, bf16[64,128]{1,0:T(8,128)(2,1)} %emb_ref.1, bf16[64,128]{1,0:T(8,128)(2,1)} %bitcast.6, ...), custom_call_target="tpu_custom_call" | custom-call | flops 1000000 | bytes 1000000 | tf_op jit(solution)/shard_map/pallas_call | solution.py:281
  4.7 0.4 %collective-permute-done.emb_ref = bf16[1,64,128]{2,1,0:T(8,128)(2,1)S(1)} collective-permute-done((bf16[1,64,128]{2,1,0:T(8,128)(2,1)}, bf16[1,64,128]{2,1,0:T(8,128)(2,1)S(1)}, u32[]{:S(2)}, u32[]{:S(2)}) %collective-permute-start) | collective-permute-done | bytes 16416 | tf_op jit(solution)/shard_map/ppermute | solution.py:345
  5.1 0.2 shard_map.65
  5.3 1.9 %collective-permute-start.1 = (bf16[2,32,128]{2,1,0:T(8,128)(2,1)S(1)}, bf16[2,32,128]{2,1,0:T(8,128)(2,1)S(1)}, u32[]{:S(2)}, u32[]{:S(2)}) collective-permute-start(bf16[2,32,128]{2,1,0:T(8,128)(2,1)S(1)} %shard_map.65), channel_id=1, source_target_pairs={{0,10},{2,8},{4,14},{6,12},{8,2},{10,0},{12,6},{14,4},{16,26},{18,... | collective-permute-start | bytes 49160 | tf_op jit(solution)/shard_map/ppermute | solution.py:345
  7.2 0.3 %shard_map.66 = (bf16[1152,256]{1,0:T(8,128)(2,1)S(1)}, bf16[1152,256]{1,0:T(8,128)(2,1)S(1)}) custom-call(bf16[4,64,576]{2,1,0:T(8,128)(2,1)S(1)} %get-tuple-element.41.cw_ref), custom_call_target="tpu_custom_call" | custom-call | flops 1000000 | bytes 1000000 | tf_op jit(solution)/shard_map/pallas_call | solution.py:326
  7.5 1.2 %collective-permute-done.1 = bf16[2,32,128]{2,1,0:T(8,128)(2,1)S(1)} collective-permute-done((bf16[2,32,128]{2,1,0:T(8,128)(2,1)S(1)}, bf16[2,32,128]{2,1,0:T(8,128)(2,1)S(1)}, u32[]{:S(2)}, u32[]{:S(2)}) %collective-permute-start.1) | collective-permute-done | bytes 16416 | tf_op jit(solution)/shard_map/ppermute | solution.py:345
  8.7 1.6 %collective-permute-start.2 = (bf16[4,32,128]{2,1,0:T(8,128)(2,1)S(1)}, bf16[4,32,128]{2,1,0:T(8,128)(2,1)S(1)}, u32[]{:S(2)}, u32[]{:S(2)}) collective-permute-start(bf16[4,32,128]{2,1,0:T(8,128)(2,1)S(1)} %pad_maximum_fusion.2), channel_id=1, source_target_pairs={{0,6},{2,4},{4,2},{6,0},{8,14},{10,12},{12,10},{14,8},{16,22},{18,... | collective-permute-start | bytes 98312 | tf_op jit(solution)/shard_map/ppermute | solution.py:345
  10.3 0.3 %shard_map.67 = (bf16[1152,256]{1,0:T(8,128)(2,1)S(1)}, bf16[1152,256]{1,0:T(8,128)(2,1)S(1)}) custom-call(bf16[4,64,576]{2,1,0:T(8,128)(2,1)S(1)} %get-tuple-element.41.cw_ref), custom_call_target="tpu_custom_call" | custom-call | flops 1000000 | bytes 1000000 | tf_op jit(solution)/shard_map/pallas_call | solution.py:326
  10.6 1.4 %collective-permute-done.2 = bf16[4,32,128]{2,1,0:T(8,128)(2,1)S(1)} collective-permute-done((bf16[4,32,128]{2,1,0:T(8,128)(2,1)S(1)}, bf16[4,32,128]{2,1,0:T(8,128)(2,1)S(1)}, u32[]{:S(2)}, u32[]{:S(2)}) %collective-permute-start.2) | collective-permute-done | bytes 32800 | tf_op jit(solution)/shard_map/ppermute | solution.py:345
  12.0 0.6 %collective-permute-start.3 = (bf16[8,32,128]{2,1,0:T(8,128)(2,1)S(1)}, bf16[8,32,128]{2,1,0:T(8,128)(2,1)S(1)}, u32[]{:S(2)}, u32[]{:S(2)}) collective-permute-start(bf16[8,32,128]{2,1,0:T(8,128)(2,1)S(1)} %pad_maximum_fusion.1), channel_id=1, source_target_pairs={{0,2},{2,0},{4,6},{6,4},{8,10},{10,8},{12,14},{14,12},{16,18},{18,... | collective-permute-start | bytes 196616 | tf_op jit(solution)/shard_map/ppermute | solution.py:345
  12.6 0.9 %collective-permute-done.3 = bf16[8,32,128]{2,1,0:T(8,128)(2,1)S(1)} collective-permute-done((bf16[8,32,128]{2,1,0:T(8,128)(2,1)S(1)}, bf16[8,32,128]{2,1,0:T(8,128)(2,1)S(1)}, u32[]{:S(2)}, u32[]{:S(2)}) %collective-permute-start.3) | collective-permute-done | bytes 65568 | tf_op jit(solution)/shard_map/ppermute | solution.py:345
  13.5 6.7 %shard_map.68 = bf16[64,4096]{1,0:T(8,128)(2,1)} custom-call(s32[16]{0:T(128)S(4)} %get-tuple-element.33.slot_ref, bf16[16,32,128]{2,1,0:T(8,128)(2,1)S(1)} %pad_maximum_fusion.bin_ref, f32[1,128]{1,0:T(1,128)S(1)} %get-tuple-element.45.pb_ref, f32[4,128]{1,0:T(4,128)S(1)} %get-tuple-element.46.cb_ref, bf16[1152,256]{1,0:T(8,128)(2,1)S(1)} %get-tuple-element.47.refs_0_, ...), custom_call_target="tpu_custom_call" | custom-call | flops 8000000000 | bytes 4000000 | tf_op jit(solution)/shard_map/pallas_call | solution.py:239
  (3 shorter events, 0.0 us)
Async XLA Ops:
  0.0 5.1 %collective-permute-start = (bf16[1,64,128]{2,1,0:T(8,128)(2,1)}, bf16[1,64,128]{2,1,0:T(8,128)(2,1)S(1)}, u32[]{:S(2)}, u32[]{:S(2)}) collective-permute-start(bf16[1,64,128]{2,1,0:T(8,128)(2,1)} %bitcast.7), channel_id=1, source_target_pairs={{0,18},{2,16},{4,22},{6,20},{8,26},{10,24},{12,30},{14,28},{16,2},... | collective-permute-start | bytes 49160 | tf_op jit(solution)/shard_map/ppermute | solution.py:345
  5.3 3.3 %collective-permute-start.1 = (bf16[2,32,128]{2,1,0:T(8,128)(2,1)S(1)}, bf16[2,32,128]{2,1,0:T(8,128)(2,1)S(1)}, u32[]{:S(2)}, u32[]{:S(2)}) collective-permute-start(bf16[2,32,128]{2,1,0:T(8,128)(2,1)S(1)} %shard_map.65), channel_id=1, source_target_pairs={{0,10},{2,8},{4,14},{6,12},{8,2},{10,0},{12,6},{14,4},{16,26},{18,... | collective-permute-start | bytes 49160 | tf_op jit(solution)/shard_map/ppermute | solution.py:345
  8.7 3.3 %collective-permute-start.2 = (bf16[4,32,128]{2,1,0:T(8,128)(2,1)S(1)}, bf16[4,32,128]{2,1,0:T(8,128)(2,1)S(1)}, u32[]{:S(2)}, u32[]{:S(2)}) collective-permute-start(bf16[4,32,128]{2,1,0:T(8,128)(2,1)S(1)} %pad_maximum_fusion.2), channel_id=1, source_target_pairs={{0,6},{2,4},{4,2},{6,0},{8,14},{10,12},{12,10},{14,8},{16,22},{18,... | collective-permute-start | bytes 98312 | tf_op jit(solution)/shard_map/ppermute | solution.py:345
  12.0 1.5 %collective-permute-start.3 = (bf16[8,32,128]{2,1,0:T(8,128)(2,1)S(1)}, bf16[8,32,128]{2,1,0:T(8,128)(2,1)S(1)}, u32[]{:S(2)}, u32[]{:S(2)}) collective-permute-start(bf16[8,32,128]{2,1,0:T(8,128)(2,1)S(1)} %pad_maximum_fusion.1), channel_id=1, source_target_pairs={{0,2},{2,0},{4,6},{6,4},{8,10},{10,8},{12,14},{14,12},{16,18},{18,... | collective-permute-start | bytes 196616 | tf_op jit(solution)/shard_map/ppermute | solution.py:345

commit v7 on v6

--- a/solution.py
+++ b/solution.py
@@ -8,6 +8,7 @@
 from jax.sharding import PartitionSpec as P
 
 GROUP = 4
+FIRST_GROUP = 6
 BASE = 8
 EDGE = 16
 
@@ -198,8 +199,9 @@
         size = rows - 2 * start
         count = (tile + 2 * halos[l + 1]) // (4 * dil)
         blocks = [(j, e) for j in reversed(range(count)) for e in range(dil)]
-        for at in range(0, len(blocks), GROUP):
-            some = blocks[at : at + GROUP]
+        group_size = GROUP if l else FIRST_GROUP
+        for at in range(0, len(blocks), group_size):
+            some = blocks[at : at + group_size]
             need = [(2 * j + s) * dil + e for j, e in some for s in range(3)]
             if l == 0:
                 for group in need:

time: 20.4 us -> 20.4 us (level)
  no operation moved by 1% of the time
where the time goes in v7:
time: 20.4 us; the launch traced here: 20.2 us
  Pallas kernels  8.62 us (42%)
  starting transfers between devices  7.56 us (37%)
  waiting for transfers between devices  3.94 us (19%)
    ppermute x4, starting transfers between devices, on_device(): lax.ppermute(table, 'pos', [(i, i ^ (1 << bit | 1)) for i in range(npos)])  7.56 us
    pallas_call x1, Pallas kernels, tile_call(): pl.pallas_call(functools.partial(tile_kernel, (layers, tile, ch, npos, no...  6.67 us
    ppermute x4, waiting for transfers between devices, on_device(): lax.ppermute(table, 'pos', [(i, i ^ (1 << bit | 1)) for i in range(npos)])  3.94 us
    pallas_call x1, Pallas kernels, parameters_call(): pl.pallas_call(parameters_kernel, out_shape=(pltpu.SMEM(block_slot.shape,...  1.25 us
    pallas_call x2, Pallas kernels, band_call(): pl.pallas_call(functools.partial(weights_kernel, ch, which), out_shape=(p...  0.5 us
  transfers between devices with their start and end apart: 4, of which 4 were waited for; matrix products, arithmetic and copies ran while one was open for 0% of the time, Pallas kernels for 9%

profile of v7, /device:TPU:0, one launch (start us, length us, event | category | flops | bytes accessed | tf_op | source)
XLA Modules:
  0.0 20.2 jit_solution(3685857482854113844)
XLA Ops:
  0.0 3.5 %collective-permute-start = (bf16[1,64,128]{2,1,0:T(8,128)(2,1)}, bf16[1,64,128]{2,1,0:T(8,128)(2,1)S(1)}, u32[]{:S(2)}, u32[]{:S(2)}) collective-permute-start(bf16[1,64,128]{2,1,0:T(8,128)(2,1)} %bitcast.7), channel_id=1, source_target_pairs={{0,18},{2,16},{4,22},{6,20},{8,26},{10,24},{12,30},{14,28},{16,2},... | collective-permute-start | bytes 49160 | tf_op jit(solution)/shard_map/ppermute | solution.py:347
  3.5 1.3 %shard_map.64 = (s32[16]{0:T(128)S(4)}, bf16[1,32,128]{2,1,0:T(8,128)(2,1)S(1)}, bf16[64,128]{1,0:T(8,128)(2,1)S(1)}, f32[1,128]{1,0:T(1,128)S(1)}, f32[4,128]{1...) custom-call(s32[16]{0:T(128)} %slot_ref.1, bf16[64,128]{1,0:T(8,128)(2,1)} %emb_ref.1, bf16[64,128]{1,0:T(8,128)(2,1)} %bitcast.6, ...), custom_call_target="tpu_custom_call" | custom-call | flops 1000000 | bytes 1000000 | tf_op jit(solution)/shard_map/pallas_call | solution.py:283
  4.7 0.4 %collective-permute-done.emb_ref = bf16[1,64,128]{2,1,0:T(8,128)(2,1)S(1)} collective-permute-done((bf16[1,64,128]{2,1,0:T(8,128)(2,1)}, bf16[1,64,128]{2,1,0:T(8,128)(2,1)S(1)}, u32[]{:S(2)}, u32[]{:S(2)}) %collective-permute-start) | collective-permute-done | bytes 16416 | tf_op jit(solution)/shard_map/ppermute | solution.py:347
  5.1 0.2 shard_map.65
  5.3 1.9 %collective-permute-start.1 = (bf16[2,32,128]{2,1,0:T(8,128)(2,1)S(1)}, bf16[2,32,128]{2,1,0:T(8,128)(2,1)S(1)}, u32[]{:S(2)}, u32[]{:S(2)}) collective-permute-start(bf16[2,32,128]{2,1,0:T(8,128)(2,1)S(1)} %shard_map.65), channel_id=1, source_target_pairs={{0,10},{2,8},{4,14},{6,12},{8,2},{10,0},{12,6},{14,4},{16,26},{18,... | collective-permute-start | bytes 49160 | tf_op jit(solution)/shard_map/ppermute | solution.py:347
  7.2 0.3 %shard_map.66 = (bf16[1152,256]{1,0:T(8,128)(2,1)S(1)}, bf16[1152,256]{1,0:T(8,128)(2,1)S(1)}) custom-call(bf16[4,64,576]{2,1,0:T(8,128)(2,1)S(1)} %get-tuple-element.41.cw_ref), custom_call_target="tpu_custom_call" | custom-call | flops 1000000 | bytes 1000000 | tf_op jit(solution)/shard_map/pallas_call | solution.py:328
  7.5 1.2 %collective-permute-done.1 = bf16[2,32,128]{2,1,0:T(8,128)(2,1)S(1)} collective-permute-done((bf16[2,32,128]{2,1,0:T(8,128)(2,1)S(1)}, bf16[2,32,128]{2,1,0:T(8,128)(2,1)S(1)}, u32[]{:S(2)}, u32[]{:S(2)}) %collective-permute-start.1) | collective-permute-done | bytes 16416 | tf_op jit(solution)/shard_map/ppermute | solution.py:347
  8.7 1.6 %collective-permute-start.2 = (bf16[4,32,128]{2,1,0:T(8,128)(2,1)S(1)}, bf16[4,32,128]{2,1,0:T(8,128)(2,1)S(1)}, u32[]{:S(2)}, u32[]{:S(2)}) collective-permute-start(bf16[4,32,128]{2,1,0:T(8,128)(2,1)S(1)} %pad_maximum_fusion.2), channel_id=1, source_target_pairs={{0,6},{2,4},{4,2},{6,0},{8,14},{10,12},{12,10},{14,8},{16,22},{18,... | collective-permute-start | bytes 98312 | tf_op jit(solution)/shard_map/ppermute | solution.py:347
  10.3 0.3 %shard_map.67 = (bf16[1152,256]{1,0:T(8,128)(2,1)S(1)}, bf16[1152,256]{1,0:T(8,128)(2,1)S(1)}) custom-call(bf16[4,64,576]{2,1,0:T(8,128)(2,1)S(1)} %get-tuple-element.41.cw_ref), custom_call_target="tpu_custom_call" | custom-call | flops 1000000 | bytes 1000000 | tf_op jit(solution)/shard_map/pallas_call | solution.py:328
  10.6 1.4 %collective-permute-done.2 = bf16[4,32,128]{2,1,0:T(8,128)(2,1)S(1)} collective-permute-done((bf16[4,32,128]{2,1,0:T(8,128)(2,1)S(1)}, bf16[4,32,128]{2,1,0:T(8,128)(2,1)S(1)}, u32[]{:S(2)}, u32[]{:S(2)}) %collective-permute-start.2) | collective-permute-done | bytes 32800 | tf_op jit(solution)/shard_map/ppermute | solution.py:347
  12.0 0.6 %collective-permute-start.3 = (bf16[8,32,128]{2,1,0:T(8,128)(2,1)S(1)}, bf16[8,32,128]{2,1,0:T(8,128)(2,1)S(1)}, u32[]{:S(2)}, u32[]{:S(2)}) collective-permute-start(bf16[8,32,128]{2,1,0:T(8,128)(2,1)S(1)} %pad_maximum_fusion.1), channel_id=1, source_target_pairs={{0,2},{2,0},{4,6},{6,4},{8,10},{10,8},{12,14},{14,12},{16,18},{18,... | collective-permute-start | bytes 196616 | tf_op jit(solution)/shard_map/ppermute | solution.py:347
  12.6 0.9 %collective-permute-done.3 = bf16[8,32,128]{2,1,0:T(8,128)(2,1)S(1)} collective-permute-done((bf16[8,32,128]{2,1,0:T(8,128)(2,1)S(1)}, bf16[8,32,128]{2,1,0:T(8,128)(2,1)S(1)}, u32[]{:S(2)}, u32[]{:S(2)}) %collective-permute-start.3) | collective-permute-done | bytes 65568 | tf_op jit(solution)/shard_map/ppermute | solution.py:347
  13.5 6.7 %shard_map.68 = bf16[64,4096]{1,0:T(8,128)(2,1)} custom-call(s32[16]{0:T(128)S(4)} %get-tuple-element.33.slot_ref, bf16[16,32,128]{2,1,0:T(8,128)(2,1)S(1)} %pad_maximum_fusion.bin_ref, f32[1,128]{1,0:T(1,128)S(1)} %get-tuple-element.45.pb_ref, f32[4,128]{1,0:T(4,128)S(1)} %get-tuple-element.46.cb_ref, bf16[1152,256]{1,0:T(8,128)(2,1)S(1)} %get-tuple-element.47.refs_0_, ...), custom_call_target="tpu_custom_call" | custom-call | flops 8000000000 | bytes 4000000 | tf_op jit(solution)/shard_map/pallas_call | solution.py:241
  (3 shorter events, 0.0 us)
Async XLA Ops:
  0.0 5.1 %collective-permute-start = (bf16[1,64,128]{2,1,0:T(8,128)(2,1)}, bf16[1,64,128]{2,1,0:T(8,128)(2,1)S(1)}, u32[]{:S(2)}, u32[]{:S(2)}) collective-permute-start(bf16[1,64,128]{2,1,0:T(8,128)(2,1)} %bitcast.7), channel_id=1, source_target_pairs={{0,18},{2,16},{4,22},{6,20},{8,26},{10,24},{12,30},{14,28},{16,2},... | collective-permute-start | bytes 49160 | tf_op jit(solution)/shard_map/ppermute | solution.py:347
  5.3 3.3 %collective-permute-start.1 = (bf16[2,32,128]{2,1,0:T(8,128)(2,1)S(1)}, bf16[2,32,128]{2,1,0:T(8,128)(2,1)S(1)}, u32[]{:S(2)}, u32[]{:S(2)}) collective-permute-start(bf16[2,32,128]{2,1,0:T(8,128)(2,1)S(1)} %shard_map.65), channel_id=1, source_target_pairs={{0,10},{2,8},{4,14},{6,12},{8,2},{10,0},{12,6},{14,4},{16,26},{18,... | collective-permute-start | bytes 49160 | tf_op jit(solution)/shard_map/ppermute | solution.py:347
  8.7 3.3 %collective-permute-start.2 = (bf16[4,32,128]{2,1,0:T(8,128)(2,1)S(1)}, bf16[4,32,128]{2,1,0:T(8,128)(2,1)S(1)}, u32[]{:S(2)}, u32[]{:S(2)}) collective-permute-start(bf16[4,32,128]{2,1,0:T(8,128)(2,1)S(1)} %pad_maximum_fusion.2), channel_id=1, source_target_pairs={{0,6},{2,4},{4,2},{6,0},{8,14},{10,12},{12,10},{14,8},{16,22},{18,... | collective-permute-start | bytes 98312 | tf_op jit(solution)/shard_map/ppermute | solution.py:347
  12.0 1.5 %collective-permute-start.3 = (bf16[8,32,128]{2,1,0:T(8,128)(2,1)S(1)}, bf16[8,32,128]{2,1,0:T(8,128)(2,1)S(1)}, u32[]{:S(2)}, u32[]{:S(2)}) collective-permute-start(bf16[8,32,128]{2,1,0:T(8,128)(2,1)S(1)} %pad_maximum_fusion.1), channel_id=1, source_target_pairs={{0,2},{2,0},{4,6},{6,4},{8,10},{10,8},{12,14},{14,12},{16,18},{18,... | collective-permute-start | bytes 196616 | tf_op jit(solution)/shard_map/ppermute | solution.py:347

commit v8 on v7

--- a/solution.py
+++ b/solution.py
@@ -156,11 +156,17 @@
         ready[0].add(group)
 
     stretch = 2**layers
-    span = 2 * stretch * ch
-
-    def send(j):
-        here = (slice(None), pl.ds(j * span, span))
-        return pltpu.make_async_copy(made_ref.at[here], out_ref.at[here], sems.at[j])
+    runs = stretch // 2 // GROUP
+
+    def sends(j, run):
+        copies = []
+        for k in range(4):
+            first = 2 * stretch * j + run * GROUP + k * stretch // 2
+            here = (slice(None), pl.ds(first * ch, GROUP * ch))
+            copies.append(
+                pltpu.make_async_copy(made_ref.at[here], out_ref.at[here], sems.at[(j * runs + run) * 4 + k])
+            )
+        return copies
 
     def finish(l, some, acc):
         dil = 2**l
@@ -189,8 +195,9 @@
                     col += stretch * ch
                     value = pick(pltpu.roll(even[s], ch, 1), new[s])
                     made_ref[:, col : col + wide] = value.astype(made_ref.dtype)
-                if e == dil - 1:
-                    send(j).start()
+                if e % GROUP == GROUP - 1:
+                    for copy in sends(j, e // GROUP):
+                        copy.start()
 
     unfinished = None
     for l in range(layers):
@@ -228,7 +235,9 @@
             unfinished = (l, some, acc)
     finish(*unfinished)
     for j in range(tile // (2 * stretch)):
-        send(j).wait()
+        for run in range(runs):
+            for copy in sends(j, run):
+                copy.wait()
 
 
 def tile_call(npos, noff, order, layers, block_slot, table, proj_bias, conv_bias, banded):
@@ -252,7 +261,7 @@
             pltpu.VMEM(((EDGE + 1) * EDGE, wide), jnp.float32),
             pltpu.VMEM((high, wide), jnp.float32),
             pltpu.VMEM((tile, tile * ch), jnp.bfloat16),
-            pltpu.SemaphoreType.DMA((tile // 2 ** (layers + 1),)),
+            pltpu.SemaphoreType.DMA((tile // GROUP,)),
         ],
         compiler_params=pltpu.CompilerParams(vmem_limit_bytes=48 * 1024 * 1024),
         cost_estimate=pl.CostEstimate(flops=8000000000, bytes_accessed=4000000, transcendentals=2000000),

time: 20.4 us -> 20.5 us (level)
  no operation moved by 1% of the time
where the time goes in v8:
time: 20.5 us; the launch traced here: 20.3 us
  Pallas kernels  8.77 us (43%)
  starting transfers between devices  7.56 us (37%)
  waiting for transfers between devices  3.94 us (19%)
    ppermute x4, starting transfers between devices, on_device(): lax.ppermute(table, 'pos', [(i, i ^ (1 << bit | 1)) for i in range(npos)])  7.56 us
    pallas_call x1, Pallas kernels, tile_call(): pl.pallas_call(functools.partial(tile_kernel, (layers, tile, ch, npos, no...  6.83 us
    ppermute x4, waiting for transfers between devices, on_device(): lax.ppermute(table, 'pos', [(i, i ^ (1 << bit | 1)) for i in range(npos)])  3.94 us
    pallas_call x1, Pallas kernels, parameters_call(): pl.pallas_call(parameters_kernel, out_shape=(pltpu.SMEM(block_slot.shape,...  1.25 us
    pallas_call x2, Pallas kernels, band_call(): pl.pallas_call(functools.partial(weights_kernel, ch, which), out_shape=(p...  0.5 us
  transfers between devices with their start and end apart: 4, of which 4 were waited for; matrix products, arithmetic and copies ran while one was open for 0% of the time, Pallas kernels for 9%

profile of v8, /device:TPU:0, one launch (start us, length us, event | category | flops | bytes accessed | tf_op | source)
XLA Modules:
  0.0 20.3 jit_solution(15676517196048704886)
XLA Ops:
  0.0 3.5 %collective-permute-start = (bf16[1,64,128]{2,1,0:T(8,128)(2,1)}, bf16[1,64,128]{2,1,0:T(8,128)(2,1)S(1)}, u32[]{:S(2)}, u32[]{:S(2)}) collective-permute-start(bf16[1,64,128]{2,1,0:T(8,128)(2,1)} %bitcast.7), channel_id=1, source_target_pairs={{0,18},{2,16},{4,22},{6,20},{8,26},{10,24},{12,30},{14,28},{16,2},... | collective-permute-start | bytes 49160 | tf_op jit(solution)/shard_map/ppermute | solution.py:356
  3.5 1.3 %shard_map.64 = (s32[16]{0:T(128)S(4)}, bf16[1,32,128]{2,1,0:T(8,128)(2,1)S(1)}, bf16[64,128]{1,0:T(8,128)(2,1)S(1)}, f32[1,128]{1,0:T(1,128)S(1)}, f32[4,128]{1...) custom-call(s32[16]{0:T(128)} %slot_ref.1, bf16[64,128]{1,0:T(8,128)(2,1)} %emb_ref.1, bf16[64,128]{1,0:T(8,128)(2,1)} %bitcast.6, ...), custom_call_target="tpu_custom_call" | custom-call | flops 1000000 | bytes 1000000 | tf_op jit(solution)/shard_map/pallas_call | solution.py:292
  4.7 0.4 %collective-permute-done.emb_ref = bf16[1,64,128]{2,1,0:T(8,128)(2,1)S(1)} collective-permute-done((bf16[1,64,128]{2,1,0:T(8,128)(2,1)}, bf16[1,64,128]{2,1,0:T(8,128)(2,1)S(1)}, u32[]{:S(2)}, u32[]{:S(2)}) %collective-permute-start) | collective-permute-done | bytes 16416 | tf_op jit(solution)/shard_map/ppermute | solution.py:356
  5.1 0.2 shard_map.65
  5.3 1.9 %collective-permute-start.1 = (bf16[2,32,128]{2,1,0:T(8,128)(2,1)S(1)}, bf16[2,32,128]{2,1,0:T(8,128)(2,1)S(1)}, u32[]{:S(2)}, u32[]{:S(2)}) collective-permute-start(bf16[2,32,128]{2,1,0:T(8,128)(2,1)S(1)} %shard_map.65), channel_id=1, source_target_pairs={{0,10},{2,8},{4,14},{6,12},{8,2},{10,0},{12,6},{14,4},{16,26},{18,... | collective-permute-start | bytes 49160 | tf_op jit(solution)/shard_map/ppermute | solution.py:356
  7.2 0.3 %shard_map.66 = (bf16[1152,256]{1,0:T(8,128)(2,1)S(1)}, bf16[1152,256]{1,0:T(8,128)(2,1)S(1)}) custom-call(bf16[4,64,576]{2,1,0:T(8,128)(2,1)S(1)} %get-tuple-element.41.cw_ref), custom_call_target="tpu_custom_call" | custom-call | flops 1000000 | bytes 1000000 | tf_op jit(solution)/shard_map/pallas_call | solution.py:337
  7.5 1.2 %collective-permute-done.1 = bf16[2,32,128]{2,1,0:T(8,128)(2,1)S(1)} collective-permute-done((bf16[2,32,128]{2,1,0:T(8,128)(2,1)S(1)}, bf16[2,32,128]{2,1,0:T(8,128)(2,1)S(1)}, u32[]{:S(2)}, u32[]{:S(2)}) %collective-permute-start.1) | collective-permute-done | bytes 16416 | tf_op jit(solution)/shard_map/ppermute | solution.py:356
  8.7 1.6 %collective-permute-start.2 = (bf16[4,32,128]{2,1,0:T(8,128)(2,1)S(1)}, bf16[4,32,128]{2,1,0:T(8,128)(2,1)S(1)}, u32[]{:S(2)}, u32[]{:S(2)}) collective-permute-start(bf16[4,32,128]{2,1,0:T(8,128)(2,1)S(1)} %pad_maximum_fusion.2), channel_id=1, source_target_pairs={{0,6},{2,4},{4,2},{6,0},{8,14},{10,12},{12,10},{14,8},{16,22},{18,... | collective-permute-start | bytes 98312 | tf_op jit(solution)/shard_map/ppermute | solution.py:356
  10.3 0.3 %shard_map.67 = (bf16[1152,256]{1,0:T(8,128)(2,1)S(1)}, bf16[1152,256]{1,0:T(8,128)(2,1)S(1)}) custom-call(bf16[4,64,576]{2,1,0:T(8,128)(2,1)S(1)} %get-tuple-element.41.cw_ref), custom_call_target="tpu_custom_call" | custom-call | flops 1000000 | bytes 1000000 | tf_op jit(solution)/shard_map/pallas_call | solution.py:337
  10.6 1.4 %collective-permute-done.2 = bf16[4,32,128]{2,1,0:T(8,128)(2,1)S(1)} collective-permute-done((bf16[4,32,128]{2,1,0:T(8,128)(2,1)S(1)}, bf16[4,32,128]{2,1,0:T(8,128)(2,1)S(1)}, u32[]{:S(2)}, u32[]{:S(2)}) %collective-permute-start.2) | collective-permute-done | bytes 32800 | tf_op jit(solution)/shard_map/ppermute | solution.py:356
  12.0 0.6 %collective-permute-start.3 = (bf16[8,32,128]{2,1,0:T(8,128)(2,1)S(1)}, bf16[8,32,128]{2,1,0:T(8,128)(2,1)S(1)}, u32[]{:S(2)}, u32[]{:S(2)}) collective-permute-start(bf16[8,32,128]{2,1,0:T(8,128)(2,1)S(1)} %pad_maximum_fusion.1), channel_id=1, source_target_pairs={{0,2},{2,0},{4,6},{6,4},{8,10},{10,8},{12,14},{14,12},{16,18},{18,... | collective-permute-start | bytes 196616 | tf_op jit(solution)/shard_map/ppermute | solution.py:356
  12.6 0.9 %collective-permute-done.3 = bf16[8,32,128]{2,1,0:T(8,128)(2,1)S(1)} collective-permute-done((bf16[8,32,128]{2,1,0:T(8,128)(2,1)S(1)}, bf16[8,32,128]{2,1,0:T(8,128)(2,1)S(1)}, u32[]{:S(2)}, u32[]{:S(2)}) %collective-permute-start.3) | collective-permute-done | bytes 65568 | tf_op jit(solution)/shard_map/ppermute | solution.py:356
  13.5 6.8 %shard_map.68 = bf16[64,4096]{1,0:T(8,128)(2,1)} custom-call(s32[16]{0:T(128)S(4)} %get-tuple-element.33.slot_ref, bf16[16,32,128]{2,1,0:T(8,128)(2,1)S(1)} %pad_maximum_fusion.bin_ref, f32[1,128]{1,0:T(1,128)S(1)} %get-tuple-element.45.pb_ref, f32[4,128]{1,0:T(4,128)S(1)} %get-tuple-element.46.cb_ref, bf16[1152,256]{1,0:T(8,128)(2,1)S(1)} %get-tuple-element.47.refs_0_, ...), custom_call_target="tpu_custom_call" | custom-call | flops 8000000000 | bytes 4000000 | tf_op jit(solution)/shard_map/pallas_call | solution.py:250
  (3 shorter events, 0.0 us)
Async XLA Ops:
  0.0 5.1 %collective-permute-start = (bf16[1,64,128]{2,1,0:T(8,128)(2,1)}, bf16[1,64,128]{2,1,0:T(8,128)(2,1)S(1)}, u32[]{:S(2)}, u32[]{:S(2)}) collective-permute-start(bf16[1,64,128]{2,1,0:T(8,128)(2,1)} %bitcast.7), channel_id=1, source_target_pairs={{0,18},{2,16},{4,22},{6,20},{8,26},{10,24},{12,30},{14,28},{16,2},... | collective-permute-start | bytes 49160 | tf_op jit(solution)/shard_map/ppermute | solution.py:356
  5.3 3.3 %collective-permute-start.1 = (bf16[2,32,128]{2,1,0:T(8,128)(2,1)S(1)}, bf16[2,32,128]{2,1,0:T(8,128)(2,1)S(1)}, u32[]{:S(2)}, u32[]{:S(2)}) collective-permute-start(bf16[2,32,128]{2,1,0:T(8,128)(2,1)S(1)} %shard_map.65), channel_id=1, source_target_pairs={{0,10},{2,8},{4,14},{6,12},{8,2},{10,0},{12,6},{14,4},{16,26},{18,... | collective-permute-start | bytes 49160 | tf_op jit(solution)/shard_map/ppermute | solution.py:356
  8.7 3.3 %collective-permute-start.2 = (bf16[4,32,128]{2,1,0:T(8,128)(2,1)S(1)}, bf16[4,32,128]{2,1,0:T(8,128)(2,1)S(1)}, u32[]{:S(2)}, u32[]{:S(2)}) collective-permute-start(bf16[4,32,128]{2,1,0:T(8,128)(2,1)S(1)} %pad_maximum_fusion.2), channel_id=1, source_target_pairs={{0,6},{2,4},{4,2},{6,0},{8,14},{10,12},{12,10},{14,8},{16,22},{18,... | collective-permute-start | bytes 98312 | tf_op jit(solution)/shard_map/ppermute | solution.py:356
  12.0 1.5 %collective-permute-start.3 = (bf16[8,32,128]{2,1,0:T(8,128)(2,1)S(1)}, bf16[8,32,128]{2,1,0:T(8,128)(2,1)S(1)}, u32[]{:S(2)}, u32[]{:S(2)}) collective-permute-start(bf16[8,32,128]{2,1,0:T(8,128)(2,1)S(1)} %pad_maximum_fusion.1), channel_id=1, source_target_pairs={{0,2},{2,0},{4,6},{6,4},{8,10},{10,8},{12,14},{14,12},{16,18},{18,... | collective-permute-start | bytes 196616 | tf_op jit(solution)/shard_map/ppermute | solution.py:356

commit v9 on v7

--- a/solution.py
+++ b/solution.py
@@ -254,7 +254,7 @@
             pltpu.VMEM((tile, tile * ch), jnp.bfloat16),
             pltpu.SemaphoreType.DMA((tile // 2 ** (layers + 1),)),
         ],
-        compiler_params=pltpu.CompilerParams(vmem_limit_bytes=48 * 1024 * 1024),
+        compiler_params=pltpu.CompilerParams(vmem_limit_bytes=20 * 1024 * 1024),
         cost_estimate=pl.CostEstimate(flops=8000000000, bytes_accessed=4000000, transcendentals=2000000),
     )(block_slot, table, proj_bias, conv_bias, *banded)
 

time: 20.4 us -> 20.4 us (level)
  no operation moved by 1% of the time
where the time goes in v9:
time: 20.4 us; the launch traced here: 20.2 us
  Pallas kernels  8.62 us (42%)
  starting transfers between devices  7.56 us (37%)
  waiting for transfers between devices  3.94 us (19%)
    ppermute x4, starting transfers between devices, on_device(): lax.ppermute(table, 'pos', [(i, i ^ (1 << bit | 1)) for i in range(npos)])  7.56 us
    pallas_call x1, Pallas kernels, tile_call(): pl.pallas_call(functools.partial(tile_kernel, (layers, tile, ch, npos, no...  6.67 us
    ppermute x4, waiting for transfers between devices, on_device(): lax.ppermute(table, 'pos', [(i, i ^ (1 << bit | 1)) for i in range(npos)])  3.94 us
    pallas_call x1, Pallas kernels, parameters_call(): pl.pallas_call(parameters_kernel, out_shape=(pltpu.SMEM(block_slot.shape,...  1.25 us
    pallas_call x2, Pallas kernels, band_call(): pl.pallas_call(functools.partial(weights_kernel, ch, which), out_shape=(p...  0.5 us
  transfers between devices with their start and end apart: 4, of which 4 were waited for; matrix products, arithmetic and copies ran while one was open for 0% of the time, Pallas kernels for 9%

profile of v9, /device:TPU:0, one launch (start us, length us, event | category | flops | bytes accessed | tf_op | source)
XLA Modules:
  0.0 20.2 jit_solution(7666533382007552053)
XLA Ops:
  0.0 3.5 %collective-permute-start = (bf16[1,64,128]{2,1,0:T(8,128)(2,1)}, bf16[1,64,128]{2,1,0:T(8,128)(2,1)S(1)}, u32[]{:S(2)}, u32[]{:S(2)}) collective-permute-start(bf16[1,64,128]{2,1,0:T(8,128)(2,1)} %bitcast.7), channel_id=1, source_target_pairs={{0,18},{2,16},{4,22},{6,20},{8,26},{10,24},{12,30},{14,28},{16,2},... | collective-permute-start | bytes 49160 | tf_op jit(solution)/shard_map/ppermute | solution.py:347
  3.5 1.3 %shard_map.64 = (s32[16]{0:T(128)S(4)}, bf16[1,32,128]{2,1,0:T(8,128)(2,1)S(1)}, bf16[64,128]{1,0:T(8,128)(2,1)S(1)}, f32[1,128]{1,0:T(1,128)S(1)}, f32[4,128]{1...) custom-call(s32[16]{0:T(128)} %slot_ref.1, bf16[64,128]{1,0:T(8,128)(2,1)} %emb_ref.1, bf16[64,128]{1,0:T(8,128)(2,1)} %bitcast.6, ...), custom_call_target="tpu_custom_call" | custom-call | flops 1000000 | bytes 1000000 | tf_op jit(solution)/shard_map/pallas_call | solution.py:283
  4.7 0.4 %collective-permute-done.emb_ref = bf16[1,64,128]{2,1,0:T(8,128)(2,1)S(1)} collective-permute-done((bf16[1,64,128]{2,1,0:T(8,128)(2,1)}, bf16[1,64,128]{2,1,0:T(8,128)(2,1)S(1)}, u32[]{:S(2)}, u32[]{:S(2)}) %collective-permute-start) | collective-permute-done | bytes 16416 | tf_op jit(solution)/shard_map/ppermute | solution.py:347
  5.1 0.2 shard_map.65
  5.3 1.9 %collective-permute-start.1 = (bf16[2,32,128]{2,1,0:T(8,128)(2,1)S(1)}, bf16[2,32,128]{2,1,0:T(8,128)(2,1)S(1)}, u32[]{:S(2)}, u32[]{:S(2)}) collective-permute-start(bf16[2,32,128]{2,1,0:T(8,128)(2,1)S(1)} %shard_map.65), channel_id=1, source_target_pairs={{0,10},{2,8},{4,14},{6,12},{8,2},{10,0},{12,6},{14,4},{16,26},{18,... | collective-permute-start | bytes 49160 | tf_op jit(solution)/shard_map/ppermute | solution.py:347
  7.2 0.3 %shard_map.66 = (bf16[1152,256]{1,0:T(8,128)(2,1)S(1)}, bf16[1152,256]{1,0:T(8,128)(2,1)S(1)}) custom-call(bf16[4,64,576]{2,1,0:T(8,128)(2,1)S(1)} %get-tuple-element.41.cw_ref), custom_call_target="tpu_custom_call" | custom-call | flops 1000000 | bytes 1000000 | tf_op jit(solution)/shard_map/pallas_call | solution.py:328
  7.5 1.2 %collective-permute-done.1 = bf16[2,32,128]{2,1,0:T(8,128)(2,1)S(1)} collective-permute-done((bf16[2,32,128]{2,1,0:T(8,128)(2,1)S(1)}, bf16[2,32,128]{2,1,0:T(8,128)(2,1)S(1)}, u32[]{:S(2)}, u32[]{:S(2)}) %collective-permute-start.1) | collective-permute-done | bytes 16416 | tf_op jit(solution)/shard_map/ppermute | solution.py:347
  8.7 1.6 %collective-permute-start.2 = (bf16[4,32,128]{2,1,0:T(8,128)(2,1)S(1)}, bf16[4,32,128]{2,1,0:T(8,128)(2,1)S(1)}, u32[]{:S(2)}, u32[]{:S(2)}) collective-permute-start(bf16[4,32,128]{2,1,0:T(8,128)(2,1)S(1)} %pad_maximum_fusion.2), channel_id=1, source_target_pairs={{0,6},{2,4},{4,2},{6,0},{8,14},{10,12},{12,10},{14,8},{16,22},{18,... | collective-permute-start | bytes 98312 | tf_op jit(solution)/shard_map/ppermute | solution.py:347
  10.3 0.3 %shard_map.67 = (bf16[1152,256]{1,0:T(8,128)(2,1)S(1)}, bf16[1152,256]{1,0:T(8,128)(2,1)S(1)}) custom-call(bf16[4,64,576]{2,1,0:T(8,128)(2,1)S(1)} %get-tuple-element.41.cw_ref), custom_call_target="tpu_custom_call" | custom-call | flops 1000000 | bytes 1000000 | tf_op jit(solution)/shard_map/pallas_call | solution.py:328
  10.6 1.4 %collective-permute-done.2 = bf16[4,32,128]{2,1,0:T(8,128)(2,1)S(1)} collective-permute-done((bf16[4,32,128]{2,1,0:T(8,128)(2,1)S(1)}, bf16[4,32,128]{2,1,0:T(8,128)(2,1)S(1)}, u32[]{:S(2)}, u32[]{:S(2)}) %collective-permute-start.2) | collective-permute-done | bytes 32800 | tf_op jit(solution)/shard_map/ppermute | solution.py:347
  12.0 0.6 %collective-permute-start.3 = (bf16[8,32,128]{2,1,0:T(8,128)(2,1)S(1)}, bf16[8,32,128]{2,1,0:T(8,128)(2,1)S(1)}, u32[]{:S(2)}, u32[]{:S(2)}) collective-permute-start(bf16[8,32,128]{2,1,0:T(8,128)(2,1)S(1)} %pad_maximum_fusion.1), channel_id=1, source_target_pairs={{0,2},{2,0},{4,6},{6,4},{8,10},{10,8},{12,14},{14,12},{16,18},{18,... | collective-permute-start | bytes 196616 | tf_op jit(solution)/shard_map/ppermute | solution.py:347
  12.6 0.9 %collective-permute-done.3 = bf16[8,32,128]{2,1,0:T(8,128)(2,1)S(1)} collective-permute-done((bf16[8,32,128]{2,1,0:T(8,128)(2,1)S(1)}, bf16[8,32,128]{2,1,0:T(8,128)(2,1)S(1)}, u32[]{:S(2)}, u32[]{:S(2)}) %collective-permute-start.3) | collective-permute-done | bytes 65568 | tf_op jit(solution)/shard_map/ppermute | solution.py:347
  13.5 6.7 %shard_map.68 = bf16[64,4096]{1,0:T(8,128)(2,1)} custom-call(s32[16]{0:T(128)S(4)} %get-tuple-element.33.slot_ref, bf16[16,32,128]{2,1,0:T(8,128)(2,1)S(1)} %pad_maximum_fusion.bin_ref, f32[1,128]{1,0:T(1,128)S(1)} %get-tuple-element.45.pb_ref, f32[4,128]{1,0:T(4,128)S(1)} %get-tuple-element.46.cb_ref, bf16[1152,256]{1,0:T(8,128)(2,1)S(1)} %get-tuple-element.47.refs_0_, ...), custom_call_target="tpu_custom_call" | custom-call | flops 8000000000 | bytes 4000000 | tf_op jit(solution)/shard_map/pallas_call | solution.py:241
  (3 shorter events, 0.0 us)
Async XLA Ops:
  0.0 5.1 %collective-permute-start = (bf16[1,64,128]{2,1,0:T(8,128)(2,1)}, bf16[1,64,128]{2,1,0:T(8,128)(2,1)S(1)}, u32[]{:S(2)}, u32[]{:S(2)}) collective-permute-start(bf16[1,64,128]{2,1,0:T(8,128)(2,1)} %bitcast.7), channel_id=1, source_target_pairs={{0,18},{2,16},{4,22},{6,20},{8,26},{10,24},{12,30},{14,28},{16,2},... | collective-permute-start | bytes 49160 | tf_op jit(solution)/shard_map/ppermute | solution.py:347
  5.3 3.3 %collective-permute-start.1 = (bf16[2,32,128]{2,1,0:T(8,128)(2,1)S(1)}, bf16[2,32,128]{2,1,0:T(8,128)(2,1)S(1)}, u32[]{:S(2)}, u32[]{:S(2)}) collective-permute-start(bf16[2,32,128]{2,1,0:T(8,128)(2,1)S(1)} %shard_map.65), channel_id=1, source_target_pairs={{0,10},{2,8},{4,14},{6,12},{8,2},{10,0},{12,6},{14,4},{16,26},{18,... | collective-permute-start | bytes 49160 | tf_op jit(solution)/shard_map/ppermute | solution.py:347
  8.7 3.3 %collective-permute-start.2 = (bf16[4,32,128]{2,1,0:T(8,128)(2,1)S(1)}, bf16[4,32,128]{2,1,0:T(8,128)(2,1)S(1)}, u32[]{:S(2)}, u32[]{:S(2)}) collective-permute-start(bf16[4,32,128]{2,1,0:T(8,128)(2,1)S(1)} %pad_maximum_fusion.2), channel_id=1, source_target_pairs={{0,6},{2,4},{4,2},{6,0},{8,14},{10,12},{12,10},{14,8},{16,22},{18,... | collective-permute-start | bytes 98312 | tf_op jit(solution)/shard_map/ppermute | solution.py:347
  12.0 1.5 %collective-permute-start.3 = (bf16[8,32,128]{2,1,0:T(8,128)(2,1)S(1)}, bf16[8,32,128]{2,1,0:T(8,128)(2,1)S(1)}, u32[]{:S(2)}, u32[]{:S(2)}) collective-permute-start(bf16[8,32,128]{2,1,0:T(8,128)(2,1)S(1)} %pad_maximum_fusion.1), channel_id=1, source_target_pairs={{0,2},{2,0},{4,6},{6,4},{8,10},{10,8},{12,14},{14,12},{16,18},{18,... | collective-permute-start | bytes 196616 | tf_op jit(solution)/shard_map/ppermute | solution.py:347
